TPU v7x, 32 devices: a whole 2x2x4 slice. The times are simulated.
32 devices in a mesh: head: 4 (over y, x), ctx: 8 (over z, core).
Axes of the slice: x: 2, y: 2, z: 4, core: 2. Of those that a mesh axis runs over, the one named last changes fastest.
Arguments:
- queries: bfloat16 [8, 160, 4096], P('ctx', 'head'), may hold values from -4.5 to 4.5
- key_rows: bfloat16 [8, 160, 512], P('ctx', 'head'), may hold values from -4.5 to 4.5
- value_rows: bfloat16 [8, 160, 512], P('ctx', 'head'), may hold values from -6 to 6
- stretch_order: int32 [32], replicated, may hold values from 0 to 31, each once
- out_weight: bfloat16 [4096, 4096], P('head'), may hold values from -0.09375 to 0.09375
Outputs:
- projected: bfloat16 [1280, 4096], P('ctx', 'head')
Inputs may be any that keep to these rules, and one draw needn't show every extreme that they name: stretch_order is a permutation of 0 to 31.
All inputs are finite; a program needn't handle non-finite values.
Results may differ from a plain program's by a relative error of at most 0.013.
Values may be sent and summed in bfloat16 or wider, within the bound.
No kernel may reach another device: no remote copies, remote signals or barrier semaphores. Data moves between devices by JAX's collectives and lax.ppermute only.
A program may use at most 64 MiB of HBM per device.

v0:
```python
import jax
import jax.numpy as jnp
from jax import lax
from jax.sharding import PartitionSpec as P

D_HEAD = 128


NEG_FILL = -1e30


def lookup_positions(order, flat_rows, span):
    table = jnp.arange(order.shape[0], dtype=jnp.int32)
    hits = (flat_rows // span)[:, None] == table[None, :]
    return jnp.sum(jnp.where(hits, order[None, :], 0), axis=1) * span + flat_rows % span


def attend_block(state, query_heads, query_pos, key_block, value_block, key_pos):
    run_max, run_sum, run_acc = state
    scores = jnp.einsum(
        "tkgd,pkd->kgtp", query_heads, key_block, preferred_element_type=jnp.float32
    ) * D_HEAD ** (-0.5)
    visible = key_pos[None, :] <= query_pos[:, None]
    scores = jnp.where(visible, scores, NEG_FILL)
    new_max = jnp.maximum(run_max, jnp.max(scores, axis=3))
    weights = jnp.where(visible, jnp.exp(scores - new_max[..., None]), 0.0)
    factor = jnp.exp(run_max - new_max)
    new_sum = run_sum * factor + jnp.sum(weights, axis=3)
    product = jnp.einsum(
        "kgtp,pkd->kgtd",
        weights.astype(jnp.bfloat16),
        value_block,
        preferred_element_type=jnp.float32,
    )
    return (new_max, new_sum, run_acc * factor[..., None] + product)


def fold_piece(
    state, query_heads, query_pos, key_piece, value_piece, flat_rows, order, span, kv_heads
):
    count = key_piece.shape[0]
    width = 512 if count % 512 == 0 else count
    blocks_n = count // width
    key_blocks = key_piece.reshape(blocks_n, width, kv_heads, D_HEAD)
    value_blocks = value_piece.reshape(blocks_n, width, kv_heads, D_HEAD)
    flat_blocks = flat_rows.reshape(blocks_n, width)

    def step_block(current, slab):
        key_block, value_block, block_rows = slab
        key_pos = lookup_positions(order, block_rows, span)
        return (
            attend_block(current, query_heads, query_pos, key_block, value_block, key_pos),
            None,
        )

    state, unused = lax.scan(step_block, state, (key_blocks, value_blocks, flat_blocks))
    return state


def on_device(queries, key_rows, value_rows, stretch_order, out_weight):
    head_count = lax.axis_size("head")
    ctx_index = lax.axis_index("ctx")
    span = queries.shape[1]
    seg_rows = span * head_count
    kv_local = key_rows.shape[2] // D_HEAD // head_count
    q_local = queries.shape[2] // D_HEAD // head_count
    groups = q_local // kv_local
    query_flat = ctx_index * seg_rows + jnp.arange(seg_rows, dtype=jnp.int32)
    query_pos = lookup_positions(stretch_order, query_flat, span)
    initial = (
        jnp.full((kv_local, groups, seg_rows), NEG_FILL, jnp.float32),
        jnp.zeros((kv_local, groups, seg_rows), jnp.float32),
        jnp.zeros((kv_local, groups, seg_rows, D_HEAD), jnp.float32),
    )
    query_ex, key_ex, value_ex = (
        lax.all_to_all(queries, "head", split_axis=2, concat_axis=1, tiled=True),
        lax.all_to_all(key_rows, "head", split_axis=2, concat_axis=1, tiled=True),
        lax.all_to_all(value_rows, "head", split_axis=2, concat_axis=1, tiled=True),
    )
    query_heads = query_ex[0].reshape(seg_rows, kv_local, groups, D_HEAD)
    piece = (
        lax.all_gather(key_ex[0], "ctx", axis=0, tiled=True),
        lax.all_gather(value_ex[0], "ctx", axis=0, tiled=True),
    )
    flat_rows = jnp.arange(piece[0].shape[0], dtype=jnp.int32)
    final = fold_piece(
        initial,
        query_heads,
        query_pos,
        piece[0],
        piece[1],
        flat_rows,
        stretch_order,
        span,
        kv_local,
    )
    run_max, run_sum, run_acc = final
    mixed = run_acc / run_sum[..., None]
    attn = (
        jnp.transpose(mixed, (2, 0, 1, 3)).reshape(seg_rows, q_local * D_HEAD).astype(jnp.bfloat16)
    )
    partial_out = jnp.dot(attn, out_weight, preferred_element_type=jnp.float32).astype(jnp.bfloat16)
    return (
        lax.psum_scatter(partial_out, "head", scatter_dimension=1, tiled=True)
        .astype(jnp.float32)
        .astype(jnp.bfloat16)
    )


def solution(mesh):
    return jax.shard_map(
        on_device,
        mesh=mesh,
        in_specs=(
            P("ctx", "head", None),
            P("ctx", "head", None),
            P("ctx", "head", None),
            P(),
            P("head", None),
        ),
        out_specs=P("ctx", "head"),
        check_vma=False,
    )
```

profile of v0, /device:TPU:0, one launch (start us, length us, event | category | flops | bytes accessed | tf_op | source)
XLA Modules:
  0.0 141.7 jit_solution(10089145926860692615)
XLA Ops:
  6.5 0.9 copy.32
  7.5 0.6 broadcast.153
  8.1 1.4 %reduce.3 = bf16[512,40]{1,0:T(8,128)(2,1)S(1)} reduce(bf16[512,1,40]{2,1,0:T(2,128)(2,1)S(1)} %bitcast.76, bf16[]{:T(256)} %broadcast.153), dimensions={1}, to_apply=%bitcast.59.reduce_sub_computation | reduce | bytes 81922
  9.5 0.8 reshape.116
  10.3 5.2 %all-to-all-start = ((bf16[4,2,2560]{2,1,0:T(2,128)(2,1)}), bf16[4,2,2560]{2,1,0:T(2,128)(2,1)S(1)}, u32[]{:S(2)}, u32[]{:S(2)}) async-start(bf16[4,2,2560]{2,1,0:T(2,128)(2,1)} %reshape.116), calls=%async_computation | async-start | bytes 81920 | tf_op jit(solution)/shard_map/all_to_all | solution.py:77
  15.5 0.7 select_reduce_fusion.1
  16.3 0.8 select_reduce_fusion
  17.0 0.9 copy.39
  18.0 1.4 %reduce.4 = bf16[512,40]{1,0:T(8,128)(2,1)S(1)} reduce(bf16[512,1,40]{2,1,0:T(2,128)(2,1)S(1)} %bitcast.79, bf16[]{:T(256)} %broadcast.153), dimensions={1}, to_apply=%bitcast.63.reduce_sub_computation | reduce | bytes 81922
  19.4 0.8 reshape.120
  20.3 4.2 %all-to-all-start.2 = ((bf16[4,2,2560]{2,1,0:T(2,128)(2,1)}), bf16[4,2,2560]{2,1,0:T(2,128)(2,1)S(1)}, u32[]{:S(2)}, u32[]{:S(2)}) async-start(bf16[4,2,2560]{2,1,0:T(2,128)(2,1)} %reshape.120), calls=%async_computation.2 | async-start | bytes 81920 | tf_op jit(solution)/shard_map/all_to_all | solution.py:78
  24.4 0.2 broadcast_compare_fusion
  24.6 4.6 %copy.35 = bf16[1,40,4096]{1,0,2:T(2,128)(2,1)S(1)} copy(bf16[1,40,4096]{2,1,0:T(8,128)(2,1)} %param.5) | data formatting | bytes 655360 | tf_op args[0]
  29.2 22.4 %reduce.2 = bf16[4096,40]{1,0:T(8,128)(2,1)S(1)} reduce(bf16[4096,1,40]{2,1,0:T(2,128)(2,1)S(1)} %bitcast.71, bf16[]{:T(256)} %broadcast.153), dimensions={1}, to_apply=%bitcast.61.reduce_sub_computation | reduce | bytes 655362
  51.6 2.4 %reshape.118 = bf16[4,2,20480]{2,1,0:T(2,128)(2,1)} reshape(bf16[4096,40]{1,0:T(8,128)(2,1)S(1)} %reduce.2) | data formatting | bytes 655360
  54.0 0.4 reshape.117
  54.4 0.1 copy.33
  54.6 4.2 %all-to-all-start.1 = ((bf16[4,2,20480]{2,1,0:T(2,128)(2,1)}), bf16[4,2,20480]{2,1,0:T(2,128)(2,1)S(1)}, u32[]{:S(2)}, u32[]{:S(2)}) async-start(bf16[4,2,20480]{2,1,0:T(2,128)(2,1)} %reshape.118), calls=%async_computation.1 | async-start | bytes 655360 | tf_op jit(solution)/shard_map/all_to_all | solution.py:76
  58.8 0.4 reshape.121
  59.1 0.1 copy.40
  59.3 14.5 %all_gather.6 = bf16[1280,128]{1,0:T(8,128)(2,1)S(1)} all-gather(bf16[160,128]{1,0:T(8,128)(2,1)S(1)} %bitcast.82), channel_id=1, replica_groups=mesh['head'=4,'ctx'=8] {'ctx'}, dimensions={0}, use_global_device_ids=true | all-gather | bytes 368640 | tf_op jit(solution)/shard_map/all_gather | solution.py:82
  73.8 15.6 %all_gather.7 = bf16[1280,128]{1,0:T(8,128)(2,1)} all-gather(bf16[160,128]{1,0:T(8,128)(2,1)S(1)} %bitcast.83), channel_id=1, replica_groups=mesh['head'=4,'ctx'=8] {'ctx'}, dimensions={0}, use_global_device_ids=true | all-gather | bytes 368640 | tf_op jit(solution)/shard_map/all_gather | solution.py:83
  89.4 3.1 %reshape.119 = bf16[4096,1,40]{2,1,0:T(2,128)(2,1)S(1)} reshape(bf16[4,2,20480]{2,1,0:T(2,128)(2,1)S(1)} %all-to-all-done.1) | data formatting | bytes 655360
  92.5 2.1 %copy.36 = bf16[1,40,4096]{2,1,0:T(8,128)(2,1)S(1)} copy(bf16[1,40,4096]{1,0,2:T(2,128)(2,1)S(1)} %bitcast.70) | data formatting | bytes 655360 | tf_op jit(solution)/shard_map/all_to_all | solution.py:76
  94.7 0.2 all_to_all.37
  94.9 0.1 copy.37
  95.1 1.4 fusion
  96.5 2.2 %fusion.1 = f32[8,160]{1,0:T(8,128)S(1)} fusion(f32[1280,160,8]{0,1,2:T(8,128)S(1)} %get-tuple-element.26, f32[8,160]{1,0:T(8,128)S(1)} %broadcast_maximum_fusion, pred[160,1280]{1,0:T(8,128)(4,1)S(1)} %broadcast_compare_fusion), kind=kLoop, calls=%fused_computation.4 | loop fusion | flops 8190720 | bytes 6768640 | tf_op jit(solution)/shard_map/while/body/eval_jaxpr/reduce_sum | solution.py:28
  98.7 2.2 %fusion.16 = bf16[160,1,8,128]{3,0,2,1:T(8,128)(2,1)S(1)} fusion(f32[1280,160,8]{0,1,2:T(8,128)S(1)} %get-tuple-element.26, f32[8,160]{1,0:T(8,128)S(1)} %broadcast_maximum_fusion, pred[160,1280]{1,0:T(8,128)(4,1)S(1)} %broadcast_compare_fusion, bf16[1280,128]{1,0:T(8,128)(2,1)S(1)} %copy-done, f32[8,160]{1,0:T(8,128)S(1)} %get-tuple-element.24, ...), kind=kOutput, calls=%fused_computation.12 | convolution fusion | flops 428113920 | bytes 7429120 | tf_op jit(solution)/shard_map/while/body/eval_jaxpr/kgtp,pkd->kgtd/dot_general | solution.py:29
  100.9 0.1 copy.42
  101.1 2.6 %convolution_convert_fusion = bf16[160,4096]{1,0:T(8,128)(2,1)} fusion(bf16[1024,4096]{1,0:T(8,128)(2,1)S(1)} %bitcast.69, bf16[20,8,8,128]{3,2,1,0:T(8,128)(2,1)S(1)} %bitcast.72), kind=kOutput, calls=%fused_computation.3 | convolution fusion | flops 1342832640 | bytes 10027008 | tf_op jit(solution)/shard_map/dot_general | solution.py:102
  103.7 31.1 %reduce-scatter.2.cloned.1.call-done = bf16[160,1024]{1,0:T(8,128)(2,1)} async-done(((bf16[160,4096]{1,0:T(8,128)(2,1)}), bf16[160,1024]{1,0:T(8,128)(2,1)}) %reduce-scatter.2.cloned.1.call-update) | async-done | bytes 327696 | tf_op jit(solution)/shard_map/reduce_scatter | solution.py:104
  (23 shorter events, 0.2 us)
Async XLA Ops:
  10.3 9.9 %all-to-all-start = ((bf16[4,2,2560]{2,1,0:T(2,128)(2,1)}), bf16[4,2,2560]{2,1,0:T(2,128)(2,1)S(1)}, u32[]{:S(2)}, u32[]{:S(2)}) async-start(bf16[4,2,2560]{2,1,0:T(2,128)(2,1)} %reshape.116), calls=%async_computation | async-start | bytes 81920 | tf_op jit(solution)/shard_map/all_to_all | solution.py:77
  20.3 34.3 %all-to-all-start.2 = ((bf16[4,2,2560]{2,1,0:T(2,128)(2,1)}), bf16[4,2,2560]{2,1,0:T(2,128)(2,1)S(1)}, u32[]{:S(2)}, u32[]{:S(2)}) async-start(bf16[4,2,2560]{2,1,0:T(2,128)(2,1)} %reshape.120), calls=%async_computation.2 | async-start | bytes 81920 | tf_op jit(solution)/shard_map/all_to_all | solution.py:78
  54.6 34.8 %all-to-all-start.1 = ((bf16[4,2,20480]{2,1,0:T(2,128)(2,1)}), bf16[4,2,20480]{2,1,0:T(2,128)(2,1)S(1)}, u32[]{:S(2)}, u32[]{:S(2)}) async-start(bf16[4,2,20480]{2,1,0:T(2,128)(2,1)} %reshape.118), calls=%async_computation.1 | async-start | bytes 655360 | tf_op jit(solution)/shard_map/all_to_all | solution.py:76
  58.8 76.1 %reduce-scatter.2.cloned.1.call-start = ((), (), s32[]{:S(2)}) async-start(), calls=%async_computation.4 | async-start | bytes 1638400 | tf_op jit(solution)/shard_map/reduce_scatter | solution.py:104
  95.1 3.6 %copy-start = (bf16[1280,128]{1,0:T(8,128)(2,1)S(1)}, bf16[1280,128]{1,0:T(8,128)(2,1)}, u32[]{:S(2)}) copy-start(bf16[1280,128]{1,0:T(8,128)(2,1)} %all_gather.7) | copy-start | bytes 983044
  96.5 4.6 %slice-start = ((s8[8388608]{0:T(1024)(128)(4,1)}), s8[4194304]{0:T(1024)(128)(4,1)S(1)}, s32[]{:S(2)}) async-start(s8[8388608]{0:T(1024)(128)(4,1)} %bitcast.68), calls=%async_computation.5 | async-start | bytes 8388608
  98.7 2.4 %slice-start.1 = ((s8[8388608]{0:T(1024)(128)(4,1)}), s8[4194304]{0:T(1024)(128)(4,1)S(1)}, s32[]{:S(2)}) async-start(s8[8388608]{0:T(1024)(128)(4,1)} %bitcast.68), calls=%async_computation.6 | async-start | bytes 8388608
Sparse Core Ops, SparseCore 0:
  103.9 30.9 reduce-scatter.1
where the time goes:
time: 142 us
  waiting for transfers between devices  31.1 us (22%)
  blocking collectives  30.1 us (21%)
  other arithmetic  29.2 us (21%)
  local copies, waits for them, and re-layouts  17.8 us (13%)
  between operations  13.7 us (10%)
  starting transfers between devices  13.6 us (10%)
  matrix products  6.23 us (4%)
    reduce_scatter x1, waiting for transfers between devices, on_device(): lax.psum_scatter(partial_out, 'head', scatter_dimension=1, tiled=True)  31.1 us
    unnamed x4, other arithmetic  25.3 us
    all_gather x1, blocking collectives, on_device(): lax.all_gather(value_ex[0], 'ctx', axis=0, tiled=True)  15.6 us
    unnamed x17, local copies, waits for them, and re-layouts  15 us
    all_gather x1, blocking collectives, on_device(): lax.all_gather(key_ex[0], 'ctx', axis=0, tiled=True)  14.5 us
    all_to_all x1, starting transfers between devices, on_device(): lax.all_to_all(key_rows, 'head', split_axis=2, concat_axis=1, tiled=True)  5.16 us
    all_to_all x1, starting transfers between devices, on_device(): lax.all_to_all(queries, 'head', split_axis=2, concat_axis=1, tiled=True)  4.2 us
    all_to_all x1, starting transfers between devices, on_device(): lax.all_to_all(value_rows, 'head', split_axis=2, concat_axis=1, tiled=True)  4.18 us
  transfers between devices with their start and end apart: 4, of which 1 were waited for; matrix products, arithmetic and copies ran while one was open for 25% of the time, Pallas kernels for 0%

commit v1 on v0

--- a/solution.py
+++ b/solution.py
@@ -1,18 +1,147 @@
+import functools
+import math
+
 import jax
 import jax.numpy as jnp
 from jax import lax
+from jax.experimental import pallas as pl
+from jax.experimental.pallas import tpu as pltpu
 from jax.sharding import PartitionSpec as P
 
 D_HEAD = 128
-
-
 NEG_FILL = -1e30
+EXP2_SCALE = D_HEAD ** (-0.5) * math.log2(math.e)
+ORDER = (3, 1, 2, 0)
+
+
+def swap(x, axis, flip, size):
+    return lax.ppermute(x, axis, [(i, i ^ flip) for i in range(size)])
 
 
 def lookup_positions(order, flat_rows, span):
     table = jnp.arange(order.shape[0], dtype=jnp.int32)
     hits = (flat_rows // span)[:, None] == table[None, :]
     return jnp.sum(jnp.where(hits, order[None, :], 0), axis=1) * span + flat_rows % span
+
+
+def attend_kernel(span, heads, n_piece, n_chunk, *refs):
+    qpos_ref, kpos_ref = refs[:2]
+    q_refs = refs[2 : 2 + n_piece]
+    kv_refs = refs[2 + n_piece : 2 + n_piece + n_chunk]
+    weight_ref, attn_ref, part_ref, k_s, v_s, bias_s, a_s, w_s, sem = refs[2 + n_piece + n_chunk :]
+    me = lax.axis_index("head")
+    cols = part_ref.shape[1]
+    start = pl.multiple_of((me ^ ORDER[0]) * cols, cols)
+    fetch = pltpu.make_async_copy(weight_ref.at[:, pl.ds(start, cols)], w_s, sem)
+    fetch.start()
+    rows = kv_refs[0].shape[0]
+    for i, ref in enumerate(kv_refs):
+        k_s[i * rows : (i + 1) * rows, :] = ref[:, :D_HEAD]
+        v_s[i * rows : (i + 1) * rows, :] = ref[:, D_HEAD:]
+    bias_s[...] = jnp.where(kpos_ref[...] <= qpos_ref[...], 0.0, NEG_FILL)
+    for piece in range(n_piece):
+        q = q_refs[piece][...].astype(jnp.float32)
+        q = jnp.concatenate([q[:, h * D_HEAD : (h + 1) * D_HEAD] for h in range(heads)], axis=0)
+        scores = lax.dot_general(
+            q.astype(jnp.bfloat16), k_s[...], (((1,), (1,)), ((), ())),
+            preferred_element_type=jnp.float32,
+        )
+        n_keys = scores.shape[1]
+        scores = scores.reshape(heads, span, n_keys) + bias_s[piece * span : (piece + 1) * span, :][None]
+        peak = jnp.max(scores, axis=2, keepdims=True)
+        weights = jnp.exp2((scores - peak) * EXP2_SCALE)
+        denom = jnp.sum(weights, axis=2, keepdims=True)
+        mixed = jnp.dot(
+            weights.astype(jnp.bfloat16).reshape(heads * span, n_keys), v_s[...],
+            preferred_element_type=jnp.float32,
+        )
+        mixed = mixed.reshape(heads, span, D_HEAD) / denom
+        at = pl.multiple_of((me ^ piece) * span, span)
+        for h in range(heads):
+            a_s[pl.ds(at, span), h * D_HEAD : (h + 1) * D_HEAD] = mixed[h]
+    attn = a_s[...].astype(jnp.bfloat16)
+    attn_ref[...] = attn
+    fetch.wait()
+    part_ref[...] = jnp.dot(attn, w_s[...], preferred_element_type=jnp.float32).astype(jnp.bfloat16)
+
+
+def attend(q_pieces, kv_chunks, qpos, kpos, weight):
+    n_piece, n_chunk = len(q_pieces), len(kv_chunks)
+    span, width = q_pieces[0].shape
+    heads = width // D_HEAD
+    seg = span * n_piece
+    rows = kv_chunks[0].shape[0]
+    n_keys = rows * n_chunk
+    cols = weight.shape[1] // n_piece
+    vmem = pl.BlockSpec(memory_space=pltpu.VMEM)
+    return pl.pallas_call(
+        functools.partial(attend_kernel, span, heads, n_piece, n_chunk),
+        out_shape=(
+            jax.ShapeDtypeStruct((seg, width), jnp.bfloat16),
+            jax.ShapeDtypeStruct((seg, cols), jnp.bfloat16),
+        ),
+        in_specs=[vmem] * (2 + n_piece + n_chunk) + [pl.BlockSpec(memory_space=pl.ANY)],
+        out_specs=(vmem, vmem),
+        scratch_shapes=[
+            pltpu.VMEM((n_keys, D_HEAD), jnp.bfloat16),
+            pltpu.VMEM((n_keys, D_HEAD), jnp.bfloat16),
+            pltpu.VMEM((seg, n_keys), jnp.float32),
+            pltpu.VMEM((seg, width), jnp.float32),
+            pltpu.VMEM((weight.shape[0], cols), jnp.bfloat16),
+            pltpu.SemaphoreType.DMA(()),
+        ],
+        compiler_params=pltpu.CompilerParams(vmem_limit_bytes=40 * 1024 * 1024),
+        cost_estimate=pl.CostEstimate(
+            flops=4 * seg * width * n_keys + 2 * seg * width * cols,
+            bytes_accessed=8 * 1024 * 1024,
+            transcendentals=seg * heads * n_keys,
+        ),
+    )(qpos, kpos, *q_pieces, *kv_chunks, weight)
+
+
+def fast_path(queries, key_rows, value_rows, stretch_order, out_weight, n_head, n_ctx):
+    me = lax.axis_index("head")
+    ctx = lax.axis_index("ctx")
+    span = queries.shape[1]
+    kv_w = key_rows.shape[2] // n_head
+    q_w = queries.shape[2] // n_head
+
+    def cut(x, k, width):
+        return lax.dynamic_slice_in_dim(x[0], (me ^ k) * width, width, 1)
+
+    kv_cut = [
+        jnp.concatenate([cut(key_rows, k, kv_w), cut(value_rows, k, kv_w)], axis=1)
+        for k in range(n_head)
+    ]
+    q_cut = [cut(queries, k, q_w) for k in range(n_head)]
+    kv_in = [kv_cut[0]] + [swap(kv_cut[k], "head", k, n_head) for k in range(1, n_head)]
+    q_in = [q_cut[0]] + [swap(q_cut[k], "head", k, n_head) for k in range(1, n_head)]
+    own = jnp.concatenate(kv_in, axis=0)
+    same_core = [own] + [swap(own, "ctx", 2 * dz, n_ctx) for dz in range(1, n_ctx // 2)]
+    other_core = [swap(x, "ctx", 1, n_ctx) for x in same_core]
+    chunks = same_core + other_core
+    chunk_ctx = [ctx ^ (2 * dz) for dz in range(n_ctx // 2)]
+    chunk_ctx = chunk_ctx + [c ^ 1 for c in chunk_ctx]
+    offsets = jnp.arange(span, dtype=jnp.int32)
+
+    def positions(ctx_ids):
+        blocks = jnp.stack([c * n_head + (me ^ k) for c in ctx_ids for k in range(n_head)])
+        table = jnp.arange(stretch_order.shape[0], dtype=jnp.int32)
+        held = jnp.sum(jnp.where(blocks[:, None] == table[None, :], stretch_order[None, :], 0), axis=1)
+        return (held[:, None] * span + offsets[None, :]).reshape(-1)
+
+    qpos = positions([ctx])[:, None]
+    kpos = positions(chunk_ctx)[None, :]
+    attn, far = attend(q_in, chunks, qpos, kpos, out_weight)
+    out_w = out_weight.shape[1] // n_head
+    total = swap(far, "head", ORDER[0], n_head).astype(jnp.float32)
+    for k in ORDER[1:]:
+        w = lax.dynamic_slice_in_dim(out_weight, (me ^ k) * out_w, out_w, 1)
+        part = jnp.dot(attn, w, preferred_element_type=jnp.float32).astype(jnp.bfloat16)
+        if k:
+            part = swap(part, "head", k, n_head)
+        total = total + part.astype(jnp.float32)
+    return total.astype(jnp.bfloat16)
 
 
 def attend_block(state, query_heads, query_pos, key_block, value_block, key_pos):
@@ -57,13 +186,12 @@
     return state
 
 
-def on_device(queries, key_rows, value_rows, stretch_order, out_weight):
-    head_count = lax.axis_size("head")
+def long_path(queries, key_rows, value_rows, stretch_order, out_weight, n_head):
     ctx_index = lax.axis_index("ctx")
     span = queries.shape[1]
-    seg_rows = span * head_count
-    kv_local = key_rows.shape[2] // D_HEAD // head_count
-    q_local = queries.shape[2] // D_HEAD // head_count
+    seg_rows = span * n_head
+    kv_local = key_rows.shape[2] // D_HEAD // n_head
+    q_local = queries.shape[2] // D_HEAD // n_head
     groups = q_local // kv_local
     query_flat = ctx_index * seg_rows + jnp.arange(seg_rows, dtype=jnp.int32)
     query_pos = lookup_positions(stretch_order, query_flat, span)
@@ -78,21 +206,11 @@
         lax.all_to_all(value_rows, "head", split_axis=2, concat_axis=1, tiled=True),
     )
     query_heads = query_ex[0].reshape(seg_rows, kv_local, groups, D_HEAD)
-    piece = (
-        lax.all_gather(key_ex[0], "ctx", axis=0, tiled=True),
-        lax.all_gather(value_ex[0], "ctx", axis=0, tiled=True),
-    )
-    flat_rows = jnp.arange(piece[0].shape[0], dtype=jnp.int32)
+    keys = lax.all_gather(key_ex[0], "ctx", axis=0, tiled=True)
+    values = lax.all_gather(value_ex[0], "ctx", axis=0, tiled=True)
+    flat_rows = jnp.arange(keys.shape[0], dtype=jnp.int32)
     final = fold_piece(
-        initial,
-        query_heads,
-        query_pos,
-        piece[0],
-        piece[1],
-        flat_rows,
-        stretch_order,
-        span,
-        kv_local,
+        initial, query_heads, query_pos, keys, values, flat_rows, stretch_order, span, kv_local
     )
     run_max, run_sum, run_acc = final
     mixed = run_acc / run_sum[..., None]
@@ -108,6 +226,13 @@
 
 
 def solution(mesh):
+    n_head, n_ctx = mesh.shape["head"], mesh.shape["ctx"]
+
+    def on_device(*args):
+        if n_ctx <= 8:
+            return fast_path(*args, n_head, n_ctx)
+        return long_path(*args, n_head)
+
     return jax.shard_map(
         on_device,
         mesh=mesh,

time: 142 us -> 51 us (0.36)
  blocking collectives: 30.1 us -> 0 us
  other arithmetic: 29.2 us -> 1.94 us
  between operations: 13.7 us -> 0.12 us
  local copies, waits for them, and re-layouts: 17.8 us -> 5.55 us
  waiting for transfers between devices: 31.1 us -> 20.1 us
  matrix products: 6.23 us -> 2.38 us
  Pallas kernels: 0 us -> 3.7 us
  starting transfers between devices: 13.6 us -> 16.9 us
    reduce_scatter x1 -> x0, waiting for transfers between devices: 31.1 us -> none  [on_device(): lax.psum_scatter(partial_out, 'head', scatter_dimension=1, tiled=True)]
    all_gather x2 -> x0, blocking collectives: 30.1 us -> none  [the longest x1 15.6 us: on_device(): lax.all_gather(value_ex[0], 'ctx', axis=0, tiled=True)]
    unnamed x4 -> x0, other arithmetic: 25.3 us -> none
    ppermute x0 -> x16, waiting for transfers between devices: none -> 20.1 us  [swap(): return lax.ppermute(x, axis, [(i, i ^ flip) for i in range(size)])]
    ppermute x0 -> x16, starting transfers between devices: none -> 16.9 us  [swap(): return lax.ppermute(x, axis, [(i, i ^ flip) for i in range(size)])]
    all_to_all x3 -> x0, starting transfers between devices: 13.5 us -> none  [the longest x1 5.16 us: on_device(): lax.all_to_all(key_rows, 'head', split_axis=2, concat_axis=1, tiled=True)]
    unnamed x17 -> x2, local copies, waits for them, and re-layouts: 15 us -> 3.38 us
    dot_general x3, matrix products: 6.23 us -> 2.38 us  [fast_path(): jnp.dot(attn, w, preferred_element_type=jnp.float32).astype(jnp.bfloat16)]
  transfers between devices with their start and end apart: 4 -> 16, of which waited for: 1 -> 6; matrix products, arithmetic and copies ran while one was open for 25% -> 6% of each run, Pallas kernels for 0% -> 0%
where the time goes in v1:
time: 51 us; the launch traced here: 50.7 us
  waiting for transfers between devices  20.1 us (39%)
  starting transfers between devices  16.9 us (33%)
  local copies, waits for them, and re-layouts  5.55 us (11%)
  Pallas kernels  3.7 us (7%)
  matrix products  2.38 us (5%)
  other arithmetic  1.94 us (4%)
    ppermute x16, waiting for transfers between devices, swap(): return lax.ppermute(x, axis, [(i, i ^ flip) for i in range(size)])  20.1 us
    ppermute x16, starting transfers between devices, swap(): return lax.ppermute(x, axis, [(i, i ^ flip) for i in range(size)])  16.9 us
    pallas_call x1, Pallas kernels, attend(): pl.pallas_call(functools.partial(attend_kernel, span, heads, n_piece, n_c...  3.7 us
    unnamed x2, local copies, waits for them, and re-layouts  3.38 us
    dot_general x3, matrix products, fast_path(): jnp.dot(attn, w, preferred_element_type=jnp.float32).astype(jnp.bfloat16)  2.38 us
    dynamic_slice x2, local copies, waits for them, and re-layouts, cut(): return lax.dynamic_slice_in_dim(x[0], (me ^ k) * width, width, 1)  1.86 us
    reduce_sum x2, other arithmetic, positions(): jnp.sum(jnp.where(blocks[:, None] == table[None, :], stretch_order[None,...  1.68 us
  transfers between devices with their start and end apart: 16, of which 6 were waited for; matrix products, arithmetic and copies ran while one was open for 6% of the time, Pallas kernels for 0%

profile of v1, /device:TPU:0, one launch (start us, length us, event | category | flops | bytes accessed | tf_op | source)
XLA Modules:
  0.0 50.7 jit_solution(1260797366129403711)
XLA Ops:
  0.0 0.8 %dynamic-slice_bitcast_fusion.10 = (bf16[40,128]{1,0:T(8,128)(2,1)S(1)}, bf16[40,128]{1,0:T(8,128)(2,1)S(1)}, bf16[40,128]{1,0:T(8,128)(2,1)S(1)}, bf16[40,128]{...) fusion(bf16[1,40,512]{2,1,0:T(8,128)(2,1)} %param.7, ...), kind=kLoop, calls=%fused_computation.29 | loop fusion | bytes 163856 | tf_op jit(solution)/shard_map/dynamic_slice | solution.py:110
  0.8 3.0 %collective-permute-start.4 = (bf16[40,256]{1,0:T(8,128)(2,1)S(1)}, bf16[40,256]{1,0:T(8,128)(2,1)S(1)}, u32[]{:S(2)}, u32[]{:S(2)}) collective-permute-start(bf16[40,256]{1,0:T(8,128)(2,1)S(1)} %pad_maximum_fusion.2), channel_id=1, source_target_pairs={{0,16},{8,24},{16,0},{24,8},{1,17},{9,25},{17,1},{25,9},{2,18},{10... | collective-permute-start | bytes 61448 | tf_op jit(solution)/shard_map/ppermute | solution.py:18
  3.9 1.4 %collective-permute-start.5 = (bf16[40,256]{1,0:T(8,128)(2,1)S(1)}, bf16[40,256]{1,0:T(8,128)(2,1)S(1)}, u32[]{:S(2)}, u32[]{:S(2)}) collective-permute-start(bf16[40,256]{1,0:T(8,128)(2,1)S(1)} %pad_maximum_fusion.3), channel_id=1, source_target_pairs={{0,24},{8,16},{16,8},{24,0},{1,25},{9,17},{17,9},{25,1},{2,26},{10... | collective-permute-start | bytes 61448 | tf_op jit(solution)/shard_map/ppermute | solution.py:18
  5.3 0.1 collective-permute-start.3
  5.5 1.0 %dynamic-slice_bitcast_fusion = (bf16[40,1024]{1,0:T(8,128)(2,1)S(1)}, bf16[40,1024]{1,0:T(8,128)(2,1)S(1)}, bf16[40,1024]{1,0:T(8,128)(2,1)S(1)}, bf16[40,1024]{1,0:T(8,128)(2,1)S(1)}) fusion(bf16[1,40,4096]{2,1,0:T(8,128)(2,1)} %param.5, s32[]{:T(128)S(6)} %select_n.44, s32[]{:T(128)S(6)} %select_n.42, s32[]{:T(128)S(6)} %select_n.41, s32[]{:T(128)S(6)} %select_n.43), kind=kLoop, calls=%fused_computation.13 | loop fusion | bytes 655376 | tf_op jit(solution)/shard_map/dynamic_slice | solution.py:110
  6.5 2.9 %collective-permute-start.2 = (bf16[40,1024]{1,0:T(8,128)(2,1)S(1)}, bf16[40,1024]{1,0:T(8,128)(2,1)S(1)}, u32[]{:S(2)}, u32[]{:S(2)}) collective-permute-start(bf16[40,1024]{1,0:T(8,128)(2,1)S(1)} %get-tuple-element.9), channel_id=1, source_target_pairs={{0,24},{8,16},{16,8},{24,0},{1,25},{9,17},{17,9},{25,1},{2,26},{10... | collective-permute-start | bytes 245768 | tf_op jit(solution)/shard_map/ppermute | solution.py:18
  9.4 0.5 %collective-permute-start = (bf16[40,1024]{1,0:T(8,128)(2,1)S(1)}, bf16[40,1024]{1,0:T(8,128)(2,1)S(1)}, u32[]{:S(2)}, u32[]{:S(2)}) collective-permute-start(bf16[40,1024]{1,0:T(8,128)(2,1)S(1)} %get-tuple-element.10), channel_id=1, source_target_pairs={{0,8},{8,0},{16,24},{24,16},{1,9},{9,1},{17,25},{25,17},{2,10},{10... | collective-permute-start | bytes 245768 | tf_op jit(solution)/shard_map/ppermute | solution.py:18
  9.9 0.1 pad_add_fusion
  10.0 0.1 stack.139
  10.1 0.8 %select_reduce_fusion = s32[32]{0:T(128)S(1)} fusion(s32[32]{0:T(128)} %param.8, s32[32]{0:T(128)S(1)} %stack.139), kind=kLoop, calls=%fused_computation.21 | loop fusion | flops 3040 | bytes 384 | tf_op jit(solution)/shard_map/reduce_sum | solution.py:130
  11.0 0.1 iota_add_fusion
  11.1 0.8 %select_reduce_fusion.1 = s32[4]{0:T(128)S(1)} fusion(s32[32]{0:T(128)} %param.8, s32[4]{0:T(128)S(1)} %pad_add_fusion), kind=kLoop, calls=%fused_computation.35 | loop fusion | flops 380 | bytes 160 | tf_op jit(solution)/shard_map/reduce_sum | solution.py:130
  11.9 3.7 %collective-permute-start.8 = (bf16[160,256]{1,0:T(8,128)(2,1)S(1)}, bf16[160,256]{1,0:T(8,128)(2,1)S(1)}, u32[]{:S(2)}, u32[]{:S(2)}) collective-permute-start(bf16[160,256]{1,0:T(8,128)(2,1)S(1)} %pad_maximum_fusion.refs_6_), channel_id=1, source_target_pairs={{0,6},{1,7},{2,4},{3,5},{4,2},{5,3},{6,0},{7,1},{8,14},{9,15},{10,... | collective-permute-start | bytes 245768 | tf_op jit(solution)/shard_map/ppermute | solution.py:18
  15.6 0.8 %collective-permute-start.6 = (bf16[160,256]{1,0:T(8,128)(2,1)S(1)}, bf16[160,256]{1,0:T(8,128)(2,1)S(1)}, u32[]{:S(2)}, u32[]{:S(2)}) collective-permute-start(bf16[160,256]{1,0:T(8,128)(2,1)S(1)} %pad_maximum_fusion.refs_6_), channel_id=1, source_target_pairs={{0,2},{1,3},{2,0},{3,1},{4,6},{5,7},{6,4},{7,5},{8,10},{9,11},{10,... | collective-permute-start | bytes 245768 | tf_op jit(solution)/shard_map/ppermute | solution.py:18
  16.4 0.4 collective-permute-start.1
  16.8 1.5 %collective-permute-done.8.refs_9_ = bf16[160,256]{1,0:T(8,128)(2,1)S(1)} collective-permute-done((bf16[160,256]{1,0:T(8,128)(2,1)S(1)}, bf16[160,256]{1,0:T(8,128)(2,1)S(1)}, u32[]{:S(2)}, u32[]{:S(2)}) %collective-permute-start.8) | collective-permute-done | bytes 81952 | tf_op jit(solution)/shard_map/ppermute | solution.py:18
  18.3 3.3 %collective-permute-done.7.refs_8_ = bf16[160,256]{1,0:T(8,128)(2,1)S(1)} collective-permute-done((bf16[160,256]{1,0:T(8,128)(2,1)S(1)}, bf16[160,256]{1,0:T(8,128)(2,1)S(1)}, u32[]{:S(2)}, u32[]{:S(2)}) %collective-permute-start.7) | collective-permute-done | bytes 81952 | tf_op jit(solution)/shard_map/ppermute | solution.py:18
  21.5 0.5 %collective-permute-start.10 = (bf16[160,256]{1,0:T(8,128)(2,1)S(1)}, bf16[160,256]{1,0:T(8,128)(2,1)S(1)}, u32[]{:S(2)}, u32[]{:S(2)}) collective-permute-start(bf16[160,256]{1,0:T(8,128)(2,1)S(1)} %collective-permute-done.6.refs_7_), channel_id=1, source_target_pairs={{0,1},{1,0},{2,3},{3,2},{4,5},{5,4},{6,7},{7,6},{8,9},{9,8},{10,11... | collective-permute-start | bytes 245768 | tf_op jit(solution)/shard_map/ppermute | solution.py:18
  22.1 0.1 add.225.refs_1_
  22.2 0.1 add.237.refs_0_
  22.3 0.5 collective-permute-done.11.refs_12_
  22.8 0.2 collective-permute-done.10.refs_11_
  23.0 3.4 %copy-done = bf16[1024,4096]{1,0:T(8,128)(2,1)S(1)} copy-done((bf16[1024,4096]{1,0:T(8,128)(2,1)S(1)}, bf16[1024,4096]{1,0:T(8,128)(2,1)}, u32[]{:S(2)}) %copy-start) | copy-done | bytes 8388632
  26.3 3.7 %shard_map.55 = (bf16[160,1024]{1,0:T(8,128)(2,1)S(1)}, bf16[160,1024]{1,0:T(8,128)(2,1)S(1)}) custom-call(s32[160,1]{1,0:T(8,128)S(1)} %add.237.refs_0_, s32[1,1280]{1,0:T(1,128)S(1)} %add.225.refs_1_, bf16[40,1024]{1,0:T(8,128)(2,1)S(1)} %get-tuple-element.11.refs_2_, bf16[40,1024]{1,0:T(8,128)(2,1)S(1)} %collective-permute-done.refs_3_, ...), custom_call_target="tpu_custom_call" | custom-call | flops 1174405120 | bytes 8388608 | tf_op jit(solution)/shard_map/pallas_call | solution.py:77
  30.0 0.5 %fusion.9 = bf16[160,1024]{1,0:T(8,128)(2,1)S(1)} fusion(bf16[160,1024]{1,0:T(8,128)(2,1)S(1)} %get-tuple-element.8, bf16[1024,4096]{1,0:T(8,128)(2,1)S(1)} %copy-done, s32[]{:T(128)S(6)} %select_n.43), kind=kOutput, calls=%fused_computation.7 | convolution fusion | flops 335708160 | bytes 2752516 | tf_op jit(solution)/shard_map/dot_general | solution.py:140
  30.6 0.5 %fusion.6 = bf16[160,1024]{1,0:T(8,128)(2,1)S(1)} fusion(bf16[160,1024]{1,0:T(8,128)(2,1)S(1)} %get-tuple-element.8, bf16[1024,4096]{1,0:T(8,128)(2,1)S(1)} %copy-done, s32[]{:T(128)S(6)} %select_n.42), kind=kOutput, calls=%fused_computation.6 | convolution fusion | flops 335708160 | bytes 2752516 | tf_op jit(solution)/shard_map/dot_general | solution.py:140
  31.1 1.5 %collective-permute-start.14 = (bf16[160,1024]{1,0:T(8,128)(2,1)S(1)}, bf16[160,1024]{1,0:T(8,128)(2,1)S(1)}, u32[]{:S(2)}, u32[]{:S(2)}) collective-permute-start(bf16[160,1024]{1,0:T(8,128)(2,1)S(1)} %fusion.6), channel_id=1, source_target_pairs={{0,8},{8,0},{16,24},{24,16},{1,9},{9,1},{17,25},{25,17},{2,10},{10... | collective-permute-start | bytes 983048 | tf_op jit(solution)/shard_map/ppermute | solution.py:18
  32.7 0.5 %collective-permute-start.15 = (bf16[160,1024]{1,0:T(8,128)(2,1)S(1)}, bf16[160,1024]{1,0:T(8,128)(2,1)S(1)}, u32[]{:S(2)}, u32[]{:S(2)}) collective-permute-start(bf16[160,1024]{1,0:T(8,128)(2,1)S(1)} %fusion.9), channel_id=1, source_target_pairs={{0,16},{8,24},{16,0},{24,8},{1,17},{9,25},{17,1},{25,9},{2,18},{10... | collective-permute-start | bytes 983048 | tf_op jit(solution)/shard_map/ppermute | solution.py:18
  33.2 1.5 %collective-permute-start.13 = (bf16[160,1024]{1,0:T(8,128)(2,1)S(1)}, bf16[160,1024]{1,0:T(8,128)(2,1)S(1)}, u32[]{:S(2)}, u32[]{:S(2)}) collective-permute-start(bf16[160,1024]{1,0:T(8,128)(2,1)S(1)} %get-tuple-element.7), channel_id=1, source_target_pairs={{0,24},{8,16},{16,8},{24,0},{1,25},{9,17},{17,9},{25,1},{2,26},{10... | collective-permute-start | bytes 983048 | tf_op jit(solution)/shard_map/ppermute | solution.py:18
  34.7 7.0 %collective-permute-done.14 = bf16[160,1024]{1,0:T(8,128)(2,1)S(1)} collective-permute-done((bf16[160,1024]{1,0:T(8,128)(2,1)S(1)}, bf16[160,1024]{1,0:T(8,128)(2,1)S(1)}, u32[]{:S(2)}, u32[]{:S(2)}) %collective-permute-start.14) | collective-permute-done | bytes 327712 | tf_op jit(solution)/shard_map/ppermute | solution.py:18
  41.7 7.7 %collective-permute-done.15 = bf16[160,1024]{1,0:T(8,128)(2,1)S(1)} collective-permute-done((bf16[160,1024]{1,0:T(8,128)(2,1)S(1)}, bf16[160,1024]{1,0:T(8,128)(2,1)S(1)}, u32[]{:S(2)}, u32[]{:S(2)}) %collective-permute-start.15) | collective-permute-done | bytes 327712 | tf_op jit(solution)/shard_map/ppermute | solution.py:18
  49.4 1.3 %fusion.21 = bf16[160,1024]{1,0:T(8,128)(2,1)} fusion(bf16[160,1024]{1,0:T(8,128)(2,1)S(1)} %get-tuple-element.8, bf16[1024,4096]{1,0:T(8,128)(2,1)S(1)} %copy-done, s32[]{:T(128)S(6)} %select_n.41, bf16[160,1024]{1,0:T(8,128)(2,1)S(1)} %collective-permute-done.15, bf16[160,1024]{1,0:T(8,128)(2,1)S(1)} %collective-permute-done.14, ...), kind=kOutput, calls=%fused_computation.11 | convolution fusion | flops 337018880 | bytes 3735556 | tf_op jit(solution)/shard_map/dot_general | solution.py:140
  (22 shorter events, 0.1 us)
Async XLA Ops:
  0.8 11.1 %collective-permute-start.4 = (bf16[40,256]{1,0:T(8,128)(2,1)S(1)}, bf16[40,256]{1,0:T(8,128)(2,1)S(1)}, u32[]{:S(2)}, u32[]{:S(2)}) collective-permute-start(bf16[40,256]{1,0:T(8,128)(2,1)S(1)} %pad_maximum_fusion.2), channel_id=1, source_target_pairs={{0,16},{8,24},{16,0},{24,8},{1,17},{9,25},{17,1},{25,9},{2,18},{10... | collective-permute-start | bytes 61448 | tf_op jit(solution)/shard_map/ppermute | solution.py:18
  3.9 8.0 %collective-permute-start.5 = (bf16[40,256]{1,0:T(8,128)(2,1)S(1)}, bf16[40,256]{1,0:T(8,128)(2,1)S(1)}, u32[]{:S(2)}, u32[]{:S(2)}) collective-permute-start(bf16[40,256]{1,0:T(8,128)(2,1)S(1)} %pad_maximum_fusion.3), channel_id=1, source_target_pairs={{0,24},{8,16},{16,8},{24,0},{1,25},{9,17},{17,9},{25,1},{2,26},{10... | collective-permute-start | bytes 61448 | tf_op jit(solution)/shard_map/ppermute | solution.py:18
  5.3 6.6 %collective-permute-start.3 = (bf16[40,256]{1,0:T(8,128)(2,1)S(1)}, bf16[40,256]{1,0:T(8,128)(2,1)S(1)}, u32[]{:S(2)}, u32[]{:S(2)}) collective-permute-start(bf16[40,256]{1,0:T(8,128)(2,1)S(1)} %pad_maximum_fusion.1), channel_id=1, source_target_pairs={{0,8},{8,0},{16,24},{24,16},{1,9},{9,1},{17,25},{25,17},{2,10},{10... | collective-permute-start | bytes 61448 | tf_op jit(solution)/shard_map/ppermute | solution.py:18
  6.5 9.9 %collective-permute-start.2 = (bf16[40,1024]{1,0:T(8,128)(2,1)S(1)}, bf16[40,1024]{1,0:T(8,128)(2,1)S(1)}, u32[]{:S(2)}, u32[]{:S(2)}) collective-permute-start(bf16[40,1024]{1,0:T(8,128)(2,1)S(1)} %get-tuple-element.9), channel_id=1, source_target_pairs={{0,24},{8,16},{16,8},{24,0},{1,25},{9,17},{17,9},{25,1},{2,26},{10... | collective-permute-start | bytes 245768 | tf_op jit(solution)/shard_map/ppermute | solution.py:18
  9.4 7.4 %collective-permute-start = (bf16[40,1024]{1,0:T(8,128)(2,1)S(1)}, bf16[40,1024]{1,0:T(8,128)(2,1)S(1)}, u32[]{:S(2)}, u32[]{:S(2)}) collective-permute-start(bf16[40,1024]{1,0:T(8,128)(2,1)S(1)} %get-tuple-element.10), channel_id=1, source_target_pairs={{0,8},{8,0},{16,24},{24,16},{1,9},{9,1},{17,25},{25,17},{2,10},{10... | collective-permute-start | bytes 245768 | tf_op jit(solution)/shard_map/ppermute | solution.py:18
  11.9 6.3 %collective-permute-start.8 = (bf16[160,256]{1,0:T(8,128)(2,1)S(1)}, bf16[160,256]{1,0:T(8,128)(2,1)S(1)}, u32[]{:S(2)}, u32[]{:S(2)}) collective-permute-start(bf16[160,256]{1,0:T(8,128)(2,1)S(1)} %pad_maximum_fusion.refs_6_), channel_id=1, source_target_pairs={{0,6},{1,7},{2,4},{3,5},{4,2},{5,3},{6,0},{7,1},{8,14},{9,15},{10,... | collective-permute-start | bytes 245768 | tf_op jit(solution)/shard_map/ppermute | solution.py:18
  15.6 5.9 %collective-permute-start.7 = (bf16[160,256]{1,0:T(8,128)(2,1)S(1)}, bf16[160,256]{1,0:T(8,128)(2,1)S(1)}, u32[]{:S(2)}, u32[]{:S(2)}) collective-permute-start(bf16[160,256]{1,0:T(8,128)(2,1)S(1)} %pad_maximum_fusion.refs_6_), channel_id=1, source_target_pairs={{0,4},{1,5},{2,6},{3,7},{4,0},{5,1},{6,2},{7,3},{8,12},{9,13},{10,... | collective-permute-start | bytes 245768 | tf_op jit(solution)/shard_map/ppermute | solution.py:18
  15.6 5.9 %collective-permute-start.6 = (bf16[160,256]{1,0:T(8,128)(2,1)S(1)}, bf16[160,256]{1,0:T(8,128)(2,1)S(1)}, u32[]{:S(2)}, u32[]{:S(2)}) collective-permute-start(bf16[160,256]{1,0:T(8,128)(2,1)S(1)} %pad_maximum_fusion.refs_6_), channel_id=1, source_target_pairs={{0,2},{1,3},{2,0},{3,1},{4,6},{5,7},{6,4},{7,5},{8,10},{9,11},{10,... | collective-permute-start | bytes 245768 | tf_op jit(solution)/shard_map/ppermute | solution.py:18
  16.4 5.9 %collective-permute-start.1 = (bf16[40,1024]{1,0:T(8,128)(2,1)S(1)}, bf16[40,1024]{1,0:T(8,128)(2,1)S(1)}, u32[]{:S(2)}, u32[]{:S(2)}) collective-permute-start(bf16[40,1024]{1,0:T(8,128)(2,1)S(1)} %get-tuple-element.12), channel_id=1, source_target_pairs={{0,16},{8,24},{16,0},{24,8},{1,17},{9,25},{17,1},{25,9},{2,18},{10... | collective-permute-start | bytes 245768 | tf_op jit(solution)/shard_map/ppermute | solution.py:18
  16.8 5.5 %collective-permute-start.9 = (bf16[160,256]{1,0:T(8,128)(2,1)S(1)}, bf16[160,256]{1,0:T(8,128)(2,1)S(1)}, u32[]{:S(2)}, u32[]{:S(2)}) collective-permute-start(bf16[160,256]{1,0:T(8,128)(2,1)S(1)} %pad_maximum_fusion.refs_6_), channel_id=1, source_target_pairs={{0,1},{1,0},{2,3},{3,2},{4,5},{5,4},{6,7},{7,6},{8,9},{9,8},{10,11... | collective-permute-start | bytes 245768 | tf_op jit(solution)/shard_map/ppermute | solution.py:18
  18.3 4.1 %collective-permute-start.12 = (bf16[160,256]{1,0:T(8,128)(2,1)S(1)}, bf16[160,256]{1,0:T(8,128)(2,1)S(1)}, u32[]{:S(2)}, u32[]{:S(2)}) collective-permute-start(bf16[160,256]{1,0:T(8,128)(2,1)S(1)} %collective-permute-done.8.refs_9_), channel_id=1, source_target_pairs={{0,1},{1,0},{2,3},{3,2},{4,5},{5,4},{6,7},{7,6},{8,9},{9,8},{10,11... | collective-permute-start | bytes 245768 | tf_op jit(solution)/shard_map/ppermute | solution.py:18
  21.5 1.3 %collective-permute-start.11 = (bf16[160,256]{1,0:T(8,128)(2,1)S(1)}, bf16[160,256]{1,0:T(8,128)(2,1)S(1)}, u32[]{:S(2)}, u32[]{:S(2)}) collective-permute-start(bf16[160,256]{1,0:T(8,128)(2,1)S(1)} %collective-permute-done.7.refs_8_), channel_id=1, source_target_pairs={{0,1},{1,0},{2,3},{3,2},{4,5},{5,4},{6,7},{7,6},{8,9},{9,8},{10,11... | collective-permute-start | bytes 245768 | tf_op jit(solution)/shard_map/ppermute | solution.py:18
  21.5 1.4 %collective-permute-start.10 = (bf16[160,256]{1,0:T(8,128)(2,1)S(1)}, bf16[160,256]{1,0:T(8,128)(2,1)S(1)}, u32[]{:S(2)}, u32[]{:S(2)}) collective-permute-start(bf16[160,256]{1,0:T(8,128)(2,1)S(1)} %collective-permute-done.6.refs_7_), channel_id=1, source_target_pairs={{0,1},{1,0},{2,3},{3,2},{4,5},{5,4},{6,7},{7,6},{8,9},{9,8},{10,11... | collective-permute-start | bytes 245768 | tf_op jit(solution)/shard_map/ppermute | solution.py:18
  22.9 3.4 %copy-start = (bf16[1024,4096]{1,0:T(8,128)(2,1)S(1)}, bf16[1024,4096]{1,0:T(8,128)(2,1)}, u32[]{:S(2)}) copy-start(bf16[1024,4096]{1,0:T(8,128)(2,1)} %refs_14_.1) | copy-start | bytes 25165828
  31.1 10.6 %collective-permute-start.14 = (bf16[160,1024]{1,0:T(8,128)(2,1)S(1)}, bf16[160,1024]{1,0:T(8,128)(2,1)S(1)}, u32[]{:S(2)}, u32[]{:S(2)}) collective-permute-start(bf16[160,1024]{1,0:T(8,128)(2,1)S(1)} %fusion.6), channel_id=1, source_target_pairs={{0,8},{8,0},{16,24},{24,16},{1,9},{9,1},{17,25},{25,17},{2,10},{10... | collective-permute-start | bytes 983048 | tf_op jit(solution)/shard_map/ppermute | solution.py:18
  32.7 16.7 %collective-permute-start.15 = (bf16[160,1024]{1,0:T(8,128)(2,1)S(1)}, bf16[160,1024]{1,0:T(8,128)(2,1)S(1)}, u32[]{:S(2)}, u32[]{:S(2)}) collective-permute-start(bf16[160,1024]{1,0:T(8,128)(2,1)S(1)} %fusion.9), channel_id=1, source_target_pairs={{0,16},{8,24},{16,0},{24,8},{1,17},{9,25},{17,1},{25,9},{2,18},{10... | collective-permute-start | bytes 983048 | tf_op jit(solution)/shard_map/ppermute | solution.py:18
  33.2 16.2 %collective-permute-start.13 = (bf16[160,1024]{1,0:T(8,128)(2,1)S(1)}, bf16[160,1024]{1,0:T(8,128)(2,1)S(1)}, u32[]{:S(2)}, u32[]{:S(2)}) collective-permute-start(bf16[160,1024]{1,0:T(8,128)(2,1)S(1)} %get-tuple-element.7), channel_id=1, source_target_pairs={{0,24},{8,16},{16,8},{24,0},{1,25},{9,17},{17,9},{25,1},{2,26},{10... | collective-permute-start | bytes 983048 | tf_op jit(solution)/shard_map/ppermute | solution.py:18

commit v2 on v0

--- a/solution.py
+++ b/solution.py
@@ -1,18 +1,338 @@
+import functools
+import math
+
 import jax
 import jax.numpy as jnp
 from jax import lax
+from jax.experimental import pallas as pl
+from jax.experimental.pallas import tpu as pltpu
 from jax.sharding import PartitionSpec as P
 
 D_HEAD = 128
-
-
 NEG_FILL = -1e30
+ROOMY = 42
+FETCHES = 8
+EXP2_SCALE = D_HEAD ** (-0.5) * math.log2(math.e)
+
+
+def swap(x, axis, flip, size):
+    return lax.ppermute(x, axis, [(i, i ^ flip) for i in range(size)])
 
 
 def lookup_positions(order, flat_rows, span):
     table = jnp.arange(order.shape[0], dtype=jnp.int32)
     hits = (flat_rows // span)[:, None] == table[None, :]
     return jnp.sum(jnp.where(hits, order[None, :], 0), axis=1) * span + flat_rows % span
+
+
+def stack_heads(q_ref, heads):
+    q = q_ref[...].astype(jnp.float32)
+    q = jnp.concatenate([q[:, h * D_HEAD : (h + 1) * D_HEAD] for h in range(heads)], axis=0)
+    return q.astype(jnp.bfloat16)
+
+
+def prepare_kernel(span, n_head, chunk_flips, order_ref, weight_ref, after_ref, *refs):
+    q_refs, (weight_out, bias_ref, q_out, sems) = refs[:n_head], refs[n_head:]
+    me, ctx = lax.axis_index("head"), lax.axis_index("ctx")
+    step = weight_ref.shape[0] // FETCHES
+    fetches = [
+        pltpu.make_async_copy(
+            weight_ref.at[i * step : (i + 1) * step], weight_out.at[i * step : (i + 1) * step], sems.at[i]
+        )
+        for i in range(FETCHES)
+    ]
+
+    @pl.when(me >= 0)
+    def start():
+        for fetch in fetches:
+            fetch.start()
+
+    n_keys = bias_ref.shape[1]
+    lane = lax.broadcasted_iota(jnp.int32, (1, n_keys), 1)
+    kpos = lane
+    for i, flip in enumerate(chunk_flips):
+        for k in range(n_head):
+            first = (i * n_head + k) * span
+            block = order_ref[(ctx ^ flip) * n_head + (me ^ k)]
+            kpos = jnp.where(lane >= first, lane + (block * span - first), kpos)
+    row = lax.broadcasted_iota(jnp.int32, (span, 1), 0)
+    for k in range(n_head):
+        qpos = row + order_ref[ctx * n_head + (me ^ k)] * span
+        bias_ref[k * span : (k + 1) * span, :] = jnp.where(kpos <= qpos, 0.0, NEG_FILL)
+        q_out[k] = stack_heads(q_refs[k], q_refs[k].shape[1] // D_HEAD)
+    for fetch in fetches:
+        fetch.wait()
+
+
+def prepare(order, weight, after, q_pieces, chunk_flips, n_keys):
+    n_head = len(q_pieces)
+    span, width = q_pieces[0].shape
+    vmem = pl.BlockSpec(memory_space=pltpu.VMEM)
+    return pl.pallas_call(
+        functools.partial(prepare_kernel, span, n_head, chunk_flips),
+        out_shape=(
+            jax.ShapeDtypeStruct(weight.shape, weight.dtype),
+            jax.ShapeDtypeStruct((span * n_head, n_keys), jnp.float32),
+            jax.ShapeDtypeStruct((n_head, span * width // D_HEAD, D_HEAD), jnp.bfloat16),
+        ),
+        in_specs=[
+            pl.BlockSpec(memory_space=pltpu.SMEM),
+            pl.BlockSpec(memory_space=pltpu.HBM),
+            pl.BlockSpec(memory_space=pl.ANY),
+        ]
+        + [vmem] * n_head,
+        out_specs=(vmem,) * 3,
+        scratch_shapes=[pltpu.SemaphoreType.DMA((FETCHES,))],
+        compiler_params=pltpu.CompilerParams(vmem_limit_bytes=ROOMY * 1024 * 1024),
+        cost_estimate=pl.CostEstimate(flops=0, bytes_accessed=4 * 1024 * 1024, transcendentals=0),
+    )(order, weight, after, *q_pieces)
+
+
+def project(attn, weight_ref, me, flip, cols):
+    at = pl.multiple_of((me ^ flip) * cols, cols)
+    part = jnp.dot(attn, weight_ref[:, pl.ds(at, cols)], preferred_element_type=jnp.float32)
+    return part.astype(jnp.bfloat16)
+
+
+def gather_keys(kv_refs, k_s, v_s):
+    rows = kv_refs[0].shape[0]
+    for i, ref in enumerate(kv_refs):
+        k_s[i * rows : (i + 1) * rows, :] = ref[:, :D_HEAD]
+        v_s[i * rows : (i + 1) * rows, :] = ref[:, D_HEAD:]
+
+
+def masked_scores(q, k_s, bias):
+    scores = lax.dot_general(
+        q, k_s[...], (((1,), (1,)), ((), ())), preferred_element_type=jnp.float32
+    )
+    span, n_keys = bias.shape
+    return scores.reshape(-1, span, n_keys) + bias[None]
+
+
+def mix_values(weights, v_s):
+    heads, span, n_keys = weights.shape
+    mixed = jnp.dot(
+        weights.reshape(heads * span, n_keys), v_s[...], preferred_element_type=jnp.float32
+    )
+    return mixed.reshape(heads, span, D_HEAD)
+
+
+def staged(n_piece, score, weigh, finish):
+    scores, held = score(0), None
+    for piece in range(n_piece):
+        ahead = score(piece + 1) if piece + 1 < n_piece else None
+        weights = weigh(piece, scores)
+        if held is not None:
+            finish(piece - 1, *held)
+        scores, held = ahead, weights
+    finish(n_piece - 1, *held)
+
+
+def early_kernel(span, n_piece, n_chunk, *refs):
+    bias_ref, q_ref = refs[:2]
+    kv_refs = refs[2 : 2 + n_chunk]
+    peak_ref, denom_ref, mixed_ref, k_s, v_s = refs[2 + n_chunk :]
+    gather_keys(kv_refs, k_s, v_s)
+    n_keys = k_s.shape[0]
+
+    def score(piece):
+        return masked_scores(q_ref[piece], k_s, bias_ref[piece * span : (piece + 1) * span, :n_keys])
+
+    def weigh(piece, scores):
+        peak = jnp.max(scores, axis=2, keepdims=True)
+        weights = jnp.exp2((scores - peak) * EXP2_SCALE)
+        peak_ref[piece] = peak
+        denom_ref[piece] = jnp.sum(weights, axis=2, keepdims=True)
+        return (weights.astype(jnp.bfloat16),)
+
+    def finish(piece, weights):
+        mixed_ref[piece] = mix_values(weights, v_s)
+
+    staged(n_piece, score, weigh, finish)
+
+
+def early_attend(bias, q_all, kv_chunks):
+    n_chunk, (n_piece, stacked, depth) = len(kv_chunks), q_all.shape
+    span = bias.shape[0] // n_piece
+    heads = stacked // span
+    n_keys = kv_chunks[0].shape[0] * n_chunk
+    vmem = pl.BlockSpec(memory_space=pltpu.VMEM)
+    column = jax.ShapeDtypeStruct((n_piece, heads, span, 1), jnp.float32)
+    return pl.pallas_call(
+        functools.partial(early_kernel, span, n_piece, n_chunk),
+        out_shape=(column, column, jax.ShapeDtypeStruct((n_piece, heads, span, depth), jnp.float32)),
+        in_specs=[vmem] * (2 + n_chunk),
+        out_specs=(vmem,) * 3,
+        scratch_shapes=[pltpu.VMEM((n_keys, D_HEAD), jnp.bfloat16)] * 2,
+        compiler_params=pltpu.CompilerParams(vmem_limit_bytes=20 * 1024 * 1024),
+        cost_estimate=pl.CostEstimate(
+            flops=4 * n_piece * stacked * depth * n_keys,
+            bytes_accessed=4 * 1024 * 1024,
+            transcendentals=n_piece * stacked * n_keys,
+        ),
+    )(bias, q_all, *kv_chunks)
+
+
+def attend_kernel(span, n_piece, n_chunk, *refs):
+    bias_ref, q_ref = refs[:2]
+    kv_refs = refs[2 : 2 + n_chunk]
+    rest = refs[2 + n_chunk :]
+    peak_ref, denom_ref, mixed_ref, weight_ref, attn_ref, low_ref, high_ref = rest[:7]
+    k_s, v_s, a_s = rest[7:]
+    me = lax.axis_index("head")
+    gather_keys(kv_refs, k_s, v_s)
+    n_keys = k_s.shape[0]
+
+    def score(piece):
+        return masked_scores(q_ref[piece], k_s, bias_ref[piece * span : (piece + 1) * span, n_keys:])
+
+    def weigh(piece, scores):
+        peak = jnp.maximum(peak_ref[piece], jnp.max(scores, axis=2, keepdims=True))
+        weights = jnp.exp2((scores - peak) * EXP2_SCALE)
+        factor = jnp.exp2((peak_ref[piece] - peak) * EXP2_SCALE)
+        denom = factor * denom_ref[piece] + jnp.sum(weights, axis=2, keepdims=True)
+        return weights.astype(jnp.bfloat16), factor, denom
+
+    def finish(piece, weights, factor, denom):
+        mixed = (factor * mixed_ref[piece] + mix_values(weights, v_s)) / denom
+        at = pl.multiple_of((me ^ piece) * span, span)
+        for h in range(mixed.shape[0]):
+            a_s[pl.ds(at, span), h * D_HEAD : (h + 1) * D_HEAD] = mixed[h]
+
+    staged(n_piece, score, weigh, finish)
+    attn = a_s[...].astype(jnp.bfloat16)
+    attn_ref[...] = attn
+    part = project(attn, weight_ref, me, 3, low_ref.shape[1])
+    half = low_ref.shape[0]
+    low_ref[...] = part[:half]
+    high_ref[...] = part[half:]
+
+
+def attend(bias, kv_chunks, state, weight):
+    n_chunk = len(kv_chunks)
+    n_piece, heads, span, depth = state[-1].shape
+    width = heads * depth
+    seg = span * n_piece
+    n_keys = kv_chunks[0].shape[0] * n_chunk
+    cols = weight.shape[1] // n_piece
+    vmem = pl.BlockSpec(memory_space=pltpu.VMEM)
+    half = jax.ShapeDtypeStruct((seg // 2, cols), jnp.bfloat16)
+    return pl.pallas_call(
+        functools.partial(attend_kernel, span, n_piece, n_chunk),
+        out_shape=(jax.ShapeDtypeStruct((seg, width), jnp.bfloat16), half, half),
+        in_specs=[vmem] * (6 + n_chunk),
+        out_specs=(vmem, vmem, vmem),
+        scratch_shapes=[
+            pltpu.VMEM((n_keys, D_HEAD), jnp.bfloat16),
+            pltpu.VMEM((n_keys, D_HEAD), jnp.bfloat16),
+            pltpu.VMEM((seg, width), jnp.float32),
+        ],
+        compiler_params=pltpu.CompilerParams(vmem_limit_bytes=28 * 1024 * 1024),
+        cost_estimate=pl.CostEstimate(
+            flops=4 * seg * width * n_keys + 2 * seg * width * cols,
+            bytes_accessed=4 * 1024 * 1024,
+            transcendentals=seg * heads * n_keys,
+        ),
+    )(bias, state[0], *kv_chunks, *state[1:], weight)
+
+
+def project_kernel(flips, attn_ref, weight_ref, *out_refs):
+    me = lax.axis_index("head")
+    half, cols = out_refs[0].shape
+    for i, flip in enumerate(flips):
+        part = project(attn_ref[...], weight_ref, me, flip, cols)
+        out_refs[2 * i][...] = part[:half]
+        out_refs[2 * i + 1][...] = part[half:]
+
+
+def project_rest(attn, weight, flips, n_head):
+    seg, width = attn.shape
+    n, cols = len(flips), weight.shape[1] // n_head
+    vmem = pl.BlockSpec(memory_space=pltpu.VMEM)
+    half = jax.ShapeDtypeStruct((seg // 2, cols), jnp.bfloat16)
+    return pl.pallas_call(
+        functools.partial(project_kernel, flips),
+        out_shape=(half,) * (2 * n),
+        in_specs=[vmem, vmem],
+        out_specs=(vmem,) * (2 * n),
+        compiler_params=pltpu.CompilerParams(vmem_limit_bytes=20 * 1024 * 1024),
+        cost_estimate=pl.CostEstimate(
+            flops=2 * seg * width * cols * n,
+            bytes_accessed=2 * width * cols * n,
+            transcendentals=0,
+        ),
+    )(attn, weight)
+
+
+def add_kernel(a_ref, b_ref, out_ref):
+    out_ref[...] = (a_ref[...].astype(jnp.float32) + b_ref[...].astype(jnp.float32)).astype(jnp.bfloat16)
+
+
+def add_pair(a, b):
+    vmem = pl.BlockSpec(memory_space=pltpu.VMEM)
+    return pl.pallas_call(
+        add_kernel,
+        out_shape=jax.ShapeDtypeStruct(a.shape, jnp.bfloat16),
+        in_specs=[vmem, vmem],
+        out_specs=vmem,
+        compiler_params=pltpu.CompilerParams(vmem_limit_bytes=6 * 1024 * 1024),
+        cost_estimate=pl.CostEstimate(flops=a.size, bytes_accessed=6 * a.size, transcendentals=0),
+    )(a, b)
+
+
+def final_kernel(*refs):
+    out_ref = refs[-1]
+    half = out_ref.shape[0] // 2
+    for i in range(2):
+        total = sum(ref[...].astype(jnp.float32) for ref in refs[3 * i : 3 * i + 3])
+        out_ref[i * half : (i + 1) * half, :] = total.astype(jnp.bfloat16)
+
+
+def final_sum(low, high):
+    vmem = pl.BlockSpec(memory_space=pltpu.VMEM)
+    rows, cols = low[0].shape
+    return pl.pallas_call(
+        final_kernel,
+        out_shape=jax.ShapeDtypeStruct((2 * rows, cols), jnp.bfloat16),
+        in_specs=[vmem] * 6,
+        out_specs=vmem,
+        compiler_params=pltpu.CompilerParams(vmem_limit_bytes=6 * 1024 * 1024),
+        cost_estimate=pl.CostEstimate(flops=4 * rows * cols, bytes_accessed=16 * rows * cols, transcendentals=0),
+    )(*low, *high)
+
+
+def fast_path(queries, key_rows, value_rows, stretch_order, out_weight, n_head, n_ctx):
+    me = lax.axis_index("head")
+
+    def cut(x, k):
+        width = x.shape[2] // n_head
+        return lax.dynamic_slice_in_dim(x[0], (me ^ k) * width, width, 1)
+
+    kv_cut = [
+        jnp.concatenate([cut(key_rows, k), cut(value_rows, k)], axis=1) for k in range(n_head)
+    ]
+    q_cut = [cut(queries, k) for k in range(n_head)]
+    kv_in = [kv_cut[0]] + [swap(kv_cut[k], "head", k, n_head) for k in range(1, n_head)]
+    own = jnp.concatenate(kv_in, axis=0)
+    q_in = [q_cut[0]] + [swap(q_cut[k], "head", k, n_head) for k in range(1, n_head)]
+    flips = [2 * dz for dz in range(n_ctx // 2)]
+    chunk_flips = tuple(flips + [f ^ 1 for f in flips])
+    weight, bias, q_all = prepare(stretch_order, out_weight, own, q_in, chunk_flips, own.shape[0] * n_ctx)
+    far_keys = [swap(own, "ctx", f, n_ctx) for f in flips[1:]]
+    far_keys, bias = lax.optimization_barrier((far_keys, bias))
+    same_core = [own] + far_keys
+    other_core = [swap(x, "ctx", 1, n_ctx) for x in same_core]
+    state = early_attend(bias, q_all, same_core)
+    attn, far_low, far_high = attend(bias, other_core, (q_all, *state), weight)
+    x_far = swap(far_low, "head", 1, n_head)
+    y_far = swap(far_high, "head", 2, n_head)
+    x_low, x_high, y_low, y_high = project_rest(attn, weight, (1, 2), n_head)
+    x_near = swap(x_low, "head", 1, n_head)
+    y_near = swap(y_high, "head", 2, n_head)
+    own_low, own_high = project_rest(attn, weight, (0,), n_head)
+    y_sum = swap(add_pair(y_low, x_far), "head", 2, n_head)
+    x_sum = swap(add_pair(x_high, y_far), "head", 1, n_head)
+    return final_sum((own_low, x_near, y_sum), (own_high, y_near, x_sum))
 
 
 def attend_block(state, query_heads, query_pos, key_block, value_block, key_pos):
@@ -57,13 +377,12 @@
     return state
 
 
-def on_device(queries, key_rows, value_rows, stretch_order, out_weight):
-    head_count = lax.axis_size("head")
+def long_path(queries, key_rows, value_rows, stretch_order, out_weight, n_head):
     ctx_index = lax.axis_index("ctx")
     span = queries.shape[1]
-    seg_rows = span * head_count
-    kv_local = key_rows.shape[2] // D_HEAD // head_count
-    q_local = queries.shape[2] // D_HEAD // head_count
+    seg_rows = span * n_head
+    kv_local = key_rows.shape[2] // D_HEAD // n_head
+    q_local = queries.shape[2] // D_HEAD // n_head
     groups = q_local // kv_local
     query_flat = ctx_index * seg_rows + jnp.arange(seg_rows, dtype=jnp.int32)
     query_pos = lookup_positions(stretch_order, query_flat, span)
@@ -78,21 +397,11 @@
         lax.all_to_all(value_rows, "head", split_axis=2, concat_axis=1, tiled=True),
     )
     query_heads = query_ex[0].reshape(seg_rows, kv_local, groups, D_HEAD)
-    piece = (
-        lax.all_gather(key_ex[0], "ctx", axis=0, tiled=True),
-        lax.all_gather(value_ex[0], "ctx", axis=0, tiled=True),
-    )
-    flat_rows = jnp.arange(piece[0].shape[0], dtype=jnp.int32)
+    keys = lax.all_gather(key_ex[0], "ctx", axis=0, tiled=True)
+    values = lax.all_gather(value_ex[0], "ctx", axis=0, tiled=True)
+    flat_rows = jnp.arange(keys.shape[0], dtype=jnp.int32)
     final = fold_piece(
-        initial,
-        query_heads,
-        query_pos,
-        piece[0],
-        piece[1],
-        flat_rows,
-        stretch_order,
-        span,
-        kv_local,
+        initial, query_heads, query_pos, keys, values, flat_rows, stretch_order, span, kv_local
     )
     run_max, run_sum, run_acc = final
     mixed = run_acc / run_sum[..., None]
@@ -108,6 +417,13 @@
 
 
 def solution(mesh):
+    n_head, n_ctx = mesh.shape["head"], mesh.shape["ctx"]
+
+    def on_device(*args):
+        if n_ctx <= 8:
+            return fast_path(*args, n_head, n_ctx)
+        return long_path(*args, n_head)
+
     return jax.shard_map(
         on_device,
         mesh=mesh,

time: 142 us -> 41.1 us (0.29)
  blocking collectives: 30.1 us -> 0 us
  other arithmetic: 29.2 us -> 0.02 us
  waiting for transfers between devices: 31.1 us -> 5.2 us
  local copies, waits for them, and re-layouts: 17.8 us -> 2.51 us
  between operations: 13.7 us -> 0.14 us
  Pallas kernels: 0 us -> 11.1 us
  starting transfers between devices: 13.6 us -> 21.9 us
  matrix products: 6.23 us -> 0 us
    reduce_scatter x1 -> x0, waiting for transfers between devices: 31.1 us -> none  [on_device(): lax.psum_scatter(partial_out, 'head', scatter_dimension=1, tiled=True)]
    all_gather x2 -> x0, blocking collectives: 30.1 us -> none  [the longest x1 15.6 us: on_device(): lax.all_gather(value_ex[0], 'ctx', axis=0, tiled=True)]
    unnamed x4 -> x0, other arithmetic: 25.3 us -> none
    ppermute x0 -> x19, starting transfers between devices: none -> 21.9 us  [swap(): return lax.ppermute(x, axis, [(i, i ^ flip) for i in range(size)])]
    unnamed x17 -> x2, local copies, waits for them, and re-layouts: 15 us -> 0.65 us
    all_to_all x3 -> x0, starting transfers between devices: 13.5 us -> none  [the longest x1 5.16 us: on_device(): lax.all_to_all(key_rows, 'head', split_axis=2, concat_axis=1, tiled=True)]
    pallas_call x0 -> x8, Pallas kernels: none -> 11.1 us  [the longest x1 4.02 us: prepare(): pl.pallas_call(functools.partial(prepare_kernel, span, n_head, chunk_flip...]
    dot_general x3 -> x0, matrix products: 6.23 us -> none  [the longest x1 2.64 us: on_device(): jnp.dot(attn, out_weight, preferred_element_type=jnp.float32)]
  transfers between devices with their start and end apart: 4 -> 19, of which waited for: 1 -> 4; matrix products, arithmetic and copies ran while one was open for 25% -> 3% of each run, Pallas kernels for 0% -> 17%
where the time goes in v2:
time: 41.1 us; the launch traced here: 40.9 us
  starting transfers between devices  21.9 us (53%)
  Pallas kernels  11.1 us (27%)
  waiting for transfers between devices  5.2 us (13%)
  local copies, waits for them, and re-layouts  2.51 us (6%)
    ppermute x19, starting transfers between devices, swap(): return lax.ppermute(x, axis, [(i, i ^ flip) for i in range(size)])  21.9 us
    ppermute x19, waiting for transfers between devices, swap(): return lax.ppermute(x, axis, [(i, i ^ flip) for i in range(size)])  5.2 us
    pallas_call x1, Pallas kernels, prepare(): pl.pallas_call(functools.partial(prepare_kernel, span, n_head, chunk_flip...  4.02 us
    pallas_call x1, Pallas kernels, attend(): pl.pallas_call(functools.partial(attend_kernel, span, n_piece, n_chunk),...  3.2 us
    dynamic_slice x2, local copies, waits for them, and re-layouts, cut(): return lax.dynamic_slice_in_dim(x[0], (me ^ k) * width, width, 1)  1.86 us
    pallas_call x1, Pallas kernels, early_attend(): pl.pallas_call(functools.partial(early_kernel, span, n_piece, n_chunk), o...  1.53 us
    pallas_call x2, Pallas kernels, project_rest(): pl.pallas_call(functools.partial(project_kernel, flips), out_shape=(half,...  1.39 us
    pallas_call x1, Pallas kernels, final_sum(): pl.pallas_call(final_kernel, out_shape=jax.ShapeDtypeStruct((2 * rows, co...  0.84 us
  transfers between devices with their start and end apart: 19, of which 4 were waited for; matrix products, arithmetic and copies ran while one was open for 3% of the time, Pallas kernels for 17%

profile of v2, /device:TPU:0, one launch (start us, length us, event | category | flops | bytes accessed | tf_op | source)
XLA Modules:
  0.0 40.9 jit_solution(12085524398762774028)
XLA Ops:
  0.0 0.8 %dynamic-slice_bitcast_fusion.10 = (bf16[40,128]{1,0:T(8,128)(2,1)S(1)}, bf16[40,128]{1,0:T(8,128)(2,1)S(1)}, bf16[40,128]{1,0:T(8,128)(2,1)S(1)}, bf16[40,128]{...) fusion(bf16[1,40,512]{2,1,0:T(8,128)(2,1)} %param.7, ...), kind=kLoop, calls=%fused_computation.14 | loop fusion | bytes 163856 | tf_op jit(solution)/shard_map/dynamic_slice | solution.py:309
  0.8 3.0 %collective-permute-start.1 = (bf16[40,256]{1,0:T(8,128)(2,1)S(1)}, bf16[40,256]{1,0:T(8,128)(2,1)S(1)}, u32[]{:S(2)}, u32[]{:S(2)}) collective-permute-start(bf16[40,256]{1,0:T(8,128)(2,1)S(1)} %pad_maximum_fusion.2), channel_id=1, source_target_pairs={{0,16},{8,24},{16,0},{24,8},{1,17},{9,25},{17,1},{25,9},{2,18},{10... | collective-permute-start | bytes 61448 | tf_op jit(solution)/shard_map/ppermute | solution.py:19
  3.9 1.4 %collective-permute-start.2 = (bf16[40,256]{1,0:T(8,128)(2,1)S(1)}, bf16[40,256]{1,0:T(8,128)(2,1)S(1)}, u32[]{:S(2)}, u32[]{:S(2)}) collective-permute-start(bf16[40,256]{1,0:T(8,128)(2,1)S(1)} %pad_maximum_fusion.3), channel_id=1, source_target_pairs={{0,24},{8,16},{16,8},{24,0},{1,25},{9,17},{17,9},{25,1},{2,26},{10... | collective-permute-start | bytes 61448 | tf_op jit(solution)/shard_map/ppermute | solution.py:19
  5.3 0.1 collective-permute-start
  5.5 1.0 %dynamic-slice_bitcast_fusion = (bf16[40,1024]{1,0:T(8,128)(2,1)S(1)}, bf16[40,1024]{1,0:T(8,128)(2,1)S(1)}, bf16[40,1024]{1,0:T(8,128)(2,1)S(1)}, bf16[40,1024]{1,0:T(8,128)(2,1)S(1)}) fusion(bf16[1,40,4096]{2,1,0:T(8,128)(2,1)} %param.5, s32[]{:T(128)S(6)} %select_n.35, s32[]{:T(128)S(6)} %select_n.33, s32[]{:T(128)S(6)} %select_n.32, s32[]{:T(128)S(6)} %select_n.34), kind=kLoop, calls=%fused_computation.1 | loop fusion | bytes 655376 | tf_op jit(solution)/shard_map/dynamic_slice | solution.py:309
  6.5 2.9 %collective-permute-start.8 = (bf16[40,1024]{1,0:T(8,128)(2,1)S(1)}, bf16[40,1024]{1,0:T(8,128)(2,1)S(1)}, u32[]{:S(2)}, u32[]{:S(2)}) collective-permute-start(bf16[40,1024]{1,0:T(8,128)(2,1)S(1)} %get-tuple-element.43), channel_id=1, source_target_pairs={{0,24},{8,16},{16,8},{24,0},{1,25},{9,17},{17,9},{25,1},{2,26},{10... | collective-permute-start | bytes 245768 | tf_op jit(solution)/shard_map/ppermute | solution.py:19
  9.4 0.5 %collective-permute-start.6 = (bf16[40,1024]{1,0:T(8,128)(2,1)S(1)}, bf16[40,1024]{1,0:T(8,128)(2,1)S(1)}, u32[]{:S(2)}, u32[]{:S(2)}) collective-permute-start(bf16[40,1024]{1,0:T(8,128)(2,1)S(1)} %get-tuple-element.44), channel_id=1, source_target_pairs={{0,8},{8,0},{16,24},{24,16},{1,9},{9,1},{17,25},{25,17},{2,10},{10... | collective-permute-start | bytes 245768 | tf_op jit(solution)/shard_map/ppermute | solution.py:19
  9.9 0.0 collective-permute-done.1
  9.9 0.1 collective-permute-start.7
  10.1 4.1 %collective-permute-start.5 = (bf16[160,256]{1,0:T(8,128)(2,1)S(1)}, bf16[160,256]{1,0:T(8,128)(2,1)S(1)}, u32[]{:S(2)}, u32[]{:S(2)}) collective-permute-start(bf16[160,256]{1,0:T(8,128)(2,1)S(1)} %pad_maximum_fusion.after_ref.refs_2_), channel_id=1, source_target_pairs={{0,6},{1,7},{2,4},{3,5},{4,2},{5,3},{6,0},{7,1},{8,14},{9,15},{10,... | collective-permute-start | bytes 245768 | tf_op jit(solution)/shard_map/ppermute | solution.py:19
  14.1 0.6 %collective-permute-start.3 = (bf16[160,256]{1,0:T(8,128)(2,1)S(1)}, bf16[160,256]{1,0:T(8,128)(2,1)S(1)}, u32[]{:S(2)}, u32[]{:S(2)}) collective-permute-start(bf16[160,256]{1,0:T(8,128)(2,1)S(1)} %pad_maximum_fusion.after_ref.refs_2_), channel_id=1, source_target_pairs={{0,2},{1,3},{2,0},{3,1},{4,6},{5,7},{6,4},{7,5},{8,10},{9,11},{10,... | collective-permute-start | bytes 245768 | tf_op jit(solution)/shard_map/ppermute | solution.py:19
  14.8 0.0 copy-start
  14.8 0.6 %copy-done = s32[32]{0:T(128)S(1)} copy-done((s32[32]{0:T(128)S(1)}, s32[32]{0:T(128)}, u32[]{:S(2)}) %copy-start) | copy-done | bytes 152
  15.5 4.0 %shard_map.55 = (bf16[1024,4096]{1,0:T(8,128)(2,1)S(1)}, f32[160,1280]{1,0:T(8,128)S(1)}, bf16[4,320,128]{2,1,0:T(8,128)(2,1)S(1)}) custom-call(s32[32]{0:T(128)S(1)} %copy-done, bf16[1024,4096]{1,0:T(8,128)(2,1)} %weight_ref.1, bf16[160,256]{1,0:T(8,128)(2,1)S(1)} %pad_maximum_fusion.after_ref.refs_2_, bf16[40,1024]{1,0:T(8,128)(2,1)S(1)} %get-tuple-element.45.refs_0_, ...), custom_call_target="tpu_custom_call" | custom-call | bytes 4194304 | tf_op jit(solution)/shard_map/pallas_call | solution.py:71
  19.5 0.3 collective-permute-done.4.refs_4_
  19.8 0.3 collective-permute-start.10
  20.1 0.2 collective-permute-start.11
  20.3 0.3 collective-permute-start.12
  20.6 1.5 %shard_map.56 = (f32[4,8,40,1]{3,2,1,0:T(8,128)S(1)}, f32[4,8,40,1]{3,2,1,0:T(8,128)S(1)}, f32[4,8,40,128]{3,2,1,0:T(8,128)S(1)}) custom-call(f32[160,1280]{1,0:T(8,128)S(1)} %get-tuple-element.25.refs_0_, bf16[4,320,128]{2,1,0:T(8,128)(2,1)S(1)} %get-tuple-element.26.refs_1_, bf16[160,256]{1,0:T(8,128)(2,1)S(1)} %pad_maximum_fusion.after_ref.refs_2_, ...), custom_call_target="tpu_custom_call" | custom-call | flops 419430400 | bytes 4194304 | tf_op jit(solution)/shard_map/pallas_call | solution.py:161
  22.2 3.2 %shard_map.57 = (bf16[160,1024]{1,0:T(8,128)(2,1)S(1)}, bf16[80,1024]{1,0:T(8,128)(2,1)S(1)}, bf16[80,1024]{1,0:T(8,128)(2,1)S(1)}) custom-call(f32[160,1280]{1,0:T(8,128)S(1)} %get-tuple-element.25.refs_0_, bf16[4,320,128]{2,1,0:T(8,128)(2,1)S(1)} %get-tuple-element.26.refs_1_, bf16[160,256]{1,0:T(8,128)(2,1)S(1)} %collective-permute-done.9.refs_2_, ...), custom_call_target="tpu_custom_call" | custom-call | flops 754974720 | bytes 4194304 | tf_op jit(solution)/shard_map/pallas_call | solution.py:220
  25.4 1.7 %collective-permute-start.14 = (bf16[80,1024]{1,0:T(8,128)(2,1)S(1)}, bf16[80,1024]{1,0:T(8,128)(2,1)S(1)}, u32[]{:S(2)}, u32[]{:S(2)}) collective-permute-start(bf16[80,1024]{1,0:T(8,128)(2,1)S(1)} %get-tuple-element.38), channel_id=1, source_target_pairs={{0,8},{8,0},{16,24},{24,16},{1,9},{9,1},{17,25},{25,17},{2,10},{10... | collective-permute-start | bytes 491528 | tf_op jit(solution)/shard_map/ppermute | solution.py:19
  27.1 1.5 %collective-permute-start.17 = (bf16[80,1024]{1,0:T(8,128)(2,1)S(1)}, bf16[80,1024]{1,0:T(8,128)(2,1)S(1)}, u32[]{:S(2)}, u32[]{:S(2)}) collective-permute-start(bf16[80,1024]{1,0:T(8,128)(2,1)S(1)} %get-tuple-element.42), channel_id=1, source_target_pairs={{0,16},{8,24},{16,0},{24,8},{1,17},{9,25},{17,1},{25,9},{2,18},{10... | collective-permute-start | bytes 491528 | tf_op jit(solution)/shard_map/ppermute | solution.py:19
  28.6 0.9 %shard_map.59 = (bf16[80,1024]{1,0:T(8,128)(2,1)S(1)}, bf16[80,1024]{1,0:T(8,128)(2,1)S(1)}, bf16[80,1024]{1,0:T(8,128)(2,1)S(1)}, bf16[80,1024]{1,0:T(8,128)(2,1)S(1)}) custom-call(bf16[160,1024]{1,0:T(8,128)(2,1)S(1)} %get-tuple-element.34.attn_ref, bf16[1024,4096]{1,0:T(8,128)(2,1)S(1)} %get-tuple-element.33.refs_9_.weight_ref), custom_call_target="tpu_custom_call" | custom-call | flops 671088640 | bytes 4194304 | tf_op jit(solution)/shard_map/pallas_call | solution.py:253
  29.5 0.6 %collective-permute-start.13 = (bf16[80,1024]{1,0:T(8,128)(2,1)S(1)}, bf16[80,1024]{1,0:T(8,128)(2,1)S(1)}, u32[]{:S(2)}, u32[]{:S(2)}) collective-permute-start(bf16[80,1024]{1,0:T(8,128)(2,1)S(1)} %get-tuple-element.36), channel_id=1, source_target_pairs={{0,8},{8,0},{16,24},{24,16},{1,9},{9,1},{17,25},{25,17},{2,10},{10... | collective-permute-start | bytes 491528 | tf_op jit(solution)/shard_map/ppermute | solution.py:19
  30.1 0.4 collective-permute-start.16
  30.4 1.3 %collective-permute-done.14.b_ref = bf16[80,1024]{1,0:T(8,128)(2,1)S(1)} collective-permute-done((bf16[80,1024]{1,0:T(8,128)(2,1)S(1)}, bf16[80,1024]{1,0:T(8,128)(2,1)S(1)}, u32[]{:S(2)}, u32[]{:S(2)}) %collective-permute-start.14) | collective-permute-done | bytes 163872 | tf_op jit(solution)/shard_map/ppermute | solution.py:19
  31.8 2.5 %collective-permute-start.15 = (bf16[80,1024]{1,0:T(8,128)(2,1)S(1)}, bf16[80,1024]{1,0:T(8,128)(2,1)S(1)}, u32[]{:S(2)}, u32[]{:S(2)}) collective-permute-start(bf16[80,1024]{1,0:T(8,128)(2,1)S(1)} %shard_map.60), channel_id=1, source_target_pairs={{0,16},{8,24},{16,0},{24,8},{1,17},{9,25},{17,1},{25,9},{2,18},{10... | collective-permute-start | bytes 491528 | tf_op jit(solution)/shard_map/ppermute | solution.py:19
  34.3 1.6 %collective-permute-start.18 = (bf16[80,1024]{1,0:T(8,128)(2,1)S(1)}, bf16[80,1024]{1,0:T(8,128)(2,1)S(1)}, u32[]{:S(2)}, u32[]{:S(2)}) collective-permute-start(bf16[80,1024]{1,0:T(8,128)(2,1)S(1)} %shard_map.61), channel_id=1, source_target_pairs={{0,8},{8,0},{16,24},{24,16},{1,9},{9,1},{17,25},{25,17},{2,10},{10... | collective-permute-start | bytes 491528 | tf_op jit(solution)/shard_map/ppermute | solution.py:19
  35.9 0.5 %shard_map.58 = (bf16[80,1024]{1,0:T(8,128)(2,1)S(1)}, bf16[80,1024]{1,0:T(8,128)(2,1)S(1)}) custom-call(bf16[160,1024]{1,0:T(8,128)(2,1)S(1)} %get-tuple-element.34.attn_ref, bf16[1024,4096]{1,0:T(8,128)(2,1)S(1)} %get-tuple-element.33.refs_9_.weight_ref), custom_call_target="tpu_custom_call" | custom-call | flops 335544320 | bytes 2097152 | tf_op jit(solution)/shard_map/pallas_call | solution.py:253
  36.4 1.1 %collective-permute-done.16.refs_4_ = bf16[80,1024]{1,0:T(8,128)(2,1)S(1)} collective-permute-done((bf16[80,1024]{1,0:T(8,128)(2,1)S(1)}, bf16[80,1024]{1,0:T(8,128)(2,1)S(1)}, u32[]{:S(2)}, u32[]{:S(2)}) %collective-permute-start.16) | collective-permute-done | bytes 163872 | tf_op jit(solution)/shard_map/ppermute | solution.py:19
  37.5 2.5 %collective-permute-done.15.refs_2_ = bf16[80,1024]{1,0:T(8,128)(2,1)S(1)} collective-permute-done((bf16[80,1024]{1,0:T(8,128)(2,1)S(1)}, bf16[80,1024]{1,0:T(8,128)(2,1)S(1)}, u32[]{:S(2)}, u32[]{:S(2)}) %collective-permute-start.15) | collective-permute-done | bytes 163872 | tf_op jit(solution)/shard_map/ppermute | solution.py:19
  40.0 0.8 %shard_map.62 = bf16[160,1024]{1,0:T(8,128)(2,1)} custom-call(bf16[80,1024]{1,0:T(8,128)(2,1)S(1)} %get-tuple-element.35.refs_0_, bf16[80,1024]{1,0:T(8,128)(2,1)S(1)} %collective-permute-done.13.refs_1_, bf16[80,1024]{1,0:T(8,128)(2,1)S(1)} %collective-permute-done.15.refs_2_, bf16[80,1024]{1,0:T(8,128)(2,1)S(1)} %get-tuple-element.39.refs_3_, ...), custom_call_target="tpu_custom_call" | custom-call | flops 327680 | bytes 1310720 | tf_op jit(solution)/shard_map/pallas_call | solution.py:294
  (22 shorter events, 0.1 us)
Async XLA Ops:
  0.8 9.1 %collective-permute-start.1 = (bf16[40,256]{1,0:T(8,128)(2,1)S(1)}, bf16[40,256]{1,0:T(8,128)(2,1)S(1)}, u32[]{:S(2)}, u32[]{:S(2)}) collective-permute-start(bf16[40,256]{1,0:T(8,128)(2,1)S(1)} %pad_maximum_fusion.2), channel_id=1, source_target_pairs={{0,16},{8,24},{16,0},{24,8},{1,17},{9,25},{17,1},{25,9},{2,18},{10... | collective-permute-start | bytes 61448 | tf_op jit(solution)/shard_map/ppermute | solution.py:19
  3.9 6.2 %collective-permute-start.2 = (bf16[40,256]{1,0:T(8,128)(2,1)S(1)}, bf16[40,256]{1,0:T(8,128)(2,1)S(1)}, u32[]{:S(2)}, u32[]{:S(2)}) collective-permute-start(bf16[40,256]{1,0:T(8,128)(2,1)S(1)} %pad_maximum_fusion.3), channel_id=1, source_target_pairs={{0,24},{8,16},{16,8},{24,0},{1,25},{9,17},{17,9},{25,1},{2,26},{10... | collective-permute-start | bytes 61448 | tf_op jit(solution)/shard_map/ppermute | solution.py:19
  5.3 4.7 %collective-permute-start = (bf16[40,256]{1,0:T(8,128)(2,1)S(1)}, bf16[40,256]{1,0:T(8,128)(2,1)S(1)}, u32[]{:S(2)}, u32[]{:S(2)}) collective-permute-start(bf16[40,256]{1,0:T(8,128)(2,1)S(1)} %pad_maximum_fusion.1), channel_id=1, source_target_pairs={{0,8},{8,0},{16,24},{24,16},{1,9},{9,1},{17,25},{25,17},{2,10},{10... | collective-permute-start | bytes 61448 | tf_op jit(solution)/shard_map/ppermute | solution.py:19
  6.5 7.7 %collective-permute-start.8 = (bf16[40,1024]{1,0:T(8,128)(2,1)S(1)}, bf16[40,1024]{1,0:T(8,128)(2,1)S(1)}, u32[]{:S(2)}, u32[]{:S(2)}) collective-permute-start(bf16[40,1024]{1,0:T(8,128)(2,1)S(1)} %get-tuple-element.43), channel_id=1, source_target_pairs={{0,24},{8,16},{16,8},{24,0},{1,25},{9,17},{17,9},{25,1},{2,26},{10... | collective-permute-start | bytes 245768 | tf_op jit(solution)/shard_map/ppermute | solution.py:19
  9.4 5.4 %collective-permute-start.6 = (bf16[40,1024]{1,0:T(8,128)(2,1)S(1)}, bf16[40,1024]{1,0:T(8,128)(2,1)S(1)}, u32[]{:S(2)}, u32[]{:S(2)}) collective-permute-start(bf16[40,1024]{1,0:T(8,128)(2,1)S(1)} %get-tuple-element.44), channel_id=1, source_target_pairs={{0,8},{8,0},{16,24},{24,16},{1,9},{9,1},{17,25},{25,17},{2,10},{10... | collective-permute-start | bytes 245768 | tf_op jit(solution)/shard_map/ppermute | solution.py:19
  9.9 4.8 %collective-permute-start.7 = (bf16[40,1024]{1,0:T(8,128)(2,1)S(1)}, bf16[40,1024]{1,0:T(8,128)(2,1)S(1)}, u32[]{:S(2)}, u32[]{:S(2)}) collective-permute-start(bf16[40,1024]{1,0:T(8,128)(2,1)S(1)} %get-tuple-element.46), channel_id=1, source_target_pairs={{0,16},{8,24},{16,0},{24,8},{1,17},{9,25},{17,1},{25,9},{2,18},{10... | collective-permute-start | bytes 245768 | tf_op jit(solution)/shard_map/ppermute | solution.py:19
  10.1 9.4 %collective-permute-start.5 = (bf16[160,256]{1,0:T(8,128)(2,1)S(1)}, bf16[160,256]{1,0:T(8,128)(2,1)S(1)}, u32[]{:S(2)}, u32[]{:S(2)}) collective-permute-start(bf16[160,256]{1,0:T(8,128)(2,1)S(1)} %pad_maximum_fusion.after_ref.refs_2_), channel_id=1, source_target_pairs={{0,6},{1,7},{2,4},{3,5},{4,2},{5,3},{6,0},{7,1},{8,14},{9,15},{10,... | collective-permute-start | bytes 245768 | tf_op jit(solution)/shard_map/ppermute | solution.py:19
  14.1 5.6 %collective-permute-start.4 = (bf16[160,256]{1,0:T(8,128)(2,1)S(1)}, bf16[160,256]{1,0:T(8,128)(2,1)S(1)}, u32[]{:S(2)}, u32[]{:S(2)}) collective-permute-start(bf16[160,256]{1,0:T(8,128)(2,1)S(1)} %pad_maximum_fusion.after_ref.refs_2_), channel_id=1, source_target_pairs={{0,4},{1,5},{2,6},{3,7},{4,0},{5,1},{6,2},{7,3},{8,12},{9,13},{10,... | collective-permute-start | bytes 245768 | tf_op jit(solution)/shard_map/ppermute | solution.py:19
  14.1 5.6 %collective-permute-start.3 = (bf16[160,256]{1,0:T(8,128)(2,1)S(1)}, bf16[160,256]{1,0:T(8,128)(2,1)S(1)}, u32[]{:S(2)}, u32[]{:S(2)}) collective-permute-start(bf16[160,256]{1,0:T(8,128)(2,1)S(1)} %pad_maximum_fusion.after_ref.refs_2_), channel_id=1, source_target_pairs={{0,2},{1,3},{2,0},{3,1},{4,6},{5,7},{6,4},{7,5},{8,10},{9,11},{10,... | collective-permute-start | bytes 245768 | tf_op jit(solution)/shard_map/ppermute | solution.py:19
  14.8 7.3 %collective-permute-start.9 = (bf16[160,256]{1,0:T(8,128)(2,1)S(1)}, bf16[160,256]{1,0:T(8,128)(2,1)S(1)}, u32[]{:S(2)}, u32[]{:S(2)}) collective-permute-start(bf16[160,256]{1,0:T(8,128)(2,1)S(1)} %pad_maximum_fusion.after_ref.refs_2_), channel_id=1, source_target_pairs={{0,1},{1,0},{2,3},{3,2},{4,5},{5,4},{6,7},{7,6},{8,9},{9,8},{10,11... | collective-permute-start | bytes 245768 | tf_op jit(solution)/shard_map/ppermute | solution.py:19
  14.8 0.7 %copy-start = (s32[32]{0:T(128)S(1)}, s32[32]{0:T(128)}, u32[]{:S(2)}) copy-start(s32[32]{0:T(128)} %order_ref.1) | copy-start | bytes 388
  19.8 2.4 %collective-permute-start.10 = (bf16[160,256]{1,0:T(8,128)(2,1)S(1)}, bf16[160,256]{1,0:T(8,128)(2,1)S(1)}, u32[]{:S(2)}, u32[]{:S(2)}) collective-permute-start(bf16[160,256]{1,0:T(8,128)(2,1)S(1)} %collective-permute-done.3.refs_3_), channel_id=1, source_target_pairs={{0,1},{1,0},{2,3},{3,2},{4,5},{5,4},{6,7},{7,6},{8,9},{9,8},{10,11... | collective-permute-start | bytes 245768 | tf_op jit(solution)/shard_map/ppermute | solution.py:19
  20.1 2.1 %collective-permute-start.11 = (bf16[160,256]{1,0:T(8,128)(2,1)S(1)}, bf16[160,256]{1,0:T(8,128)(2,1)S(1)}, u32[]{:S(2)}, u32[]{:S(2)}) collective-permute-start(bf16[160,256]{1,0:T(8,128)(2,1)S(1)} %collective-permute-done.4.refs_4_), channel_id=1, source_target_pairs={{0,1},{1,0},{2,3},{3,2},{4,5},{5,4},{6,7},{7,6},{8,9},{9,8},{10,11... | collective-permute-start | bytes 245768 | tf_op jit(solution)/shard_map/ppermute | solution.py:19
  20.3 1.9 %collective-permute-start.12 = (bf16[160,256]{1,0:T(8,128)(2,1)S(1)}, bf16[160,256]{1,0:T(8,128)(2,1)S(1)}, u32[]{:S(2)}, u32[]{:S(2)}) collective-permute-start(bf16[160,256]{1,0:T(8,128)(2,1)S(1)} %collective-permute-done.5.refs_5_), channel_id=1, source_target_pairs={{0,1},{1,0},{2,3},{3,2},{4,5},{5,4},{6,7},{7,6},{8,9},{9,8},{10,11... | collective-permute-start | bytes 245768 | tf_op jit(solution)/shard_map/ppermute | solution.py:19
  25.4 6.4 %collective-permute-start.14 = (bf16[80,1024]{1,0:T(8,128)(2,1)S(1)}, bf16[80,1024]{1,0:T(8,128)(2,1)S(1)}, u32[]{:S(2)}, u32[]{:S(2)}) collective-permute-start(bf16[80,1024]{1,0:T(8,128)(2,1)S(1)} %get-tuple-element.38), channel_id=1, source_target_pairs={{0,8},{8,0},{16,24},{24,16},{1,9},{9,1},{17,25},{25,17},{2,10},{10... | collective-permute-start | bytes 491528 | tf_op jit(solution)/shard_map/ppermute | solution.py:19
  27.1 7.2 %collective-permute-start.17 = (bf16[80,1024]{1,0:T(8,128)(2,1)S(1)}, bf16[80,1024]{1,0:T(8,128)(2,1)S(1)}, u32[]{:S(2)}, u32[]{:S(2)}) collective-permute-start(bf16[80,1024]{1,0:T(8,128)(2,1)S(1)} %get-tuple-element.42), channel_id=1, source_target_pairs={{0,16},{8,24},{16,0},{24,8},{1,17},{9,25},{17,1},{25,9},{2,18},{10... | collective-permute-start | bytes 491528 | tf_op jit(solution)/shard_map/ppermute | solution.py:19
  29.5 6.9 %collective-permute-start.13 = (bf16[80,1024]{1,0:T(8,128)(2,1)S(1)}, bf16[80,1024]{1,0:T(8,128)(2,1)S(1)}, u32[]{:S(2)}, u32[]{:S(2)}) collective-permute-start(bf16[80,1024]{1,0:T(8,128)(2,1)S(1)} %get-tuple-element.36), channel_id=1, source_target_pairs={{0,8},{8,0},{16,24},{24,16},{1,9},{9,1},{17,25},{25,17},{2,10},{10... | collective-permute-start | bytes 491528 | tf_op jit(solution)/shard_map/ppermute | solution.py:19
  30.1 7.4 %collective-permute-start.16 = (bf16[80,1024]{1,0:T(8,128)(2,1)S(1)}, bf16[80,1024]{1,0:T(8,128)(2,1)S(1)}, u32[]{:S(2)}, u32[]{:S(2)}) collective-permute-start(bf16[80,1024]{1,0:T(8,128)(2,1)S(1)} %get-tuple-element.40), channel_id=1, source_target_pairs={{0,16},{8,24},{16,0},{24,8},{1,17},{9,25},{17,1},{25,9},{2,18},{10... | collective-permute-start | bytes 491528 | tf_op jit(solution)/shard_map/ppermute | solution.py:19
  31.8 8.2 %collective-permute-start.15 = (bf16[80,1024]{1,0:T(8,128)(2,1)S(1)}, bf16[80,1024]{1,0:T(8,128)(2,1)S(1)}, u32[]{:S(2)}, u32[]{:S(2)}) collective-permute-start(bf16[80,1024]{1,0:T(8,128)(2,1)S(1)} %shard_map.60), channel_id=1, source_target_pairs={{0,16},{8,24},{16,0},{24,8},{1,17},{9,25},{17,1},{25,9},{2,18},{10... | collective-permute-start | bytes 491528 | tf_op jit(solution)/shard_map/ppermute | solution.py:19
  34.3 5.7 %collective-permute-start.18 = (bf16[80,1024]{1,0:T(8,128)(2,1)S(1)}, bf16[80,1024]{1,0:T(8,128)(2,1)S(1)}, u32[]{:S(2)}, u32[]{:S(2)}) collective-permute-start(bf16[80,1024]{1,0:T(8,128)(2,1)S(1)} %shard_map.61), channel_id=1, source_target_pairs={{0,8},{8,0},{16,24},{24,16},{1,9},{9,1},{17,25},{25,17},{2,10},{10... | collective-permute-start | bytes 491528 | tf_op jit(solution)/shard_map/ppermute | solution.py:19

commit v3 on v2

--- a/solution.py
+++ b/solution.py
@@ -25,14 +25,8 @@
     return jnp.sum(jnp.where(hits, order[None, :], 0), axis=1) * span + flat_rows % span
 
 
-def stack_heads(q_ref, heads):
-    q = q_ref[...].astype(jnp.float32)
-    q = jnp.concatenate([q[:, h * D_HEAD : (h + 1) * D_HEAD] for h in range(heads)], axis=0)
-    return q.astype(jnp.bfloat16)
-
-
 def prepare_kernel(span, n_head, chunk_flips, order_ref, weight_ref, after_ref, *refs):
-    q_refs, (weight_out, bias_ref, q_out, sems) = refs[:n_head], refs[n_head:]
+    q_refs, (weight_out, qpos_ref, kpos_ref, q_out, q_s, sems) = refs[:n_head], refs[n_head:]
     me, ctx = lax.axis_index("head"), lax.axis_index("ctx")
     step = weight_ref.shape[0] // FETCHES
     fetches = [
@@ -47,19 +41,24 @@
         for fetch in fetches:
             fetch.start()
 
-    n_keys = bias_ref.shape[1]
-    lane = lax.broadcasted_iota(jnp.int32, (1, n_keys), 1)
-    kpos = lane
+    row = lax.broadcasted_iota(jnp.int32, (span, D_HEAD), 0)
     for i, flip in enumerate(chunk_flips):
         for k in range(n_head):
             first = (i * n_head + k) * span
             block = order_ref[(ctx ^ flip) * n_head + (me ^ k)]
-            kpos = jnp.where(lane >= first, lane + (block * span - first), kpos)
-    row = lax.broadcasted_iota(jnp.int32, (span, 1), 0)
+            kpos_ref[first : first + span, :] = row + block * span
+    heads = q_refs[0].shape[1] // D_HEAD
+    lane = lax.broadcasted_iota(jnp.int32, qpos_ref.shape, 1)
+    qpos = lane
+    for i in range(heads * n_head):
+        block = order_ref[ctx * n_head + i % n_head]
+        qpos = jnp.where(lane >= i * span, lane + (block - i) * span, qpos)
+    qpos_ref[...] = qpos
     for k in range(n_head):
-        qpos = row + order_ref[ctx * n_head + (me ^ k)] * span
-        bias_ref[k * span : (k + 1) * span, :] = jnp.where(kpos <= qpos, 0.0, NEG_FILL)
-        q_out[k] = stack_heads(q_refs[k], q_refs[k].shape[1] // D_HEAD)
+        at = pl.multiple_of((me ^ k) * span, span)
+        q_s[pl.ds(at, span), :] = q_refs[k][...].astype(jnp.float32)
+    stacked = jnp.concatenate([q_s[:, h * D_HEAD : (h + 1) * D_HEAD] for h in range(heads)], axis=0)
+    q_out[...] = stacked.T.astype(jnp.bfloat16)
     for fetch in fetches:
         fetch.wait()
 
@@ -67,13 +66,15 @@
 def prepare(order, weight, after, q_pieces, chunk_flips, n_keys):
     n_head = len(q_pieces)
     span, width = q_pieces[0].shape
+    columns = span * n_head * width // D_HEAD
     vmem = pl.BlockSpec(memory_space=pltpu.VMEM)
     return pl.pallas_call(
         functools.partial(prepare_kernel, span, n_head, chunk_flips),
         out_shape=(
             jax.ShapeDtypeStruct(weight.shape, weight.dtype),
-            jax.ShapeDtypeStruct((span * n_head, n_keys), jnp.float32),
-            jax.ShapeDtypeStruct((n_head, span * width // D_HEAD, D_HEAD), jnp.bfloat16),
+            jax.ShapeDtypeStruct((1, columns), jnp.int32),
+            jax.ShapeDtypeStruct((n_keys, D_HEAD), jnp.int32),
+            jax.ShapeDtypeStruct((D_HEAD, columns), jnp.bfloat16),
         ),
         in_specs=[
             pl.BlockSpec(memory_space=pltpu.SMEM),
@@ -81,8 +82,11 @@
             pl.BlockSpec(memory_space=pl.ANY),
         ]
         + [vmem] * n_head,
-        out_specs=(vmem,) * 3,
-        scratch_shapes=[pltpu.SemaphoreType.DMA((FETCHES,))],
+        out_specs=(vmem,) * 4,
+        scratch_shapes=[
+            pltpu.VMEM((span * n_head, width), jnp.float32),
+            pltpu.SemaphoreType.DMA((FETCHES,)),
+        ],
         compiler_params=pltpu.CompilerParams(vmem_limit_bytes=ROOMY * 1024 * 1024),
         cost_estimate=pl.CostEstimate(flops=0, bytes_accessed=4 * 1024 * 1024, transcendentals=0),
     )(order, weight, after, *q_pieces)
@@ -94,146 +98,89 @@
     return part.astype(jnp.bfloat16)
 
 
-def gather_keys(kv_refs, k_s, v_s):
-    rows = kv_refs[0].shape[0]
-    for i, ref in enumerate(kv_refs):
-        k_s[i * rows : (i + 1) * rows, :] = ref[:, :D_HEAD]
-        v_s[i * rows : (i + 1) * rows, :] = ref[:, D_HEAD:]
-
-
-def masked_scores(q, k_s, bias):
-    scores = lax.dot_general(
-        q, k_s[...], (((1,), (1,)), ((), ())), preferred_element_type=jnp.float32
-    )
-    span, n_keys = bias.shape
-    return scores.reshape(-1, span, n_keys) + bias[None]
-
-
-def mix_values(weights, v_s):
-    heads, span, n_keys = weights.shape
-    mixed = jnp.dot(
-        weights.reshape(heads * span, n_keys), v_s[...], preferred_element_type=jnp.float32
-    )
-    return mixed.reshape(heads, span, D_HEAD)
-
-
-def staged(n_piece, score, weigh, finish):
-    scores, held = score(0), None
-    for piece in range(n_piece):
-        ahead = score(piece + 1) if piece + 1 < n_piece else None
-        weights = weigh(piece, scores)
-        if held is not None:
-            finish(piece - 1, *held)
-        scores, held = ahead, weights
-    finish(n_piece - 1, *held)
-
-
-def early_kernel(span, n_piece, n_chunk, *refs):
-    bias_ref, q_ref = refs[:2]
-    kv_refs = refs[2 : 2 + n_chunk]
-    peak_ref, denom_ref, mixed_ref, k_s, v_s = refs[2 + n_chunk :]
-    gather_keys(kv_refs, k_s, v_s)
-    n_keys = k_s.shape[0]
-
-    def score(piece):
-        return masked_scores(q_ref[piece], k_s, bias_ref[piece * span : (piece + 1) * span, :n_keys])
-
-    def weigh(piece, scores):
-        peak = jnp.max(scores, axis=2, keepdims=True)
-        weights = jnp.exp2((scores - peak) * EXP2_SCALE)
-        peak_ref[piece] = peak
-        denom_ref[piece] = jnp.sum(weights, axis=2, keepdims=True)
-        return (weights.astype(jnp.bfloat16),)
-
-    def finish(piece, weights):
-        mixed_ref[piece] = mix_values(weights, v_s)
-
-    staged(n_piece, score, weigh, finish)
-
-
-def early_attend(bias, q_all, kv_chunks):
-    n_chunk, (n_piece, stacked, depth) = len(kv_chunks), q_all.shape
-    span = bias.shape[0] // n_piece
-    heads = stacked // span
+def masked_scores(kv_refs, kpos, qpos_ref, q_ref):
+    keys = jnp.concatenate([ref[:, :D_HEAD] for ref in kv_refs], axis=0)
+    scores = jnp.dot(keys, q_ref[...], preferred_element_type=jnp.float32)
+    kpos = jnp.concatenate([kpos] * (scores.shape[1] // D_HEAD), axis=1)
+    return jnp.where(kpos <= qpos_ref[...], scores, NEG_FILL)
+
+
+def mix_values(kv_refs, weights):
+    values = jnp.concatenate([ref[:, D_HEAD:] for ref in kv_refs], axis=0)
+    return jnp.dot(values.T, weights.astype(jnp.bfloat16), preferred_element_type=jnp.float32)
+
+
+def early_kernel(n_chunk, kpos_ref, qpos_ref, q_ref, *refs):
+    kv_refs, (peak_ref, denom_ref, mixed_ref) = refs[:n_chunk], refs[n_chunk:]
+    n_keys = kv_refs[0].shape[0] * n_chunk
+    scores = masked_scores(kv_refs, kpos_ref[:n_keys, :], qpos_ref, q_ref)
+    peak = jnp.max(scores, axis=0, keepdims=True)
+    weights = jnp.exp2((scores - peak) * EXP2_SCALE)
+    peak_ref[...] = peak
+    denom_ref[...] = jnp.sum(weights, axis=0, keepdims=True)
+    mixed_ref[...] = mix_values(kv_refs, weights)
+
+
+def early_attend(kpos, qpos, q_all, kv_chunks):
+    n_chunk, (depth, columns) = len(kv_chunks), q_all.shape
     n_keys = kv_chunks[0].shape[0] * n_chunk
     vmem = pl.BlockSpec(memory_space=pltpu.VMEM)
-    column = jax.ShapeDtypeStruct((n_piece, heads, span, 1), jnp.float32)
-    return pl.pallas_call(
-        functools.partial(early_kernel, span, n_piece, n_chunk),
-        out_shape=(column, column, jax.ShapeDtypeStruct((n_piece, heads, span, depth), jnp.float32)),
-        in_specs=[vmem] * (2 + n_chunk),
+    line = jax.ShapeDtypeStruct((1, columns), jnp.float32)
+    return pl.pallas_call(
+        functools.partial(early_kernel, n_chunk),
+        out_shape=(line, line, jax.ShapeDtypeStruct((depth, columns), jnp.float32)),
+        in_specs=[vmem] * (3 + n_chunk),
         out_specs=(vmem,) * 3,
-        scratch_shapes=[pltpu.VMEM((n_keys, D_HEAD), jnp.bfloat16)] * 2,
         compiler_params=pltpu.CompilerParams(vmem_limit_bytes=20 * 1024 * 1024),
         cost_estimate=pl.CostEstimate(
-            flops=4 * n_piece * stacked * depth * n_keys,
+            flops=4 * columns * depth * n_keys,
             bytes_accessed=4 * 1024 * 1024,
-            transcendentals=n_piece * stacked * n_keys,
-        ),
-    )(bias, q_all, *kv_chunks)
-
-
-def attend_kernel(span, n_piece, n_chunk, *refs):
-    bias_ref, q_ref = refs[:2]
-    kv_refs = refs[2 : 2 + n_chunk]
-    rest = refs[2 + n_chunk :]
-    peak_ref, denom_ref, mixed_ref, weight_ref, attn_ref, low_ref, high_ref = rest[:7]
-    k_s, v_s, a_s = rest[7:]
-    me = lax.axis_index("head")
-    gather_keys(kv_refs, k_s, v_s)
-    n_keys = k_s.shape[0]
-
-    def score(piece):
-        return masked_scores(q_ref[piece], k_s, bias_ref[piece * span : (piece + 1) * span, n_keys:])
-
-    def weigh(piece, scores):
-        peak = jnp.maximum(peak_ref[piece], jnp.max(scores, axis=2, keepdims=True))
-        weights = jnp.exp2((scores - peak) * EXP2_SCALE)
-        factor = jnp.exp2((peak_ref[piece] - peak) * EXP2_SCALE)
-        denom = factor * denom_ref[piece] + jnp.sum(weights, axis=2, keepdims=True)
-        return weights.astype(jnp.bfloat16), factor, denom
-
-    def finish(piece, weights, factor, denom):
-        mixed = (factor * mixed_ref[piece] + mix_values(weights, v_s)) / denom
-        at = pl.multiple_of((me ^ piece) * span, span)
-        for h in range(mixed.shape[0]):
-            a_s[pl.ds(at, span), h * D_HEAD : (h + 1) * D_HEAD] = mixed[h]
-
-    staged(n_piece, score, weigh, finish)
-    attn = a_s[...].astype(jnp.bfloat16)
+            transcendentals=columns * n_keys,
+        ),
+    )(kpos, qpos, q_all, *kv_chunks)
+
+
+def attend_kernel(n_chunk, kpos_ref, qpos_ref, q_ref, *refs):
+    kv_refs = refs[:n_chunk]
+    peak_ref, denom_ref, mixed_ref, weight_ref, attn_ref, low_ref, high_ref = refs[n_chunk:]
+    seg, width = attn_ref.shape
+    n_keys = kv_refs[0].shape[0] * n_chunk
+    scores = masked_scores(kv_refs, kpos_ref[n_keys:, :], qpos_ref, q_ref)
+    peak = jnp.maximum(peak_ref[...], jnp.max(scores, axis=0, keepdims=True))
+    weights = jnp.exp2((scores - peak) * EXP2_SCALE)
+    factor = jnp.exp2((peak_ref[...] - peak) * EXP2_SCALE)
+    inverse = 1.0 / (factor * denom_ref[...] + jnp.sum(weights, axis=0, keepdims=True))
+    mixed = mixed_ref[...] * (factor * inverse) + mix_values(kv_refs, weights) * inverse
+    mixed = mixed.T.astype(jnp.bfloat16)
+    heads = width // D_HEAD
+    attn = jnp.concatenate([mixed[h * seg : (h + 1) * seg] for h in range(heads)], axis=1)
     attn_ref[...] = attn
-    part = project(attn, weight_ref, me, 3, low_ref.shape[1])
+    part = project(attn, weight_ref, lax.axis_index("head"), 3, low_ref.shape[1])
     half = low_ref.shape[0]
     low_ref[...] = part[:half]
     high_ref[...] = part[half:]
 
 
-def attend(bias, kv_chunks, state, weight):
-    n_chunk = len(kv_chunks)
-    n_piece, heads, span, depth = state[-1].shape
-    width = heads * depth
-    seg = span * n_piece
+def attend(kpos, qpos, q_all, kv_chunks, state, weight, n_head):
+    n_chunk, (depth, columns) = len(kv_chunks), q_all.shape
+    width, out_width = weight.shape
+    seg = columns * depth // width
     n_keys = kv_chunks[0].shape[0] * n_chunk
-    cols = weight.shape[1] // n_piece
+    cols = out_width // n_head
     vmem = pl.BlockSpec(memory_space=pltpu.VMEM)
     half = jax.ShapeDtypeStruct((seg // 2, cols), jnp.bfloat16)
     return pl.pallas_call(
-        functools.partial(attend_kernel, span, n_piece, n_chunk),
+        functools.partial(attend_kernel, n_chunk),
         out_shape=(jax.ShapeDtypeStruct((seg, width), jnp.bfloat16), half, half),
-        in_specs=[vmem] * (6 + n_chunk),
+        in_specs=[vmem] * (7 + n_chunk),
         out_specs=(vmem, vmem, vmem),
-        scratch_shapes=[
-            pltpu.VMEM((n_keys, D_HEAD), jnp.bfloat16),
-            pltpu.VMEM((n_keys, D_HEAD), jnp.bfloat16),
-            pltpu.VMEM((seg, width), jnp.float32),
-        ],
         compiler_params=pltpu.CompilerParams(vmem_limit_bytes=28 * 1024 * 1024),
         cost_estimate=pl.CostEstimate(
-            flops=4 * seg * width * n_keys + 2 * seg * width * cols,
+            flops=4 * columns * depth * n_keys + 2 * seg * width * cols,
             bytes_accessed=4 * 1024 * 1024,
-            transcendentals=seg * heads * n_keys,
-        ),
-    )(bias, state[0], *kv_chunks, *state[1:], weight)
+            transcendentals=columns * n_keys,
+        ),
+    )(kpos, qpos, q_all, *kv_chunks, *state, weight)
 
 
 def project_kernel(flips, attn_ref, weight_ref, *out_refs):
@@ -317,13 +264,15 @@
     q_in = [q_cut[0]] + [swap(q_cut[k], "head", k, n_head) for k in range(1, n_head)]
     flips = [2 * dz for dz in range(n_ctx // 2)]
     chunk_flips = tuple(flips + [f ^ 1 for f in flips])
-    weight, bias, q_all = prepare(stretch_order, out_weight, own, q_in, chunk_flips, own.shape[0] * n_ctx)
+    weight, qpos, kpos, q_all = prepare(
+        stretch_order, out_weight, own, q_in, chunk_flips, own.shape[0] * n_ctx
+    )
     far_keys = [swap(own, "ctx", f, n_ctx) for f in flips[1:]]
-    far_keys, bias = lax.optimization_barrier((far_keys, bias))
+    far_keys, kpos = lax.optimization_barrier((far_keys, kpos))
     same_core = [own] + far_keys
     other_core = [swap(x, "ctx", 1, n_ctx) for x in same_core]
-    state = early_attend(bias, q_all, same_core)
-    attn, far_low, far_high = attend(bias, other_core, (q_all, *state), weight)
+    state = early_attend(kpos, qpos, q_all, same_core)
+    attn, far_low, far_high = attend(kpos, qpos, q_all, other_core, state, weight, n_head)
     x_far = swap(far_low, "head", 1, n_head)
     y_far = swap(far_high, "head", 2, n_head)
     x_low, x_high, y_low, y_high = project_rest(attn, weight, (1, 2), n_head)

time: 41.1 us -> 40.2 us (0.978)
  Pallas kernels: 11.1 us -> 10.3 us
    pallas_call x2, Pallas kernels: 4.73 us -> 3.8 us  [the longest x1 2.31 us: attend(): pl.pallas_call(functools.partial(attend_kernel, n_chunk), out_shape=(jax....]
  transfers between devices with their start and end apart: 19 -> 19, of which waited for: 4 -> 4; matrix products, arithmetic and copies ran while one was open for 3% -> 3% of each run, Pallas kernels for 17% -> 18%
where the time goes in v3:
time: 40.2 us; the launch traced here: 40 us
  starting transfers between devices  22.1 us (55%)
  Pallas kernels  10.3 us (26%)
  waiting for transfers between devices  5 us (12%)
  local copies, waits for them, and re-layouts  2.51 us (6%)
    ppermute x19, starting transfers between devices, swap(): return lax.ppermute(x, axis, [(i, i ^ flip) for i in range(size)])  22.1 us
    ppermute x19, waiting for transfers between devices, swap(): return lax.ppermute(x, axis, [(i, i ^ flip) for i in range(size)])  5 us
    pallas_call x1, Pallas kernels, prepare(): pl.pallas_call(functools.partial(prepare_kernel, span, n_head, chunk_flip...  4.11 us
    pallas_call x1, Pallas kernels, attend(): pl.pallas_call(functools.partial(attend_kernel, n_chunk), out_shape=(jax....  2.31 us
    dynamic_slice x2, local copies, waits for them, and re-layouts, cut(): return lax.dynamic_slice_in_dim(x[0], (me ^ k) * width, width, 1)  1.86 us
    pallas_call x1, Pallas kernels, early_attend(): pl.pallas_call(functools.partial(early_kernel, n_chunk), out_shape=(line,...  1.5 us
    pallas_call x2, Pallas kernels, project_rest(): pl.pallas_call(functools.partial(project_kernel, flips), out_shape=(half,...  1.42 us
    pallas_call x1, Pallas kernels, final_sum(): pl.pallas_call(final_kernel, out_shape=jax.ShapeDtypeStruct((2 * rows, co...  0.84 us
  transfers between devices with their start and end apart: 19, of which 4 were waited for; matrix products, arithmetic and copies ran while one was open for 3% of the time, Pallas kernels for 18%

profile of v3, /device:TPU:0, one launch (start us, length us, event | category | flops | bytes accessed | tf_op | source)
XLA Modules:
  0.0 40.0 jit_solution(17865899055781262307)
XLA Ops:
  0.0 0.8 %dynamic-slice_bitcast_fusion.10 = (bf16[40,128]{1,0:T(8,128)(2,1)S(1)}, bf16[40,128]{1,0:T(8,128)(2,1)S(1)}, bf16[40,128]{1,0:T(8,128)(2,1)S(1)}, bf16[40,128]{...) fusion(bf16[1,40,512]{2,1,0:T(8,128)(2,1)} %param.7, ...), kind=kLoop, calls=%fused_computation.14 | loop fusion | bytes 163856 | tf_op jit(solution)/shard_map/dynamic_slice | solution.py:256
  0.8 3.0 %collective-permute-start.1 = (bf16[40,256]{1,0:T(8,128)(2,1)S(1)}, bf16[40,256]{1,0:T(8,128)(2,1)S(1)}, u32[]{:S(2)}, u32[]{:S(2)}) collective-permute-start(bf16[40,256]{1,0:T(8,128)(2,1)S(1)} %pad_maximum_fusion.2), channel_id=1, source_target_pairs={{0,16},{8,24},{16,0},{24,8},{1,17},{9,25},{17,1},{25,9},{2,18},{10... | collective-permute-start | bytes 61448 | tf_op jit(solution)/shard_map/ppermute | solution.py:19
  3.9 1.4 %collective-permute-start.2 = (bf16[40,256]{1,0:T(8,128)(2,1)S(1)}, bf16[40,256]{1,0:T(8,128)(2,1)S(1)}, u32[]{:S(2)}, u32[]{:S(2)}) collective-permute-start(bf16[40,256]{1,0:T(8,128)(2,1)S(1)} %pad_maximum_fusion.3), channel_id=1, source_target_pairs={{0,24},{8,16},{16,8},{24,0},{1,25},{9,17},{17,9},{25,1},{2,26},{10... | collective-permute-start | bytes 61448 | tf_op jit(solution)/shard_map/ppermute | solution.py:19
  5.3 0.1 collective-permute-start
  5.5 1.0 %dynamic-slice_bitcast_fusion = (bf16[40,1024]{1,0:T(8,128)(2,1)S(1)}, bf16[40,1024]{1,0:T(8,128)(2,1)S(1)}, bf16[40,1024]{1,0:T(8,128)(2,1)S(1)}, bf16[40,1024]{1,0:T(8,128)(2,1)S(1)}) fusion(bf16[1,40,4096]{2,1,0:T(8,128)(2,1)} %param.5, s32[]{:T(128)S(6)} %select_n.35, s32[]{:T(128)S(6)} %select_n.33, s32[]{:T(128)S(6)} %select_n.32, s32[]{:T(128)S(6)} %select_n.34), kind=kLoop, calls=%fused_computation.1 | loop fusion | bytes 655376 | tf_op jit(solution)/shard_map/dynamic_slice | solution.py:256
  6.5 2.9 %collective-permute-start.8 = (bf16[40,1024]{1,0:T(8,128)(2,1)S(1)}, bf16[40,1024]{1,0:T(8,128)(2,1)S(1)}, u32[]{:S(2)}, u32[]{:S(2)}) collective-permute-start(bf16[40,1024]{1,0:T(8,128)(2,1)S(1)} %get-tuple-element.45), channel_id=1, source_target_pairs={{0,24},{8,16},{16,8},{24,0},{1,25},{9,17},{17,9},{25,1},{2,26},{10... | collective-permute-start | bytes 245768 | tf_op jit(solution)/shard_map/ppermute | solution.py:19
  9.4 0.5 %collective-permute-start.6 = (bf16[40,1024]{1,0:T(8,128)(2,1)S(1)}, bf16[40,1024]{1,0:T(8,128)(2,1)S(1)}, u32[]{:S(2)}, u32[]{:S(2)}) collective-permute-start(bf16[40,1024]{1,0:T(8,128)(2,1)S(1)} %get-tuple-element.46), channel_id=1, source_target_pairs={{0,8},{8,0},{16,24},{24,16},{1,9},{9,1},{17,25},{25,17},{2,10},{10... | collective-permute-start | bytes 245768 | tf_op jit(solution)/shard_map/ppermute | solution.py:19
  9.9 0.1 collective-permute-start.7
  10.0 0.0 collective-permute-done.2
  10.1 4.1 %collective-permute-start.5 = (bf16[160,256]{1,0:T(8,128)(2,1)S(1)}, bf16[160,256]{1,0:T(8,128)(2,1)S(1)}, u32[]{:S(2)}, u32[]{:S(2)}) collective-permute-start(bf16[160,256]{1,0:T(8,128)(2,1)S(1)} %pad_maximum_fusion.after_ref.refs_0_), channel_id=1, source_target_pairs={{0,6},{1,7},{2,4},{3,5},{4,2},{5,3},{6,0},{7,1},{8,14},{9,15},{10,... | collective-permute-start | bytes 245768 | tf_op jit(solution)/shard_map/ppermute | solution.py:19
  14.1 0.6 %collective-permute-start.3 = (bf16[160,256]{1,0:T(8,128)(2,1)S(1)}, bf16[160,256]{1,0:T(8,128)(2,1)S(1)}, u32[]{:S(2)}, u32[]{:S(2)}) collective-permute-start(bf16[160,256]{1,0:T(8,128)(2,1)S(1)} %pad_maximum_fusion.after_ref.refs_0_), channel_id=1, source_target_pairs={{0,2},{1,3},{2,0},{3,1},{4,6},{5,7},{6,4},{7,5},{8,10},{9,11},{10,... | collective-permute-start | bytes 245768 | tf_op jit(solution)/shard_map/ppermute | solution.py:19
  14.8 0.0 copy-start
  14.8 0.6 %copy-done = s32[32]{0:T(128)S(1)} copy-done((s32[32]{0:T(128)S(1)}, s32[32]{0:T(128)}, u32[]{:S(2)}) %copy-start) | copy-done | bytes 152
  15.5 4.1 %shard_map.55 = (bf16[1024,4096]{1,0:T(8,128)(2,1)S(1)}, s32[1,1280]{1,0:T(1,128)S(1)}, s32[1280,128]{1,0:T(8,128)S(1)}, bf16[128,1280]{1,0:T(8,128)(2,1)S(1)}) custom-call(s32[32]{0:T(128)S(1)} %copy-done, bf16[1024,4096]{1,0:T(8,128)(2,1)} %weight_ref.1, bf16[160,256]{1,0:T(8,128)(2,1)S(1)} %pad_maximum_fusion.after_ref.refs_0_, ...), custom_call_target="tpu_custom_call" | custom-call | bytes 4194304 | tf_op jit(solution)/shard_map/pallas_call | solution.py:71
  19.6 0.2 collective-permute-done.4.refs_2_
  19.8 0.4 %collective-permute-start.10 = (bf16[160,256]{1,0:T(8,128)(2,1)S(1)}, bf16[160,256]{1,0:T(8,128)(2,1)S(1)}, u32[]{:S(2)}, u32[]{:S(2)}) collective-permute-start(bf16[160,256]{1,0:T(8,128)(2,1)S(1)} %collective-permute-done.3.refs_1_), channel_id=1, source_target_pairs={{0,1},{1,0},{2,3},{3,2},{4,5},{5,4},{6,7},{7,6},{8,9},{9,8},{10,11... | collective-permute-start | bytes 245768 | tf_op jit(solution)/shard_map/ppermute | solution.py:19
  20.2 0.1 collective-permute-start.11
  20.3 0.4 %collective-permute-start.12 = (bf16[160,256]{1,0:T(8,128)(2,1)S(1)}, bf16[160,256]{1,0:T(8,128)(2,1)S(1)}, u32[]{:S(2)}, u32[]{:S(2)}) collective-permute-start(bf16[160,256]{1,0:T(8,128)(2,1)S(1)} %collective-permute-done.5.refs_3_), channel_id=1, source_target_pairs={{0,1},{1,0},{2,3},{3,2},{4,5},{5,4},{6,7},{7,6},{8,9},{9,8},{10,11... | collective-permute-start | bytes 245768 | tf_op jit(solution)/shard_map/ppermute | solution.py:19
  20.7 1.5 %shard_map.56 = (f32[1,1280]{1,0:T(1,128)S(1)}, f32[1,1280]{1,0:T(1,128)S(1)}, f32[128,1280]{1,0:T(8,128)S(1)}) custom-call(s32[1280,128]{1,0:T(8,128)S(1)} %get-tuple-element.26.kpos_ref, s32[1,1280]{1,0:T(1,128)S(1)} %get-tuple-element.27.qpos_ref, bf16[128,1280]{1,0:T(8,128)(2,1)S(1)} %get-tuple-element.28.q_ref, ...), custom_call_target="tpu_custom_call" | custom-call | flops 419430400 | bytes 4194304 | tf_op jit(solution)/shard_map/pallas_call | solution.py:129
  22.2 2.3 %shard_map.57 = (bf16[160,1024]{1,0:T(8,128)(2,1)S(1)}, bf16[80,1024]{1,0:T(8,128)(2,1)S(1)}, bf16[80,1024]{1,0:T(8,128)(2,1)S(1)}) custom-call(s32[1280,128]{1,0:T(8,128)S(1)} %get-tuple-element.26.kpos_ref, s32[1,1280]{1,0:T(1,128)S(1)} %get-tuple-element.27.qpos_ref, bf16[128,1280]{1,0:T(8,128)(2,1)S(1)} %get-tuple-element.28.q_ref, ...), custom_call_target="tpu_custom_call" | custom-call | flops 754974720 | bytes 4194304 | tf_op jit(solution)/shard_map/pallas_call | solution.py:172
  24.5 1.7 %collective-permute-start.14 = (bf16[80,1024]{1,0:T(8,128)(2,1)S(1)}, bf16[80,1024]{1,0:T(8,128)(2,1)S(1)}, u32[]{:S(2)}, u32[]{:S(2)}) collective-permute-start(bf16[80,1024]{1,0:T(8,128)(2,1)S(1)} %get-tuple-element.40), channel_id=1, source_target_pairs={{0,8},{8,0},{16,24},{24,16},{1,9},{9,1},{17,25},{25,17},{2,10},{10... | collective-permute-start | bytes 491528 | tf_op jit(solution)/shard_map/ppermute | solution.py:19
  26.2 1.5 %collective-permute-start.17 = (bf16[80,1024]{1,0:T(8,128)(2,1)S(1)}, bf16[80,1024]{1,0:T(8,128)(2,1)S(1)}, u32[]{:S(2)}, u32[]{:S(2)}) collective-permute-start(bf16[80,1024]{1,0:T(8,128)(2,1)S(1)} %get-tuple-element.44), channel_id=1, source_target_pairs={{0,16},{8,24},{16,0},{24,8},{1,17},{9,25},{17,1},{25,9},{2,18},{10... | collective-permute-start | bytes 491528 | tf_op jit(solution)/shard_map/ppermute | solution.py:19
  27.8 0.9 %shard_map.59 = (bf16[80,1024]{1,0:T(8,128)(2,1)S(1)}, bf16[80,1024]{1,0:T(8,128)(2,1)S(1)}, bf16[80,1024]{1,0:T(8,128)(2,1)S(1)}, bf16[80,1024]{1,0:T(8,128)(2,1)S(1)}) custom-call(bf16[160,1024]{1,0:T(8,128)(2,1)S(1)} %get-tuple-element.36.attn_ref, bf16[1024,4096]{1,0:T(8,128)(2,1)S(1)} %get-tuple-element.35.refs_7_.weight_ref), custom_call_target="tpu_custom_call" | custom-call | flops 671088640 | bytes 4194304 | tf_op jit(solution)/shard_map/pallas_call | solution.py:200
  28.7 0.6 %collective-permute-start.13 = (bf16[80,1024]{1,0:T(8,128)(2,1)S(1)}, bf16[80,1024]{1,0:T(8,128)(2,1)S(1)}, u32[]{:S(2)}, u32[]{:S(2)}) collective-permute-start(bf16[80,1024]{1,0:T(8,128)(2,1)S(1)} %get-tuple-element.38), channel_id=1, source_target_pairs={{0,8},{8,0},{16,24},{24,16},{1,9},{9,1},{17,25},{25,17},{2,10},{10... | collective-permute-start | bytes 491528 | tf_op jit(solution)/shard_map/ppermute | solution.py:19
  29.3 0.3 collective-permute-start.16
  29.6 1.2 %collective-permute-done.14.b_ref = bf16[80,1024]{1,0:T(8,128)(2,1)S(1)} collective-permute-done((bf16[80,1024]{1,0:T(8,128)(2,1)S(1)}, bf16[80,1024]{1,0:T(8,128)(2,1)S(1)}, u32[]{:S(2)}, u32[]{:S(2)}) %collective-permute-start.14) | collective-permute-done | bytes 163872 | tf_op jit(solution)/shard_map/ppermute | solution.py:19
  30.9 2.6 %collective-permute-start.15 = (bf16[80,1024]{1,0:T(8,128)(2,1)S(1)}, bf16[80,1024]{1,0:T(8,128)(2,1)S(1)}, u32[]{:S(2)}, u32[]{:S(2)}) collective-permute-start(bf16[80,1024]{1,0:T(8,128)(2,1)S(1)} %shard_map.60), channel_id=1, source_target_pairs={{0,16},{8,24},{16,0},{24,8},{1,17},{9,25},{17,1},{25,9},{2,18},{10... | collective-permute-start | bytes 491528 | tf_op jit(solution)/shard_map/ppermute | solution.py:19
  33.5 1.6 %collective-permute-start.18 = (bf16[80,1024]{1,0:T(8,128)(2,1)S(1)}, bf16[80,1024]{1,0:T(8,128)(2,1)S(1)}, u32[]{:S(2)}, u32[]{:S(2)}) collective-permute-start(bf16[80,1024]{1,0:T(8,128)(2,1)S(1)} %shard_map.61), channel_id=1, source_target_pairs={{0,8},{8,0},{16,24},{24,16},{1,9},{9,1},{17,25},{25,17},{2,10},{10... | collective-permute-start | bytes 491528 | tf_op jit(solution)/shard_map/ppermute | solution.py:19
  35.0 0.5 %shard_map.58 = (bf16[80,1024]{1,0:T(8,128)(2,1)S(1)}, bf16[80,1024]{1,0:T(8,128)(2,1)S(1)}) custom-call(bf16[160,1024]{1,0:T(8,128)(2,1)S(1)} %get-tuple-element.36.attn_ref, bf16[1024,4096]{1,0:T(8,128)(2,1)S(1)} %get-tuple-element.35.refs_7_.weight_ref), custom_call_target="tpu_custom_call" | custom-call | flops 335544320 | bytes 2097152 | tf_op jit(solution)/shard_map/pallas_call | solution.py:200
  35.6 1.1 %collective-permute-done.16.refs_4_ = bf16[80,1024]{1,0:T(8,128)(2,1)S(1)} collective-permute-done((bf16[80,1024]{1,0:T(8,128)(2,1)S(1)}, bf16[80,1024]{1,0:T(8,128)(2,1)S(1)}, u32[]{:S(2)}, u32[]{:S(2)}) %collective-permute-start.16) | collective-permute-done | bytes 163872 | tf_op jit(solution)/shard_map/ppermute | solution.py:19
  36.7 2.5 %collective-permute-done.15.refs_2_ = bf16[80,1024]{1,0:T(8,128)(2,1)S(1)} collective-permute-done((bf16[80,1024]{1,0:T(8,128)(2,1)S(1)}, bf16[80,1024]{1,0:T(8,128)(2,1)S(1)}, u32[]{:S(2)}, u32[]{:S(2)}) %collective-permute-start.15) | collective-permute-done | bytes 163872 | tf_op jit(solution)/shard_map/ppermute | solution.py:19
  39.2 0.8 %shard_map.62 = bf16[160,1024]{1,0:T(8,128)(2,1)} custom-call(bf16[80,1024]{1,0:T(8,128)(2,1)S(1)} %get-tuple-element.37.refs_0_, bf16[80,1024]{1,0:T(8,128)(2,1)S(1)} %collective-permute-done.13.refs_1_, bf16[80,1024]{1,0:T(8,128)(2,1)S(1)} %collective-permute-done.15.refs_2_, bf16[80,1024]{1,0:T(8,128)(2,1)S(1)} %get-tuple-element.41.refs_3_, ...), custom_call_target="tpu_custom_call" | custom-call | flops 327680 | bytes 1310720 | tf_op jit(solution)/shard_map/pallas_call | solution.py:241
  (22 shorter events, 0.1 us)
Async XLA Ops:
  0.8 9.1 %collective-permute-start.1 = (bf16[40,256]{1,0:T(8,128)(2,1)S(1)}, bf16[40,256]{1,0:T(8,128)(2,1)S(1)}, u32[]{:S(2)}, u32[]{:S(2)}) collective-permute-start(bf16[40,256]{1,0:T(8,128)(2,1)S(1)} %pad_maximum_fusion.2), channel_id=1, source_target_pairs={{0,16},{8,24},{16,0},{24,8},{1,17},{9,25},{17,1},{25,9},{2,18},{10... | collective-permute-start | bytes 61448 | tf_op jit(solution)/shard_map/ppermute | solution.py:19
  3.9 6.2 %collective-permute-start.2 = (bf16[40,256]{1,0:T(8,128)(2,1)S(1)}, bf16[40,256]{1,0:T(8,128)(2,1)S(1)}, u32[]{:S(2)}, u32[]{:S(2)}) collective-permute-start(bf16[40,256]{1,0:T(8,128)(2,1)S(1)} %pad_maximum_fusion.3), channel_id=1, source_target_pairs={{0,24},{8,16},{16,8},{24,0},{1,25},{9,17},{17,9},{25,1},{2,26},{10... | collective-permute-start | bytes 61448 | tf_op jit(solution)/shard_map/ppermute | solution.py:19
  5.3 4.7 %collective-permute-start = (bf16[40,256]{1,0:T(8,128)(2,1)S(1)}, bf16[40,256]{1,0:T(8,128)(2,1)S(1)}, u32[]{:S(2)}, u32[]{:S(2)}) collective-permute-start(bf16[40,256]{1,0:T(8,128)(2,1)S(1)} %pad_maximum_fusion.1), channel_id=1, source_target_pairs={{0,8},{8,0},{16,24},{24,16},{1,9},{9,1},{17,25},{25,17},{2,10},{10... | collective-permute-start | bytes 61448 | tf_op jit(solution)/shard_map/ppermute | solution.py:19
  6.5 7.7 %collective-permute-start.8 = (bf16[40,1024]{1,0:T(8,128)(2,1)S(1)}, bf16[40,1024]{1,0:T(8,128)(2,1)S(1)}, u32[]{:S(2)}, u32[]{:S(2)}) collective-permute-start(bf16[40,1024]{1,0:T(8,128)(2,1)S(1)} %get-tuple-element.45), channel_id=1, source_target_pairs={{0,24},{8,16},{16,8},{24,0},{1,25},{9,17},{17,9},{25,1},{2,26},{10... | collective-permute-start | bytes 245768 | tf_op jit(solution)/shard_map/ppermute | solution.py:19
  9.4 5.4 %collective-permute-start.6 = (bf16[40,1024]{1,0:T(8,128)(2,1)S(1)}, bf16[40,1024]{1,0:T(8,128)(2,1)S(1)}, u32[]{:S(2)}, u32[]{:S(2)}) collective-permute-start(bf16[40,1024]{1,0:T(8,128)(2,1)S(1)} %get-tuple-element.46), channel_id=1, source_target_pairs={{0,8},{8,0},{16,24},{24,16},{1,9},{9,1},{17,25},{25,17},{2,10},{10... | collective-permute-start | bytes 245768 | tf_op jit(solution)/shard_map/ppermute | solution.py:19
  9.9 4.8 %collective-permute-start.7 = (bf16[40,1024]{1,0:T(8,128)(2,1)S(1)}, bf16[40,1024]{1,0:T(8,128)(2,1)S(1)}, u32[]{:S(2)}, u32[]{:S(2)}) collective-permute-start(bf16[40,1024]{1,0:T(8,128)(2,1)S(1)} %get-tuple-element.48), channel_id=1, source_target_pairs={{0,16},{8,24},{16,0},{24,8},{1,17},{9,25},{17,1},{25,9},{2,18},{10... | collective-permute-start | bytes 245768 | tf_op jit(solution)/shard_map/ppermute | solution.py:19
  10.1 9.5 %collective-permute-start.5 = (bf16[160,256]{1,0:T(8,128)(2,1)S(1)}, bf16[160,256]{1,0:T(8,128)(2,1)S(1)}, u32[]{:S(2)}, u32[]{:S(2)}) collective-permute-start(bf16[160,256]{1,0:T(8,128)(2,1)S(1)} %pad_maximum_fusion.after_ref.refs_0_), channel_id=1, source_target_pairs={{0,6},{1,7},{2,4},{3,5},{4,2},{5,3},{6,0},{7,1},{8,14},{9,15},{10,... | collective-permute-start | bytes 245768 | tf_op jit(solution)/shard_map/ppermute | solution.py:19
  14.1 5.6 %collective-permute-start.4 = (bf16[160,256]{1,0:T(8,128)(2,1)S(1)}, bf16[160,256]{1,0:T(8,128)(2,1)S(1)}, u32[]{:S(2)}, u32[]{:S(2)}) collective-permute-start(bf16[160,256]{1,0:T(8,128)(2,1)S(1)} %pad_maximum_fusion.after_ref.refs_0_), channel_id=1, source_target_pairs={{0,4},{1,5},{2,6},{3,7},{4,0},{5,1},{6,2},{7,3},{8,12},{9,13},{10,... | collective-permute-start | bytes 245768 | tf_op jit(solution)/shard_map/ppermute | solution.py:19
  14.1 5.6 %collective-permute-start.3 = (bf16[160,256]{1,0:T(8,128)(2,1)S(1)}, bf16[160,256]{1,0:T(8,128)(2,1)S(1)}, u32[]{:S(2)}, u32[]{:S(2)}) collective-permute-start(bf16[160,256]{1,0:T(8,128)(2,1)S(1)} %pad_maximum_fusion.after_ref.refs_0_), channel_id=1, source_target_pairs={{0,2},{1,3},{2,0},{3,1},{4,6},{5,7},{6,4},{7,5},{8,10},{9,11},{10,... | collective-permute-start | bytes 245768 | tf_op jit(solution)/shard_map/ppermute | solution.py:19
  14.8 7.4 %collective-permute-start.9 = (bf16[160,256]{1,0:T(8,128)(2,1)S(1)}, bf16[160,256]{1,0:T(8,128)(2,1)S(1)}, u32[]{:S(2)}, u32[]{:S(2)}) collective-permute-start(bf16[160,256]{1,0:T(8,128)(2,1)S(1)} %pad_maximum_fusion.after_ref.refs_0_), channel_id=1, source_target_pairs={{0,1},{1,0},{2,3},{3,2},{4,5},{5,4},{6,7},{7,6},{8,9},{9,8},{10,11... | collective-permute-start | bytes 245768 | tf_op jit(solution)/shard_map/ppermute | solution.py:19
  14.8 0.7 %copy-start = (s32[32]{0:T(128)S(1)}, s32[32]{0:T(128)}, u32[]{:S(2)}) copy-start(s32[32]{0:T(128)} %order_ref.1) | copy-start | bytes 388
  19.8 2.4 %collective-permute-start.10 = (bf16[160,256]{1,0:T(8,128)(2,1)S(1)}, bf16[160,256]{1,0:T(8,128)(2,1)S(1)}, u32[]{:S(2)}, u32[]{:S(2)}) collective-permute-start(bf16[160,256]{1,0:T(8,128)(2,1)S(1)} %collective-permute-done.3.refs_1_), channel_id=1, source_target_pairs={{0,1},{1,0},{2,3},{3,2},{4,5},{5,4},{6,7},{7,6},{8,9},{9,8},{10,11... | collective-permute-start | bytes 245768 | tf_op jit(solution)/shard_map/ppermute | solution.py:19
  20.2 2.0 %collective-permute-start.11 = (bf16[160,256]{1,0:T(8,128)(2,1)S(1)}, bf16[160,256]{1,0:T(8,128)(2,1)S(1)}, u32[]{:S(2)}, u32[]{:S(2)}) collective-permute-start(bf16[160,256]{1,0:T(8,128)(2,1)S(1)} %collective-permute-done.4.refs_2_), channel_id=1, source_target_pairs={{0,1},{1,0},{2,3},{3,2},{4,5},{5,4},{6,7},{7,6},{8,9},{9,8},{10,11... | collective-permute-start | bytes 245768 | tf_op jit(solution)/shard_map/ppermute | solution.py:19
  20.3 1.9 %collective-permute-start.12 = (bf16[160,256]{1,0:T(8,128)(2,1)S(1)}, bf16[160,256]{1,0:T(8,128)(2,1)S(1)}, u32[]{:S(2)}, u32[]{:S(2)}) collective-permute-start(bf16[160,256]{1,0:T(8,128)(2,1)S(1)} %collective-permute-done.5.refs_3_), channel_id=1, source_target_pairs={{0,1},{1,0},{2,3},{3,2},{4,5},{5,4},{6,7},{7,6},{8,9},{9,8},{10,11... | collective-permute-start | bytes 245768 | tf_op jit(solution)/shard_map/ppermute | solution.py:19
  24.5 6.3 %collective-permute-start.14 = (bf16[80,1024]{1,0:T(8,128)(2,1)S(1)}, bf16[80,1024]{1,0:T(8,128)(2,1)S(1)}, u32[]{:S(2)}, u32[]{:S(2)}) collective-permute-start(bf16[80,1024]{1,0:T(8,128)(2,1)S(1)} %get-tuple-element.40), channel_id=1, source_target_pairs={{0,8},{8,0},{16,24},{24,16},{1,9},{9,1},{17,25},{25,17},{2,10},{10... | collective-permute-start | bytes 491528 | tf_op jit(solution)/shard_map/ppermute | solution.py:19
  26.2 7.2 %collective-permute-start.17 = (bf16[80,1024]{1,0:T(8,128)(2,1)S(1)}, bf16[80,1024]{1,0:T(8,128)(2,1)S(1)}, u32[]{:S(2)}, u32[]{:S(2)}) collective-permute-start(bf16[80,1024]{1,0:T(8,128)(2,1)S(1)} %get-tuple-element.44), channel_id=1, source_target_pairs={{0,16},{8,24},{16,0},{24,8},{1,17},{9,25},{17,1},{25,9},{2,18},{10... | collective-permute-start | bytes 491528 | tf_op jit(solution)/shard_map/ppermute | solution.py:19
  28.7 6.9 %collective-permute-start.13 = (bf16[80,1024]{1,0:T(8,128)(2,1)S(1)}, bf16[80,1024]{1,0:T(8,128)(2,1)S(1)}, u32[]{:S(2)}, u32[]{:S(2)}) collective-permute-start(bf16[80,1024]{1,0:T(8,128)(2,1)S(1)} %get-tuple-element.38), channel_id=1, source_target_pairs={{0,8},{8,0},{16,24},{24,16},{1,9},{9,1},{17,25},{25,17},{2,10},{10... | collective-permute-start | bytes 491528 | tf_op jit(solution)/shard_map/ppermute | solution.py:19
  29.3 7.4 %collective-permute-start.16 = (bf16[80,1024]{1,0:T(8,128)(2,1)S(1)}, bf16[80,1024]{1,0:T(8,128)(2,1)S(1)}, u32[]{:S(2)}, u32[]{:S(2)}) collective-permute-start(bf16[80,1024]{1,0:T(8,128)(2,1)S(1)} %get-tuple-element.42), channel_id=1, source_target_pairs={{0,16},{8,24},{16,0},{24,8},{1,17},{9,25},{17,1},{25,9},{2,18},{10... | collective-permute-start | bytes 491528 | tf_op jit(solution)/shard_map/ppermute | solution.py:19
  30.9 8.3 %collective-permute-start.15 = (bf16[80,1024]{1,0:T(8,128)(2,1)S(1)}, bf16[80,1024]{1,0:T(8,128)(2,1)S(1)}, u32[]{:S(2)}, u32[]{:S(2)}) collective-permute-start(bf16[80,1024]{1,0:T(8,128)(2,1)S(1)} %shard_map.60), channel_id=1, source_target_pairs={{0,16},{8,24},{16,0},{24,8},{1,17},{9,25},{17,1},{25,9},{2,18},{10... | collective-permute-start | bytes 491528 | tf_op jit(solution)/shard_map/ppermute | solution.py:19
  33.5 5.7 %collective-permute-start.18 = (bf16[80,1024]{1,0:T(8,128)(2,1)S(1)}, bf16[80,1024]{1,0:T(8,128)(2,1)S(1)}, u32[]{:S(2)}, u32[]{:S(2)}) collective-permute-start(bf16[80,1024]{1,0:T(8,128)(2,1)S(1)} %shard_map.61), channel_id=1, source_target_pairs={{0,8},{8,0},{16,24},{24,16},{1,9},{9,1},{17,25},{25,17},{2,10},{10... | collective-permute-start | bytes 491528 | tf_op jit(solution)/shard_map/ppermute | solution.py:19

commit v4 on v3

--- a/solution.py
+++ b/solution.py
@@ -11,12 +11,24 @@
 D_HEAD = 128
 NEG_FILL = -1e30
 ROOMY = 42
+STRIPE = 256
 FETCHES = 8
 EXP2_SCALE = D_HEAD ** (-0.5) * math.log2(math.e)
 
 
 def swap(x, axis, flip, size):
     return lax.ppermute(x, axis, [(i, i ^ flip) for i in range(size)])
+
+
+def swap_by_core(x, flips, n_head, n_ctx):
+    pairs = [
+        (j * n_ctx + c, (j ^ flips[c % 2]) * n_ctx + c) for j in range(n_head) for c in range(n_ctx)
+    ]
+    return lax.ppermute(x, ("head", "ctx"), pairs)
+
+
+def first_flip():
+    return 1 + lax.rem(lax.axis_index("ctx"), 2)
 
 
 def lookup_positions(order, flat_rows, span):
@@ -92,33 +104,56 @@
     )(order, weight, after, *q_pieces)
 
 
-def project(attn, weight_ref, me, flip, cols):
-    at = pl.multiple_of((me ^ flip) * cols, cols)
+def project(attn, weight_ref, flip, cols):
+    at = pl.multiple_of((lax.axis_index("head") ^ flip) * cols, cols)
     part = jnp.dot(attn, weight_ref[:, pl.ds(at, cols)], preferred_element_type=jnp.float32)
     return part.astype(jnp.bfloat16)
 
 
-def masked_scores(kv_refs, kpos, qpos_ref, q_ref):
+def fold_keys(kv_refs, kpos, qpos_ref, q_ref, state, emit):
     keys = jnp.concatenate([ref[:, :D_HEAD] for ref in kv_refs], axis=0)
-    scores = jnp.dot(keys, q_ref[...], preferred_element_type=jnp.float32)
-    kpos = jnp.concatenate([kpos] * (scores.shape[1] // D_HEAD), axis=1)
-    return jnp.where(kpos <= qpos_ref[...], scores, NEG_FILL)
-
-
-def mix_values(kv_refs, weights):
-    values = jnp.concatenate([ref[:, D_HEAD:] for ref in kv_refs], axis=0)
-    return jnp.dot(values.T, weights.astype(jnp.bfloat16), preferred_element_type=jnp.float32)
+    values = jnp.concatenate([ref[:, D_HEAD:] for ref in kv_refs], axis=0).T
+    kpos = jnp.concatenate([kpos] * (STRIPE // D_HEAD), axis=1)
+
+    def score(at):
+        scores = jnp.dot(keys, q_ref[:, at], preferred_element_type=jnp.float32)
+        return jnp.where(kpos <= qpos_ref[:, at], scores, NEG_FILL)
+
+    def weigh(at, scores):
+        peak = jnp.max(scores, axis=0, keepdims=True)
+        if state is not None:
+            peak = jnp.maximum(state[0][:, at], peak)
+        weights = jnp.exp2((scores - peak) * EXP2_SCALE)
+        return peak, jnp.sum(weights, axis=0, keepdims=True), weights.astype(jnp.bfloat16)
+
+    def finish(at, peak, denom, weights):
+        mixed = jnp.dot(values, weights, preferred_element_type=jnp.float32)
+        if state is not None:
+            factor = jnp.exp2((state[0][:, at] - peak) * EXP2_SCALE)
+            denom = factor * state[1][:, at] + denom
+            mixed = factor * state[2][:, at] + mixed
+        emit(at, peak, denom, mixed)
+
+    stripes = [slice(i, i + STRIPE) for i in range(0, q_ref.shape[1], STRIPE)]
+    scores, held = score(stripes[0]), None
+    for i, at in enumerate(stripes):
+        ahead = score(stripes[i + 1]) if i + 1 < len(stripes) else None
+        weighed = weigh(at, scores)
+        if held is not None:
+            finish(stripes[i - 1], *held)
+        scores, held = ahead, weighed
+    finish(stripes[-1], *held)
 
 
 def early_kernel(n_chunk, kpos_ref, qpos_ref, q_ref, *refs):
-    kv_refs, (peak_ref, denom_ref, mixed_ref) = refs[:n_chunk], refs[n_chunk:]
+    kv_refs, out = refs[:n_chunk], refs[n_chunk:]
     n_keys = kv_refs[0].shape[0] * n_chunk
-    scores = masked_scores(kv_refs, kpos_ref[:n_keys, :], qpos_ref, q_ref)
-    peak = jnp.max(scores, axis=0, keepdims=True)
-    weights = jnp.exp2((scores - peak) * EXP2_SCALE)
-    peak_ref[...] = peak
-    denom_ref[...] = jnp.sum(weights, axis=0, keepdims=True)
-    mixed_ref[...] = mix_values(kv_refs, weights)
+
+    def emit(at, peak, denom, mixed):
+        for ref, value in zip(out, (peak, denom, mixed), strict=True):
+            ref[:, at] = value
+
+    fold_keys(kv_refs, kpos_ref[:n_keys, :], qpos_ref, q_ref, None, emit)
 
 
 def early_attend(kpos, qpos, q_all, kv_chunks):
@@ -141,24 +176,21 @@
 
 
 def attend_kernel(n_chunk, kpos_ref, qpos_ref, q_ref, *refs):
-    kv_refs = refs[:n_chunk]
-    peak_ref, denom_ref, mixed_ref, weight_ref, attn_ref, low_ref, high_ref = refs[n_chunk:]
+    kv_refs, state = refs[:n_chunk], refs[n_chunk : n_chunk + 3]
+    weight_ref, attn_ref, far_ref = refs[n_chunk + 3 :]
     seg, width = attn_ref.shape
     n_keys = kv_refs[0].shape[0] * n_chunk
-    scores = masked_scores(kv_refs, kpos_ref[n_keys:, :], qpos_ref, q_ref)
-    peak = jnp.maximum(peak_ref[...], jnp.max(scores, axis=0, keepdims=True))
-    weights = jnp.exp2((scores - peak) * EXP2_SCALE)
-    factor = jnp.exp2((peak_ref[...] - peak) * EXP2_SCALE)
-    inverse = 1.0 / (factor * denom_ref[...] + jnp.sum(weights, axis=0, keepdims=True))
-    mixed = mixed_ref[...] * (factor * inverse) + mix_values(kv_refs, weights) * inverse
-    mixed = mixed.T.astype(jnp.bfloat16)
+    rows = []
+
+    def emit(at, peak, denom, mixed):
+        rows.append((mixed * (1.0 / denom)).T.astype(jnp.bfloat16))
+
+    fold_keys(kv_refs, kpos_ref[n_keys:, :], qpos_ref, q_ref, state, emit)
+    rows = jnp.concatenate(rows, axis=0)
     heads = width // D_HEAD
-    attn = jnp.concatenate([mixed[h * seg : (h + 1) * seg] for h in range(heads)], axis=1)
+    attn = jnp.concatenate([rows[h * seg : (h + 1) * seg] for h in range(heads)], axis=1)
     attn_ref[...] = attn
-    part = project(attn, weight_ref, lax.axis_index("head"), 3, low_ref.shape[1])
-    half = low_ref.shape[0]
-    low_ref[...] = part[:half]
-    high_ref[...] = part[half:]
+    far_ref[...] = project(attn, weight_ref, 3, far_ref.shape[1])
 
 
 def attend(kpos, qpos, q_all, kv_chunks, state, weight, n_head):
@@ -168,12 +200,14 @@
     n_keys = kv_chunks[0].shape[0] * n_chunk
     cols = out_width // n_head
     vmem = pl.BlockSpec(memory_space=pltpu.VMEM)
-    half = jax.ShapeDtypeStruct((seg // 2, cols), jnp.bfloat16)
     return pl.pallas_call(
         functools.partial(attend_kernel, n_chunk),
-        out_shape=(jax.ShapeDtypeStruct((seg, width), jnp.bfloat16), half, half),
+        out_shape=(
+            jax.ShapeDtypeStruct((seg, width), jnp.bfloat16),
+            jax.ShapeDtypeStruct((seg, cols), jnp.bfloat16),
+        ),
         in_specs=[vmem] * (7 + n_chunk),
-        out_specs=(vmem, vmem, vmem),
+        out_specs=(vmem, vmem),
         compiler_params=pltpu.CompilerParams(vmem_limit_bytes=28 * 1024 * 1024),
         cost_estimate=pl.CostEstimate(
             flops=4 * columns * depth * n_keys + 2 * seg * width * cols,
@@ -183,25 +217,25 @@
     )(kpos, qpos, q_all, *kv_chunks, *state, weight)
 
 
-def project_kernel(flips, attn_ref, weight_ref, *out_refs):
-    me = lax.axis_index("head")
-    half, cols = out_refs[0].shape
-    for i, flip in enumerate(flips):
-        part = project(attn_ref[...], weight_ref, me, flip, cols)
-        out_refs[2 * i][...] = part[:half]
-        out_refs[2 * i + 1][...] = part[half:]
-
-
-def project_rest(attn, weight, flips, n_head):
+def near_kernel(attn_ref, weight_ref, first_ref, second_ref):
+    flip = first_flip()
+    first_ref[...] = project(attn_ref[...], weight_ref, flip, first_ref.shape[1])
+    second_ref[...] = project(attn_ref[...], weight_ref, 3 - flip, first_ref.shape[1])
+
+
+def own_kernel(attn_ref, weight_ref, out_ref):
+    out_ref[...] = project(attn_ref[...], weight_ref, 0, out_ref.shape[1])
+
+
+def project_rest(kernel, n, attn, weight, n_head):
     seg, width = attn.shape
-    n, cols = len(flips), weight.shape[1] // n_head
+    cols = weight.shape[1] // n_head
     vmem = pl.BlockSpec(memory_space=pltpu.VMEM)
-    half = jax.ShapeDtypeStruct((seg // 2, cols), jnp.bfloat16)
     return pl.pallas_call(
-        functools.partial(project_kernel, flips),
-        out_shape=(half,) * (2 * n),
+        kernel,
+        out_shape=(jax.ShapeDtypeStruct((seg, cols), jnp.bfloat16),) * n,
         in_specs=[vmem, vmem],
-        out_specs=(vmem,) * (2 * n),
+        out_specs=(vmem,) * n,
         compiler_params=pltpu.CompilerParams(vmem_limit_bytes=20 * 1024 * 1024),
         cost_estimate=pl.CostEstimate(
             flops=2 * seg * width * cols * n,
@@ -211,41 +245,22 @@
     )(attn, weight)
 
 
-def add_kernel(a_ref, b_ref, out_ref):
-    out_ref[...] = (a_ref[...].astype(jnp.float32) + b_ref[...].astype(jnp.float32)).astype(jnp.bfloat16)
-
-
-def add_pair(a, b):
+def sum_kernel(*refs):
+    total = sum(ref[...].astype(jnp.float32) for ref in refs[:-1])
+    refs[-1][...] = total.astype(jnp.bfloat16)
+
+
+def sum_blocks(*blocks):
     vmem = pl.BlockSpec(memory_space=pltpu.VMEM)
+    size = blocks[0].size * len(blocks)
     return pl.pallas_call(
-        add_kernel,
-        out_shape=jax.ShapeDtypeStruct(a.shape, jnp.bfloat16),
-        in_specs=[vmem, vmem],
+        sum_kernel,
+        out_shape=jax.ShapeDtypeStruct(blocks[0].shape, jnp.bfloat16),
+        in_specs=[vmem] * len(blocks),
         out_specs=vmem,
         compiler_params=pltpu.CompilerParams(vmem_limit_bytes=6 * 1024 * 1024),
-        cost_estimate=pl.CostEstimate(flops=a.size, bytes_accessed=6 * a.size, transcendentals=0),
-    )(a, b)
-
-
-def final_kernel(*refs):
-    out_ref = refs[-1]
-    half = out_ref.shape[0] // 2
-    for i in range(2):
-        total = sum(ref[...].astype(jnp.float32) for ref in refs[3 * i : 3 * i + 3])
-        out_ref[i * half : (i + 1) * half, :] = total.astype(jnp.bfloat16)
-
-
-def final_sum(low, high):
-    vmem = pl.BlockSpec(memory_space=pltpu.VMEM)
-    rows, cols = low[0].shape
-    return pl.pallas_call(
-        final_kernel,
-        out_shape=jax.ShapeDtypeStruct((2 * rows, cols), jnp.bfloat16),
-        in_specs=[vmem] * 6,
-        out_specs=vmem,
-        compiler_params=pltpu.CompilerParams(vmem_limit_bytes=6 * 1024 * 1024),
-        cost_estimate=pl.CostEstimate(flops=4 * rows * cols, bytes_accessed=16 * rows * cols, transcendentals=0),
-    )(*low, *high)
+        cost_estimate=pl.CostEstimate(flops=size, bytes_accessed=2 * size, transcendentals=0),
+    )(*blocks)
 
 
 def fast_path(queries, key_rows, value_rows, stretch_order, out_weight, n_head, n_ctx):
@@ -272,16 +287,13 @@
     same_core = [own] + far_keys
     other_core = [swap(x, "ctx", 1, n_ctx) for x in same_core]
     state = early_attend(kpos, qpos, q_all, same_core)
-    attn, far_low, far_high = attend(kpos, qpos, q_all, other_core, state, weight, n_head)
-    x_far = swap(far_low, "head", 1, n_head)
-    y_far = swap(far_high, "head", 2, n_head)
-    x_low, x_high, y_low, y_high = project_rest(attn, weight, (1, 2), n_head)
-    x_near = swap(x_low, "head", 1, n_head)
-    y_near = swap(y_high, "head", 2, n_head)
-    own_low, own_high = project_rest(attn, weight, (0,), n_head)
-    y_sum = swap(add_pair(y_low, x_far), "head", 2, n_head)
-    x_sum = swap(add_pair(x_high, y_far), "head", 1, n_head)
-    return final_sum((own_low, x_near, y_sum), (own_high, y_near, x_sum))
+    attn, far = attend(kpos, qpos, q_all, other_core, state, weight, n_head)
+    passed = swap_by_core(far, (1, 2), n_head, n_ctx)
+    first, second = project_rest(near_kernel, 2, attn, weight, n_head)
+    received = swap_by_core(first, (1, 2), n_head, n_ctx)
+    (kept,) = project_rest(own_kernel, 1, attn, weight, n_head)
+    joined = swap_by_core(sum_blocks(second, passed), (2, 1), n_head, n_ctx)
+    return sum_blocks(kept, received, joined)
 
 
 def attend_block(state, query_heads, query_pos, key_block, value_block, key_pos):

time: 40.2 us -> 39.6 us (0.985)
  starting transfers between devices: 22.1 us -> 17.7 us
  waiting for transfers between devices: 5 us -> 9.18 us
    ppermute x0 -> x3, waiting for transfers between devices: none -> 8.97 us  [swap_by_core(): return lax.ppermute(x, ('head', 'ctx'), pairs)]
    ppermute x19 -> x13, starting transfers between devices: 22.1 us -> 13.8 us  [swap(): return lax.ppermute(x, axis, [(i, i ^ flip) for i in range(size)])]
    ppermute x19 -> x13, waiting for transfers between devices: 5 us -> 0.21 us  [swap(): return lax.ppermute(x, axis, [(i, i ^ flip) for i in range(size)])]
    ppermute x0 -> x3, starting transfers between devices: none -> 3.88 us  [swap_by_core(): return lax.ppermute(x, ('head', 'ctx'), pairs)]
    pallas_call x5 -> x4, Pallas kernels: 2.34 us -> 2.33 us  [the longest x2 1.41 us: project_rest(): pl.pallas_call(kernel, out_shape=(jax.ShapeDtypeStruct((seg, cols), jnp.b...]
  transfers between devices with their start and end apart: 19 -> 16, of which waited for: 4 -> 4; matrix products, arithmetic and copies ran while one was open for 3% -> 3% of each run, Pallas kernels for 18% -> 18%
where the time goes in v4:
time: 39.6 us; the launch traced here: 39.4 us
  starting transfers between devices  17.7 us (45%)
  Pallas kernels  9.92 us (25%)
  waiting for transfers between devices  9.18 us (23%)
  local copies, waits for them, and re-layouts  2.51 us (6%)
    ppermute x13, starting transfers between devices, swap(): return lax.ppermute(x, axis, [(i, i ^ flip) for i in range(size)])  13.8 us
    ppermute x3, waiting for transfers between devices, swap_by_core(): return lax.ppermute(x, ('head', 'ctx'), pairs)  8.97 us
    pallas_call x1, Pallas kernels, prepare(): pl.pallas_call(functools.partial(prepare_kernel, span, n_head, chunk_flip...  4.11 us
    ppermute x3, starting transfers between devices, swap_by_core(): return lax.ppermute(x, ('head', 'ctx'), pairs)  3.88 us
    pallas_call x1, Pallas kernels, attend(): pl.pallas_call(functools.partial(attend_kernel, n_chunk), out_shape=(jax....  1.99 us
    dynamic_slice x2, local copies, waits for them, and re-layouts, cut(): return lax.dynamic_slice_in_dim(x[0], (me ^ k) * width, width, 1)  1.86 us
    pallas_call x1, Pallas kernels, early_attend(): pl.pallas_call(functools.partial(early_kernel, n_chunk), out_shape=(line,...  1.49 us
    pallas_call x2, Pallas kernels, project_rest(): pl.pallas_call(kernel, out_shape=(jax.ShapeDtypeStruct((seg, cols), jnp.b...  1.41 us
  transfers between devices with their start and end apart: 16, of which 4 were waited for; matrix products, arithmetic and copies ran while one was open for 3% of the time, Pallas kernels for 18%

profile of v4, /device:TPU:0, one launch (start us, length us, event | category | flops | bytes accessed | tf_op | source)
XLA Modules:
  0.0 39.4 jit_solution(16667785291142043199)
XLA Ops:
  0.0 0.8 %dynamic-slice_bitcast_fusion.10 = (bf16[40,128]{1,0:T(8,128)(2,1)S(1)}, bf16[40,128]{1,0:T(8,128)(2,1)S(1)}, bf16[40,128]{1,0:T(8,128)(2,1)S(1)}, bf16[40,128]{...) fusion(bf16[1,40,512]{2,1,0:T(8,128)(2,1)} %param.7, ...), kind=kLoop, calls=%fused_computation.14 | loop fusion | bytes 163856 | tf_op jit(solution)/shard_map/dynamic_slice | solution.py:271
  0.8 3.0 %collective-permute-start.1 = (bf16[40,256]{1,0:T(8,128)(2,1)S(1)}, bf16[40,256]{1,0:T(8,128)(2,1)S(1)}, u32[]{:S(2)}, u32[]{:S(2)}) collective-permute-start(bf16[40,256]{1,0:T(8,128)(2,1)S(1)} %pad_maximum_fusion.2), channel_id=1, source_target_pairs={{0,16},{8,24},{16,0},{24,8},{1,17},{9,25},{17,1},{25,9},{2,18},{10... | collective-permute-start | bytes 61448 | tf_op jit(solution)/shard_map/ppermute | solution.py:20
  3.9 1.4 %collective-permute-start.2 = (bf16[40,256]{1,0:T(8,128)(2,1)S(1)}, bf16[40,256]{1,0:T(8,128)(2,1)S(1)}, u32[]{:S(2)}, u32[]{:S(2)}) collective-permute-start(bf16[40,256]{1,0:T(8,128)(2,1)S(1)} %pad_maximum_fusion.3), channel_id=1, source_target_pairs={{0,24},{8,16},{16,8},{24,0},{1,25},{9,17},{17,9},{25,1},{2,26},{10... | collective-permute-start | bytes 61448 | tf_op jit(solution)/shard_map/ppermute | solution.py:20
  5.3 0.1 collective-permute-start
  5.5 1.0 %dynamic-slice_bitcast_fusion = (bf16[40,1024]{1,0:T(8,128)(2,1)S(1)}, bf16[40,1024]{1,0:T(8,128)(2,1)S(1)}, bf16[40,1024]{1,0:T(8,128)(2,1)S(1)}, bf16[40,1024]{1,0:T(8,128)(2,1)S(1)}) fusion(bf16[1,40,4096]{2,1,0:T(8,128)(2,1)} %param.5, s32[]{:T(128)S(6)} %select_n.35, s32[]{:T(128)S(6)} %select_n.33, s32[]{:T(128)S(6)} %select_n.32, s32[]{:T(128)S(6)} %select_n.34), kind=kLoop, calls=%fused_computation.1 | loop fusion | bytes 655376 | tf_op jit(solution)/shard_map/dynamic_slice | solution.py:271
  6.5 2.9 %collective-permute-start.8 = (bf16[40,1024]{1,0:T(8,128)(2,1)S(1)}, bf16[40,1024]{1,0:T(8,128)(2,1)S(1)}, u32[]{:S(2)}, u32[]{:S(2)}) collective-permute-start(bf16[40,1024]{1,0:T(8,128)(2,1)S(1)} %get-tuple-element.35), channel_id=1, source_target_pairs={{0,24},{8,16},{16,8},{24,0},{1,25},{9,17},{17,9},{25,1},{2,26},{10... | collective-permute-start | bytes 245768 | tf_op jit(solution)/shard_map/ppermute | solution.py:20
  9.4 0.5 %collective-permute-start.6 = (bf16[40,1024]{1,0:T(8,128)(2,1)S(1)}, bf16[40,1024]{1,0:T(8,128)(2,1)S(1)}, u32[]{:S(2)}, u32[]{:S(2)}) collective-permute-start(bf16[40,1024]{1,0:T(8,128)(2,1)S(1)} %get-tuple-element.36), channel_id=1, source_target_pairs={{0,8},{8,0},{16,24},{24,16},{1,9},{9,1},{17,25},{25,17},{2,10},{10... | collective-permute-start | bytes 245768 | tf_op jit(solution)/shard_map/ppermute | solution.py:20
  9.9 0.0 collective-permute-done.1
  9.9 0.1 collective-permute-start.7
  10.0 0.0 collective-permute-done.2
  10.1 0.0 collective-permute-done
  10.1 4.1 %collective-permute-start.5 = (bf16[160,256]{1,0:T(8,128)(2,1)S(1)}, bf16[160,256]{1,0:T(8,128)(2,1)S(1)}, u32[]{:S(2)}, u32[]{:S(2)}) collective-permute-start(bf16[160,256]{1,0:T(8,128)(2,1)S(1)} %pad_maximum_fusion.after_ref.refs_0_), channel_id=1, source_target_pairs={{0,6},{1,7},{2,4},{3,5},{4,2},{5,3},{6,0},{7,1},{8,14},{9,15},{10,... | collective-permute-start | bytes 245768 | tf_op jit(solution)/shard_map/ppermute | solution.py:20
  14.1 0.6 %collective-permute-start.3 = (bf16[160,256]{1,0:T(8,128)(2,1)S(1)}, bf16[160,256]{1,0:T(8,128)(2,1)S(1)}, u32[]{:S(2)}, u32[]{:S(2)}) collective-permute-start(bf16[160,256]{1,0:T(8,128)(2,1)S(1)} %pad_maximum_fusion.after_ref.refs_0_), channel_id=1, source_target_pairs={{0,2},{1,3},{2,0},{3,1},{4,6},{5,7},{6,4},{7,5},{8,10},{9,11},{10,... | collective-permute-start | bytes 245768 | tf_op jit(solution)/shard_map/ppermute | solution.py:20
  14.8 0.0 copy-start
  14.8 0.6 %copy-done = s32[32]{0:T(128)S(1)} copy-done((s32[32]{0:T(128)S(1)}, s32[32]{0:T(128)}, u32[]{:S(2)}) %copy-start) | copy-done | bytes 152
  15.5 4.1 %shard_map.55 = (bf16[1024,4096]{1,0:T(8,128)(2,1)S(1)}, s32[1,1280]{1,0:T(1,128)S(1)}, s32[1280,128]{1,0:T(8,128)S(1)}, bf16[128,1280]{1,0:T(8,128)(2,1)S(1)}) custom-call(s32[32]{0:T(128)S(1)} %copy-done, bf16[1024,4096]{1,0:T(8,128)(2,1)} %weight_ref.1, bf16[160,256]{1,0:T(8,128)(2,1)S(1)} %pad_maximum_fusion.after_ref.refs_0_, ...), custom_call_target="tpu_custom_call" | custom-call | bytes 4194304 | tf_op jit(solution)/shard_map/pallas_call | solution.py:83
  19.6 0.2 collective-permute-done.4.refs_2_
  19.8 0.4 %collective-permute-start.10 = (bf16[160,256]{1,0:T(8,128)(2,1)S(1)}, bf16[160,256]{1,0:T(8,128)(2,1)S(1)}, u32[]{:S(2)}, u32[]{:S(2)}) collective-permute-start(bf16[160,256]{1,0:T(8,128)(2,1)S(1)} %collective-permute-done.3.refs_1_), channel_id=1, source_target_pairs={{0,1},{1,0},{2,3},{3,2},{4,5},{5,4},{6,7},{7,6},{8,9},{9,8},{10,11... | collective-permute-start | bytes 245768 | tf_op jit(solution)/shard_map/ppermute | solution.py:20
  20.2 0.1 collective-permute-start.11
  20.3 0.4 %collective-permute-start.12 = (bf16[160,256]{1,0:T(8,128)(2,1)S(1)}, bf16[160,256]{1,0:T(8,128)(2,1)S(1)}, u32[]{:S(2)}, u32[]{:S(2)}) collective-permute-start(bf16[160,256]{1,0:T(8,128)(2,1)S(1)} %collective-permute-done.5.refs_3_), channel_id=1, source_target_pairs={{0,1},{1,0},{2,3},{3,2},{4,5},{5,4},{6,7},{7,6},{8,9},{9,8},{10,11... | collective-permute-start | bytes 245768 | tf_op jit(solution)/shard_map/ppermute | solution.py:20
  20.7 1.5 %shard_map.56 = (f32[1,1280]{1,0:T(1,128)S(1)}, f32[1,1280]{1,0:T(1,128)S(1)}, f32[128,1280]{1,0:T(8,128)S(1)}) custom-call(s32[1280,128]{1,0:T(8,128)S(1)} %get-tuple-element.21.kpos_ref, s32[1,1280]{1,0:T(1,128)S(1)} %get-tuple-element.22.qpos_ref, bf16[128,1280]{1,0:T(8,128)(2,1)S(1)} %get-tuple-element.23.q_ref, ...), custom_call_target="tpu_custom_call" | custom-call | flops 419430400 | bytes 4194304 | tf_op jit(solution)/shard_map/pallas_call | solution.py:164
  22.2 2.0 %shard_map.57 = (bf16[160,1024]{1,0:T(8,128)(2,1)S(1)}, bf16[160,1024]{1,0:T(8,128)(2,1)S(1)}) custom-call(s32[1280,128]{1,0:T(8,128)S(1)} %get-tuple-element.21.kpos_ref, s32[1,1280]{1,0:T(1,128)S(1)} %get-tuple-element.22.qpos_ref, bf16[128,1280]{1,0:T(8,128)(2,1)S(1)} %get-tuple-element.23.q_ref, bf16[160,256]{1,0:T(8,128)(2,1)S(1)} %collective-permute-done.9.refs_0_, ...), custom_call_target="tpu_custom_call" | custom-call | flops 754974720 | bytes 4194304 | tf_op jit(solution)/shard_map/pallas_call | solution.py:203
  24.2 1.7 %collective-permute-start.14 = (bf16[160,1024]{1,0:T(8,128)(2,1)S(1)}, bf16[160,1024]{1,0:T(8,128)(2,1)S(1)}, u32[]{:S(2)}, u32[]{:S(2)}) collective-permute-start(bf16[160,1024]{1,0:T(8,128)(2,1)S(1)} %get-tuple-element.34), channel_id=1, source_target_pairs={{0,8},{1,17},{2,10},{3,19},{4,12},{5,21},{6,14},{7,23},{8,0},{9,25... | collective-permute-start | bytes 983048 | tf_op jit(solution)/shard_map/ppermute | solution.py:27
  25.9 0.9 %shard_map.59 = (bf16[160,1024]{1,0:T(8,128)(2,1)S(1)}, bf16[160,1024]{1,0:T(8,128)(2,1)S(1)}) custom-call(bf16[160,1024]{1,0:T(8,128)(2,1)S(1)} %get-tuple-element.31.attn_ref, bf16[1024,4096]{1,0:T(8,128)(2,1)S(1)} %get-tuple-element.30.refs_7_.weight_ref), custom_call_target="tpu_custom_call" | custom-call | flops 671088640 | bytes 4194304 | tf_op jit(solution)/shard_map/pallas_call | solution.py:234
  26.8 0.5 %collective-permute-start.13 = (bf16[160,1024]{1,0:T(8,128)(2,1)S(1)}, bf16[160,1024]{1,0:T(8,128)(2,1)S(1)}, u32[]{:S(2)}, u32[]{:S(2)}) collective-permute-start(bf16[160,1024]{1,0:T(8,128)(2,1)S(1)} %get-tuple-element.32), channel_id=1, source_target_pairs={{0,8},{1,17},{2,10},{3,19},{4,12},{5,21},{6,14},{7,23},{8,0},{9,25... | collective-permute-start | bytes 983048 | tf_op jit(solution)/shard_map/ppermute | solution.py:27
  27.3 4.1 %collective-permute-done.14.refs_1_ = bf16[160,1024]{1,0:T(8,128)(2,1)S(1)} collective-permute-done((bf16[160,1024]{1,0:T(8,128)(2,1)S(1)}, bf16[160,1024]{1,0:T(8,128)(2,1)S(1)}, u32[]{:S(2)}, u32[]{:S(2)}) %collective-permute-start.14) | collective-permute-done | bytes 327712 | tf_op jit(solution)/shard_map/ppermute | solution.py:27
  31.4 0.1 shard_map.60
  31.4 1.7 %collective-permute-start.15 = (bf16[160,1024]{1,0:T(8,128)(2,1)S(1)}, bf16[160,1024]{1,0:T(8,128)(2,1)S(1)}, u32[]{:S(2)}, u32[]{:S(2)}) collective-permute-start(bf16[160,1024]{1,0:T(8,128)(2,1)S(1)} %shard_map.60), channel_id=1, source_target_pairs={{0,16},{1,9},{2,18},{3,11},{4,20},{5,13},{6,22},{7,15},{8,24},{9,1... | collective-permute-start | bytes 983048 | tf_op jit(solution)/shard_map/ppermute | solution.py:27
  33.2 0.5 %shard_map.58.refs_0_ = bf16[160,1024]{1,0:T(8,128)(2,1)S(1)} custom-call(bf16[160,1024]{1,0:T(8,128)(2,1)S(1)} %get-tuple-element.31.attn_ref, bf16[1024,4096]{1,0:T(8,128)(2,1)S(1)} %get-tuple-element.30.refs_7_.weight_ref), custom_call_target="tpu_custom_call" | custom-call | flops 335544320 | bytes 2097152 | tf_op jit(solution)/shard_map/pallas_call | solution.py:234
  33.7 2.6 %collective-permute-done.13.refs_1_ = bf16[160,1024]{1,0:T(8,128)(2,1)S(1)} collective-permute-done((bf16[160,1024]{1,0:T(8,128)(2,1)S(1)}, bf16[160,1024]{1,0:T(8,128)(2,1)S(1)}, u32[]{:S(2)}, u32[]{:S(2)}) %collective-permute-start.13) | collective-permute-done | bytes 327712 | tf_op jit(solution)/shard_map/ppermute | solution.py:27
  36.3 2.2 %collective-permute-done.15.refs_2_ = bf16[160,1024]{1,0:T(8,128)(2,1)S(1)} collective-permute-done((bf16[160,1024]{1,0:T(8,128)(2,1)S(1)}, bf16[160,1024]{1,0:T(8,128)(2,1)S(1)}, u32[]{:S(2)}, u32[]{:S(2)}) %collective-permute-start.15) | collective-permute-done | bytes 327712 | tf_op jit(solution)/shard_map/ppermute | solution.py:27
  38.6 0.8 %shard_map.61 = bf16[160,1024]{1,0:T(8,128)(2,1)} custom-call(bf16[160,1024]{1,0:T(8,128)(2,1)S(1)} %shard_map.58.refs_0_, bf16[160,1024]{1,0:T(8,128)(2,1)S(1)} %collective-permute-done.13.refs_1_, bf16[160,1024]{1,0:T(8,128)(2,1)S(1)} %collective-permute-done.15.refs_2_), custom_call_target="tpu_custom_call" | custom-call | flops 491520 | bytes 983040 | tf_op jit(solution)/shard_map/pallas_call | solution.py:256
  (15 shorter events, 0.1 us)
Async XLA Ops:
  0.8 9.1 %collective-permute-start.1 = (bf16[40,256]{1,0:T(8,128)(2,1)S(1)}, bf16[40,256]{1,0:T(8,128)(2,1)S(1)}, u32[]{:S(2)}, u32[]{:S(2)}) collective-permute-start(bf16[40,256]{1,0:T(8,128)(2,1)S(1)} %pad_maximum_fusion.2), channel_id=1, source_target_pairs={{0,16},{8,24},{16,0},{24,8},{1,17},{9,25},{17,1},{25,9},{2,18},{10... | collective-permute-start | bytes 61448 | tf_op jit(solution)/shard_map/ppermute | solution.py:20
  3.9 6.2 %collective-permute-start.2 = (bf16[40,256]{1,0:T(8,128)(2,1)S(1)}, bf16[40,256]{1,0:T(8,128)(2,1)S(1)}, u32[]{:S(2)}, u32[]{:S(2)}) collective-permute-start(bf16[40,256]{1,0:T(8,128)(2,1)S(1)} %pad_maximum_fusion.3), channel_id=1, source_target_pairs={{0,24},{8,16},{16,8},{24,0},{1,25},{9,17},{17,9},{25,1},{2,26},{10... | collective-permute-start | bytes 61448 | tf_op jit(solution)/shard_map/ppermute | solution.py:20
  5.3 4.7 %collective-permute-start = (bf16[40,256]{1,0:T(8,128)(2,1)S(1)}, bf16[40,256]{1,0:T(8,128)(2,1)S(1)}, u32[]{:S(2)}, u32[]{:S(2)}) collective-permute-start(bf16[40,256]{1,0:T(8,128)(2,1)S(1)} %pad_maximum_fusion.1), channel_id=1, source_target_pairs={{0,8},{8,0},{16,24},{24,16},{1,9},{9,1},{17,25},{25,17},{2,10},{10... | collective-permute-start | bytes 61448 | tf_op jit(solution)/shard_map/ppermute | solution.py:20
  6.5 7.7 %collective-permute-start.8 = (bf16[40,1024]{1,0:T(8,128)(2,1)S(1)}, bf16[40,1024]{1,0:T(8,128)(2,1)S(1)}, u32[]{:S(2)}, u32[]{:S(2)}) collective-permute-start(bf16[40,1024]{1,0:T(8,128)(2,1)S(1)} %get-tuple-element.35), channel_id=1, source_target_pairs={{0,24},{8,16},{16,8},{24,0},{1,25},{9,17},{17,9},{25,1},{2,26},{10... | collective-permute-start | bytes 245768 | tf_op jit(solution)/shard_map/ppermute | solution.py:20
  9.4 5.4 %collective-permute-start.6 = (bf16[40,1024]{1,0:T(8,128)(2,1)S(1)}, bf16[40,1024]{1,0:T(8,128)(2,1)S(1)}, u32[]{:S(2)}, u32[]{:S(2)}) collective-permute-start(bf16[40,1024]{1,0:T(8,128)(2,1)S(1)} %get-tuple-element.36), channel_id=1, source_target_pairs={{0,8},{8,0},{16,24},{24,16},{1,9},{9,1},{17,25},{25,17},{2,10},{10... | collective-permute-start | bytes 245768 | tf_op jit(solution)/shard_map/ppermute | solution.py:20
  9.9 4.8 %collective-permute-start.7 = (bf16[40,1024]{1,0:T(8,128)(2,1)S(1)}, bf16[40,1024]{1,0:T(8,128)(2,1)S(1)}, u32[]{:S(2)}, u32[]{:S(2)}) collective-permute-start(bf16[40,1024]{1,0:T(8,128)(2,1)S(1)} %get-tuple-element.38), channel_id=1, source_target_pairs={{0,16},{8,24},{16,0},{24,8},{1,17},{9,25},{17,1},{25,9},{2,18},{10... | collective-permute-start | bytes 245768 | tf_op jit(solution)/shard_map/ppermute | solution.py:20
  10.1 9.5 %collective-permute-start.5 = (bf16[160,256]{1,0:T(8,128)(2,1)S(1)}, bf16[160,256]{1,0:T(8,128)(2,1)S(1)}, u32[]{:S(2)}, u32[]{:S(2)}) collective-permute-start(bf16[160,256]{1,0:T(8,128)(2,1)S(1)} %pad_maximum_fusion.after_ref.refs_0_), channel_id=1, source_target_pairs={{0,6},{1,7},{2,4},{3,5},{4,2},{5,3},{6,0},{7,1},{8,14},{9,15},{10,... | collective-permute-start | bytes 245768 | tf_op jit(solution)/shard_map/ppermute | solution.py:20
  14.1 5.6 %collective-permute-start.4 = (bf16[160,256]{1,0:T(8,128)(2,1)S(1)}, bf16[160,256]{1,0:T(8,128)(2,1)S(1)}, u32[]{:S(2)}, u32[]{:S(2)}) collective-permute-start(bf16[160,256]{1,0:T(8,128)(2,1)S(1)} %pad_maximum_fusion.after_ref.refs_0_), channel_id=1, source_target_pairs={{0,4},{1,5},{2,6},{3,7},{4,0},{5,1},{6,2},{7,3},{8,12},{9,13},{10,... | collective-permute-start | bytes 245768 | tf_op jit(solution)/shard_map/ppermute | solution.py:20
  14.1 5.6 %collective-permute-start.3 = (bf16[160,256]{1,0:T(8,128)(2,1)S(1)}, bf16[160,256]{1,0:T(8,128)(2,1)S(1)}, u32[]{:S(2)}, u32[]{:S(2)}) collective-permute-start(bf16[160,256]{1,0:T(8,128)(2,1)S(1)} %pad_maximum_fusion.after_ref.refs_0_), channel_id=1, source_target_pairs={{0,2},{1,3},{2,0},{3,1},{4,6},{5,7},{6,4},{7,5},{8,10},{9,11},{10,... | collective-permute-start | bytes 245768 | tf_op jit(solution)/shard_map/ppermute | solution.py:20
  14.8 7.4 %collective-permute-start.9 = (bf16[160,256]{1,0:T(8,128)(2,1)S(1)}, bf16[160,256]{1,0:T(8,128)(2,1)S(1)}, u32[]{:S(2)}, u32[]{:S(2)}) collective-permute-start(bf16[160,256]{1,0:T(8,128)(2,1)S(1)} %pad_maximum_fusion.after_ref.refs_0_), channel_id=1, source_target_pairs={{0,1},{1,0},{2,3},{3,2},{4,5},{5,4},{6,7},{7,6},{8,9},{9,8},{10,11... | collective-permute-start | bytes 245768 | tf_op jit(solution)/shard_map/ppermute | solution.py:20
  14.8 0.7 %copy-start = (s32[32]{0:T(128)S(1)}, s32[32]{0:T(128)}, u32[]{:S(2)}) copy-start(s32[32]{0:T(128)} %order_ref.1) | copy-start | bytes 388
  19.8 2.4 %collective-permute-start.10 = (bf16[160,256]{1,0:T(8,128)(2,1)S(1)}, bf16[160,256]{1,0:T(8,128)(2,1)S(1)}, u32[]{:S(2)}, u32[]{:S(2)}) collective-permute-start(bf16[160,256]{1,0:T(8,128)(2,1)S(1)} %collective-permute-done.3.refs_1_), channel_id=1, source_target_pairs={{0,1},{1,0},{2,3},{3,2},{4,5},{5,4},{6,7},{7,6},{8,9},{9,8},{10,11... | collective-permute-start | bytes 245768 | tf_op jit(solution)/shard_map/ppermute | solution.py:20
  20.2 2.0 %collective-permute-start.11 = (bf16[160,256]{1,0:T(8,128)(2,1)S(1)}, bf16[160,256]{1,0:T(8,128)(2,1)S(1)}, u32[]{:S(2)}, u32[]{:S(2)}) collective-permute-start(bf16[160,256]{1,0:T(8,128)(2,1)S(1)} %collective-permute-done.4.refs_2_), channel_id=1, source_target_pairs={{0,1},{1,0},{2,3},{3,2},{4,5},{5,4},{6,7},{7,6},{8,9},{9,8},{10,11... | collective-permute-start | bytes 245768 | tf_op jit(solution)/shard_map/ppermute | solution.py:20
  20.3 1.9 %collective-permute-start.12 = (bf16[160,256]{1,0:T(8,128)(2,1)S(1)}, bf16[160,256]{1,0:T(8,128)(2,1)S(1)}, u32[]{:S(2)}, u32[]{:S(2)}) collective-permute-start(bf16[160,256]{1,0:T(8,128)(2,1)S(1)} %collective-permute-done.5.refs_3_), channel_id=1, source_target_pairs={{0,1},{1,0},{2,3},{3,2},{4,5},{5,4},{6,7},{7,6},{8,9},{9,8},{10,11... | collective-permute-start | bytes 245768 | tf_op jit(solution)/shard_map/ppermute | solution.py:20
  24.2 7.1 %collective-permute-start.14 = (bf16[160,1024]{1,0:T(8,128)(2,1)S(1)}, bf16[160,1024]{1,0:T(8,128)(2,1)S(1)}, u32[]{:S(2)}, u32[]{:S(2)}) collective-permute-start(bf16[160,1024]{1,0:T(8,128)(2,1)S(1)} %get-tuple-element.34), channel_id=1, source_target_pairs={{0,8},{1,17},{2,10},{3,19},{4,12},{5,21},{6,14},{7,23},{8,0},{9,25... | collective-permute-start | bytes 983048 | tf_op jit(solution)/shard_map/ppermute | solution.py:27
  26.8 9.5 %collective-permute-start.13 = (bf16[160,1024]{1,0:T(8,128)(2,1)S(1)}, bf16[160,1024]{1,0:T(8,128)(2,1)S(1)}, u32[]{:S(2)}, u32[]{:S(2)}) collective-permute-start(bf16[160,1024]{1,0:T(8,128)(2,1)S(1)} %get-tuple-element.32), channel_id=1, source_target_pairs={{0,8},{1,17},{2,10},{3,19},{4,12},{5,21},{6,14},{7,23},{8,0},{9,25... | collective-permute-start | bytes 983048 | tf_op jit(solution)/shard_map/ppermute | solution.py:27
  31.4 7.1 %collective-permute-start.15 = (bf16[160,1024]{1,0:T(8,128)(2,1)S(1)}, bf16[160,1024]{1,0:T(8,128)(2,1)S(1)}, u32[]{:S(2)}, u32[]{:S(2)}) collective-permute-start(bf16[160,1024]{1,0:T(8,128)(2,1)S(1)} %shard_map.60), channel_id=1, source_target_pairs={{0,16},{1,9},{2,18},{3,11},{4,20},{5,13},{6,22},{7,15},{8,24},{9,1... | collective-permute-start | bytes 983048 | tf_op jit(solution)/shard_map/ppermute | solution.py:27

commit v5 on v4

--- a/solution.py
+++ b/solution.py
@@ -13,6 +13,7 @@
 ROOMY = 42
 STRIPE = 256
 FETCHES = 8
+PARTS = 2
 EXP2_SCALE = D_HEAD ** (-0.5) * math.log2(math.e)
 
 
@@ -147,7 +148,7 @@
 
 def early_kernel(n_chunk, kpos_ref, qpos_ref, q_ref, *refs):
     kv_refs, out = refs[:n_chunk], refs[n_chunk:]
-    n_keys = kv_refs[0].shape[0] * n_chunk
+    n_keys = sum(ref.shape[0] for ref in kv_refs)
 
     def emit(at, peak, denom, mixed):
         for ref, value in zip(out, (peak, denom, mixed), strict=True):
@@ -158,7 +159,7 @@
 
 def early_attend(kpos, qpos, q_all, kv_chunks):
     n_chunk, (depth, columns) = len(kv_chunks), q_all.shape
-    n_keys = kv_chunks[0].shape[0] * n_chunk
+    n_keys = sum(chunk.shape[0] for chunk in kv_chunks)
     vmem = pl.BlockSpec(memory_space=pltpu.VMEM)
     line = jax.ShapeDtypeStruct((1, columns), jnp.float32)
     return pl.pallas_call(
@@ -177,9 +178,9 @@
 
 def attend_kernel(n_chunk, kpos_ref, qpos_ref, q_ref, *refs):
     kv_refs, state = refs[:n_chunk], refs[n_chunk : n_chunk + 3]
-    weight_ref, attn_ref, far_ref = refs[n_chunk + 3 :]
+    weight_ref, attn_ref, *far_refs = refs[n_chunk + 3 :]
     seg, width = attn_ref.shape
-    n_keys = kv_refs[0].shape[0] * n_chunk
+    n_keys = sum(ref.shape[0] for ref in kv_refs)
     rows = []
 
     def emit(at, peak, denom, mixed):
@@ -190,24 +191,24 @@
     heads = width // D_HEAD
     attn = jnp.concatenate([rows[h * seg : (h + 1) * seg] for h in range(heads)], axis=1)
     attn_ref[...] = attn
-    far_ref[...] = project(attn, weight_ref, 3, far_ref.shape[1])
+    split_rows(project(attn, weight_ref, 3, far_refs[0].shape[1]), far_refs)
 
 
 def attend(kpos, qpos, q_all, kv_chunks, state, weight, n_head):
     n_chunk, (depth, columns) = len(kv_chunks), q_all.shape
     width, out_width = weight.shape
     seg = columns * depth // width
-    n_keys = kv_chunks[0].shape[0] * n_chunk
+    n_keys = sum(chunk.shape[0] for chunk in kv_chunks)
     cols = out_width // n_head
     vmem = pl.BlockSpec(memory_space=pltpu.VMEM)
     return pl.pallas_call(
         functools.partial(attend_kernel, n_chunk),
         out_shape=(
             jax.ShapeDtypeStruct((seg, width), jnp.bfloat16),
-            jax.ShapeDtypeStruct((seg, cols), jnp.bfloat16),
+            *(jax.ShapeDtypeStruct((seg // PARTS, cols), jnp.bfloat16),) * PARTS,
         ),
         in_specs=[vmem] * (7 + n_chunk),
-        out_specs=(vmem, vmem),
+        out_specs=(vmem,) * (1 + PARTS),
         compiler_params=pltpu.CompilerParams(vmem_limit_bytes=28 * 1024 * 1024),
         cost_estimate=pl.CostEstimate(
             flops=4 * columns * depth * n_keys + 2 * seg * width * cols,
@@ -217,44 +218,59 @@
     )(kpos, qpos, q_all, *kv_chunks, *state, weight)
 
 
-def near_kernel(attn_ref, weight_ref, first_ref, second_ref):
-    flip = first_flip()
-    first_ref[...] = project(attn_ref[...], weight_ref, flip, first_ref.shape[1])
-    second_ref[...] = project(attn_ref[...], weight_ref, 3 - flip, first_ref.shape[1])
+def split_rows(block, refs):
+    rows = refs[0].shape[0]
+    for i, ref in enumerate(refs):
+        ref[...] = block[i * rows : (i + 1) * rows]
+
+
+def near_kernel(attn_ref, weight_ref, first_ref, *second_refs):
+    flip, cols = first_flip(), first_ref.shape[1]
+    first_ref[...] = project(attn_ref[...], weight_ref, flip, cols)
+    split_rows(project(attn_ref[...], weight_ref, 3 - flip, cols), second_refs)
 
 
 def own_kernel(attn_ref, weight_ref, out_ref):
     out_ref[...] = project(attn_ref[...], weight_ref, 0, out_ref.shape[1])
 
 
-def project_rest(kernel, n, attn, weight, n_head):
+def project_rest(kernel, out_rows, attn, weight, n_head):
     seg, width = attn.shape
     cols = weight.shape[1] // n_head
     vmem = pl.BlockSpec(memory_space=pltpu.VMEM)
     return pl.pallas_call(
         kernel,
-        out_shape=(jax.ShapeDtypeStruct((seg, cols), jnp.bfloat16),) * n,
+        out_shape=tuple(jax.ShapeDtypeStruct((rows, cols), jnp.bfloat16) for rows in out_rows),
         in_specs=[vmem, vmem],
-        out_specs=(vmem,) * n,
+        out_specs=(vmem,) * len(out_rows),
         compiler_params=pltpu.CompilerParams(vmem_limit_bytes=20 * 1024 * 1024),
         cost_estimate=pl.CostEstimate(
-            flops=2 * seg * width * cols * n,
-            bytes_accessed=2 * width * cols * n,
+            flops=2 * sum(out_rows) * width * cols,
+            bytes_accessed=2 * width * cols,
             transcendentals=0,
         ),
     )(attn, weight)
 
 
-def sum_kernel(*refs):
-    total = sum(ref[...].astype(jnp.float32) for ref in refs[:-1])
-    refs[-1][...] = total.astype(jnp.bfloat16)
-
-
-def sum_blocks(*blocks):
+def sum_kernel(mine_ref, theirs_ref, out_ref):
+    total = mine_ref[...].astype(jnp.float32) + theirs_ref[...].astype(jnp.float32)
+    out_ref[...] = total.astype(jnp.bfloat16)
+
+
+def final_kernel(kept_ref, received_ref, *refs):
+    out_ref = refs[-1]
+    rows = refs[0].shape[0]
+    for i, ref in enumerate(refs[:-1]):
+        at = slice(i * rows, (i + 1) * rows)
+        total = kept_ref[at].astype(jnp.float32) + received_ref[at].astype(jnp.float32)
+        out_ref[at] = (total + ref[...].astype(jnp.float32)).astype(jnp.bfloat16)
+
+
+def sum_blocks(kernel, *blocks):
     vmem = pl.BlockSpec(memory_space=pltpu.VMEM)
     size = blocks[0].size * len(blocks)
     return pl.pallas_call(
-        sum_kernel,
+        kernel,
         out_shape=jax.ShapeDtypeStruct(blocks[0].shape, jnp.bfloat16),
         in_specs=[vmem] * len(blocks),
         out_specs=vmem,
@@ -278,6 +294,7 @@
     own = jnp.concatenate(kv_in, axis=0)
     q_in = [q_cut[0]] + [swap(q_cut[k], "head", k, n_head) for k in range(1, n_head)]
     flips = [2 * dz for dz in range(n_ctx // 2)]
+    seg = own.shape[0]
     chunk_flips = tuple(flips + [f ^ 1 for f in flips])
     weight, qpos, kpos, q_all = prepare(
         stretch_order, out_weight, own, q_in, chunk_flips, own.shape[0] * n_ctx
@@ -285,15 +302,19 @@
     far_keys = [swap(own, "ctx", f, n_ctx) for f in flips[1:]]
     far_keys, kpos = lax.optimization_barrier((far_keys, kpos))
     same_core = [own] + far_keys
-    other_core = [swap(x, "ctx", 1, n_ctx) for x in same_core]
+    other_core = [swap(own, "ctx", 1, n_ctx), swap(jnp.concatenate(far_keys, axis=0), "ctx", 1, n_ctx)]
     state = early_attend(kpos, qpos, q_all, same_core)
-    attn, far = attend(kpos, qpos, q_all, other_core, state, weight, n_head)
-    passed = swap_by_core(far, (1, 2), n_head, n_ctx)
-    first, second = project_rest(near_kernel, 2, attn, weight, n_head)
+    attn, *far = attend(kpos, qpos, q_all, other_core, state, weight, n_head)
+    passed = [swap_by_core(x, (1, 2), n_head, n_ctx) for x in far]
+    half = seg // PARTS
+    first, *second = project_rest(near_kernel, (seg,) + (half,) * PARTS, attn, weight, n_head)
     received = swap_by_core(first, (1, 2), n_head, n_ctx)
-    (kept,) = project_rest(own_kernel, 1, attn, weight, n_head)
-    joined = swap_by_core(sum_blocks(second, passed), (2, 1), n_head, n_ctx)
-    return sum_blocks(kept, received, joined)
+    (kept,) = project_rest(own_kernel, (seg,), attn, weight, n_head)
+    joined = [
+        swap_by_core(sum_blocks(sum_kernel, mine, theirs), (2, 1), n_head, n_ctx)
+        for mine, theirs in zip(second, passed, strict=True)
+    ]
+    return sum_blocks(final_kernel, kept, received, *joined)
 
 
 def attend_block(state, query_heads, query_pos, key_block, value_block, key_pos):

time: 39.6 us -> 38.9 us (0.982)
  waiting for transfers between devices: 9.18 us -> 5.82 us
  starting transfers between devices: 17.7 us -> 20.2 us
    ppermute x3 -> x5, waiting for transfers between devices: 8.97 us -> 5.62 us  [swap_by_core(): return lax.ppermute(x, ('head', 'ctx'), pairs)]
    ppermute x3 -> x5, starting transfers between devices: 3.88 us -> 6.79 us  [swap_by_core(): return lax.ppermute(x, ('head', 'ctx'), pairs)]
    ppermute x13 -> x11, starting transfers between devices: 13.8 us -> 13.4 us  [swap(): return lax.ppermute(x, axis, [(i, i ^ flip) for i in range(size)])]
    pallas_call x4 -> x5, Pallas kernels: 2.33 us -> 2.34 us  [the longest x2 1.42 us: project_rest(): pl.pallas_call(kernel, out_shape=tuple((jax.ShapeDtypeStruct((rows, cols)...]
  transfers between devices with their start and end apart: 16 -> 16, of which waited for: 4 -> 6; matrix products, arithmetic and copies ran while one was open for 3% -> 3% of each run, Pallas kernels for 18% -> 18%
where the time goes in v5:
time: 38.9 us; the launch traced here: 38.6 us
  starting transfers between devices  20.2 us (52%)
  Pallas kernels  9.93 us (26%)
  waiting for transfers between devices  5.82 us (15%)
  local copies, waits for them, and re-layouts  2.51 us (6%)
    ppermute x11, starting transfers between devices, swap(): return lax.ppermute(x, axis, [(i, i ^ flip) for i in range(size)])  13.4 us
    ppermute x5, starting transfers between devices, swap_by_core(): return lax.ppermute(x, ('head', 'ctx'), pairs)  6.79 us
    ppermute x5, waiting for transfers between devices, swap_by_core(): return lax.ppermute(x, ('head', 'ctx'), pairs)  5.62 us
    pallas_call x1, Pallas kernels, prepare(): pl.pallas_call(functools.partial(prepare_kernel, span, n_head, chunk_flip...  4.11 us
    pallas_call x1, Pallas kernels, attend(): pl.pallas_call(functools.partial(attend_kernel, n_chunk), out_shape=(jax....  1.99 us
    dynamic_slice x2, local copies, waits for them, and re-layouts, cut(): return lax.dynamic_slice_in_dim(x[0], (me ^ k) * width, width, 1)  1.86 us
    pallas_call x1, Pallas kernels, early_attend(): pl.pallas_call(functools.partial(early_kernel, n_chunk), out_shape=(line,...  1.49 us
    pallas_call x2, Pallas kernels, project_rest(): pl.pallas_call(kernel, out_shape=tuple((jax.ShapeDtypeStruct((rows, cols)...  1.42 us
  transfers between devices with their start and end apart: 16, of which 6 were waited for; matrix products, arithmetic and copies ran while one was open for 3% of the time, Pallas kernels for 18%

profile of v5, /device:TPU:0, one launch (start us, length us, event | category | flops | bytes accessed | tf_op | source)
XLA Modules:
  0.0 38.6 jit_solution(10296562562473524650)
XLA Ops:
  0.0 0.8 %dynamic-slice_bitcast_fusion.10 = (bf16[40,128]{1,0:T(8,128)(2,1)S(1)}, bf16[40,128]{1,0:T(8,128)(2,1)S(1)}, bf16[40,128]{1,0:T(8,128)(2,1)S(1)}, bf16[40,128]{...) fusion(bf16[1,40,512]{2,1,0:T(8,128)(2,1)} %param.7, ...), kind=kLoop, calls=%fused_computation.15 | loop fusion | bytes 163856 | tf_op jit(solution)/shard_map/dynamic_slice | solution.py:287
  0.8 3.0 %collective-permute-start.1 = (bf16[40,256]{1,0:T(8,128)(2,1)S(1)}, bf16[40,256]{1,0:T(8,128)(2,1)S(1)}, u32[]{:S(2)}, u32[]{:S(2)}) collective-permute-start(bf16[40,256]{1,0:T(8,128)(2,1)S(1)} %pad_maximum_fusion.3), channel_id=1, source_target_pairs={{0,16},{8,24},{16,0},{24,8},{1,17},{9,25},{17,1},{25,9},{2,18},{10... | collective-permute-start | bytes 61448 | tf_op jit(solution)/shard_map/ppermute | solution.py:21
  3.9 1.4 %collective-permute-start.2 = (bf16[40,256]{1,0:T(8,128)(2,1)S(1)}, bf16[40,256]{1,0:T(8,128)(2,1)S(1)}, u32[]{:S(2)}, u32[]{:S(2)}) collective-permute-start(bf16[40,256]{1,0:T(8,128)(2,1)S(1)} %pad_maximum_fusion.4), channel_id=1, source_target_pairs={{0,24},{8,16},{16,8},{24,0},{1,25},{9,17},{17,9},{25,1},{2,26},{10... | collective-permute-start | bytes 61448 | tf_op jit(solution)/shard_map/ppermute | solution.py:21
  5.3 0.1 collective-permute-start
  5.5 1.0 %dynamic-slice_bitcast_fusion = (bf16[40,1024]{1,0:T(8,128)(2,1)S(1)}, bf16[40,1024]{1,0:T(8,128)(2,1)S(1)}, bf16[40,1024]{1,0:T(8,128)(2,1)S(1)}, bf16[40,1024]{1,0:T(8,128)(2,1)S(1)}) fusion(bf16[1,40,4096]{2,1,0:T(8,128)(2,1)} %param.5, s32[]{:T(128)S(6)} %select_n.35, s32[]{:T(128)S(6)} %select_n.33, s32[]{:T(128)S(6)} %select_n.32, s32[]{:T(128)S(6)} %select_n.34), kind=kLoop, calls=%fused_computation.2 | loop fusion | bytes 655376 | tf_op jit(solution)/shard_map/dynamic_slice | solution.py:287
  6.5 2.9 %collective-permute-start.8 = (bf16[40,1024]{1,0:T(8,128)(2,1)S(1)}, bf16[40,1024]{1,0:T(8,128)(2,1)S(1)}, u32[]{:S(2)}, u32[]{:S(2)}) collective-permute-start(bf16[40,1024]{1,0:T(8,128)(2,1)S(1)} %get-tuple-element.39), channel_id=1, source_target_pairs={{0,24},{8,16},{16,8},{24,0},{1,25},{9,17},{17,9},{25,1},{2,26},{10... | collective-permute-start | bytes 245768 | tf_op jit(solution)/shard_map/ppermute | solution.py:21
  9.4 0.5 %collective-permute-start.6 = (bf16[40,1024]{1,0:T(8,128)(2,1)S(1)}, bf16[40,1024]{1,0:T(8,128)(2,1)S(1)}, u32[]{:S(2)}, u32[]{:S(2)}) collective-permute-start(bf16[40,1024]{1,0:T(8,128)(2,1)S(1)} %get-tuple-element.40), channel_id=1, source_target_pairs={{0,8},{8,0},{16,24},{24,16},{1,9},{9,1},{17,25},{25,17},{2,10},{10... | collective-permute-start | bytes 245768 | tf_op jit(solution)/shard_map/ppermute | solution.py:21
  9.9 0.1 collective-permute-start.7
  10.0 0.0 collective-permute-done.2
  10.1 0.0 collective-permute-done
  10.1 4.1 %collective-permute-start.5 = (bf16[160,256]{1,0:T(8,128)(2,1)S(1)}, bf16[160,256]{1,0:T(8,128)(2,1)S(1)}, u32[]{:S(2)}, u32[]{:S(2)}) collective-permute-start(bf16[160,256]{1,0:T(8,128)(2,1)S(1)} %pad_maximum_fusion.1.after_ref.refs_0_), channel_id=1, source_target_pairs={{0,6},{1,7},{2,4},{3,5},{4,2},{5,3},{6,0},{7,1},{8,14},{9,15},{10,... | collective-permute-start | bytes 245768 | tf_op jit(solution)/shard_map/ppermute | solution.py:21
  14.1 0.6 %collective-permute-start.3 = (bf16[160,256]{1,0:T(8,128)(2,1)S(1)}, bf16[160,256]{1,0:T(8,128)(2,1)S(1)}, u32[]{:S(2)}, u32[]{:S(2)}) collective-permute-start(bf16[160,256]{1,0:T(8,128)(2,1)S(1)} %pad_maximum_fusion.1.after_ref.refs_0_), channel_id=1, source_target_pairs={{0,2},{1,3},{2,0},{3,1},{4,6},{5,7},{6,4},{7,5},{8,10},{9,11},{10,... | collective-permute-start | bytes 245768 | tf_op jit(solution)/shard_map/ppermute | solution.py:21
  14.8 0.7 %copy-done = s32[32]{0:T(128)S(1)} copy-done((s32[32]{0:T(128)S(1)}, s32[32]{0:T(128)}, u32[]{:S(2)}) %copy-start) | copy-done | bytes 152
  15.4 4.1 %shard_map.55 = (bf16[1024,4096]{1,0:T(8,128)(2,1)S(1)}, s32[1,1280]{1,0:T(1,128)S(1)}, s32[1280,128]{1,0:T(8,128)S(1)}, bf16[128,1280]{1,0:T(8,128)(2,1)S(1)}) custom-call(s32[32]{0:T(128)S(1)} %copy-done, bf16[1024,4096]{1,0:T(8,128)(2,1)} %weight_ref.1, bf16[160,256]{1,0:T(8,128)(2,1)S(1)} %pad_maximum_fusion.1.after_ref.refs_0_, ...), custom_call_target="tpu_custom_call" | custom-call | bytes 4194304 | tf_op jit(solution)/shard_map/pallas_call | solution.py:84
  19.6 0.2 collective-permute-done.4.refs_2_
  19.8 0.1 collective-permute-start.10
  19.9 0.5 %collective-permute-start.9 = (bf16[160,256]{1,0:T(8,128)(2,1)S(1)}, bf16[160,256]{1,0:T(8,128)(2,1)S(1)}, u32[]{:S(2)}, u32[]{:S(2)}) collective-permute-start(bf16[160,256]{1,0:T(8,128)(2,1)S(1)} %pad_maximum_fusion.1.after_ref.refs_0_), channel_id=1, source_target_pairs={{0,1},{1,0},{2,3},{3,2},{4,5},{5,4},{6,7},{7,6},{8,9},{9,8},{10,11... | collective-permute-start | bytes 245768 | tf_op jit(solution)/shard_map/ppermute | solution.py:21
  20.4 1.5 %shard_map.56 = (f32[1,1280]{1,0:T(1,128)S(1)}, f32[1,1280]{1,0:T(1,128)S(1)}, f32[128,1280]{1,0:T(8,128)S(1)}) custom-call(s32[1280,128]{1,0:T(8,128)S(1)} %get-tuple-element.23.kpos_ref, s32[1,1280]{1,0:T(1,128)S(1)} %get-tuple-element.24.qpos_ref, bf16[128,1280]{1,0:T(8,128)(2,1)S(1)} %get-tuple-element.25.q_ref, ...), custom_call_target="tpu_custom_call" | custom-call | flops 419430400 | bytes 4194304 | tf_op jit(solution)/shard_map/pallas_call | solution.py:165
  21.9 2.0 %shard_map.57 = (bf16[160,1024]{1,0:T(8,128)(2,1)S(1)}, bf16[80,1024]{1,0:T(8,128)(2,1)S(1)}, bf16[80,1024]{1,0:T(8,128)(2,1)S(1)}) custom-call(s32[1280,128]{1,0:T(8,128)S(1)} %get-tuple-element.23.kpos_ref, s32[1,1280]{1,0:T(1,128)S(1)} %get-tuple-element.24.qpos_ref, bf16[128,1280]{1,0:T(8,128)(2,1)S(1)} %get-tuple-element.25.q_ref, ...), custom_call_target="tpu_custom_call" | custom-call | flops 754974720 | bytes 4194304 | tf_op jit(solution)/shard_map/pallas_call | solution.py:204
  23.9 1.5 %collective-permute-start.12 = (bf16[80,1024]{1,0:T(8,128)(2,1)S(1)}, bf16[80,1024]{1,0:T(8,128)(2,1)S(1)}, u32[]{:S(2)}, u32[]{:S(2)}) collective-permute-start(bf16[80,1024]{1,0:T(8,128)(2,1)S(1)} %get-tuple-element.36), channel_id=1, source_target_pairs={{0,8},{1,17},{2,10},{3,19},{4,12},{5,21},{6,14},{7,23},{8,0},{9,25... | collective-permute-start | bytes 491528 | tf_op jit(solution)/shard_map/ppermute | solution.py:28
  25.4 0.5 %collective-permute-start.14 = (bf16[80,1024]{1,0:T(8,128)(2,1)S(1)}, bf16[80,1024]{1,0:T(8,128)(2,1)S(1)}, u32[]{:S(2)}, u32[]{:S(2)}) collective-permute-start(bf16[80,1024]{1,0:T(8,128)(2,1)S(1)} %get-tuple-element.38), channel_id=1, source_target_pairs={{0,8},{1,17},{2,10},{3,19},{4,12},{5,21},{6,14},{7,23},{8,0},{9,25... | collective-permute-start | bytes 491528 | tf_op jit(solution)/shard_map/ppermute | solution.py:28
  26.0 0.9 %shard_map.59 = (bf16[160,1024]{1,0:T(8,128)(2,1)S(1)}, bf16[80,1024]{1,0:T(8,128)(2,1)S(1)}, bf16[80,1024]{1,0:T(8,128)(2,1)S(1)}) custom-call(bf16[160,1024]{1,0:T(8,128)(2,1)S(1)} %get-tuple-element.33.attn_ref, bf16[1024,4096]{1,0:T(8,128)(2,1)S(1)} %get-tuple-element.32.refs_5_.weight_ref), custom_call_target="tpu_custom_call" | custom-call | flops 671088640 | bytes 2097152 | tf_op jit(solution)/shard_map/pallas_call | solution.py:241
  26.9 1.5 %collective-permute-start.11 = (bf16[160,1024]{1,0:T(8,128)(2,1)S(1)}, bf16[160,1024]{1,0:T(8,128)(2,1)S(1)}, u32[]{:S(2)}, u32[]{:S(2)}) collective-permute-start(bf16[160,1024]{1,0:T(8,128)(2,1)S(1)} %get-tuple-element.34), channel_id=1, source_target_pairs={{0,8},{1,17},{2,10},{3,19},{4,12},{5,21},{6,14},{7,23},{8,0},{9,25... | collective-permute-start | bytes 983048 | tf_op jit(solution)/shard_map/ppermute | solution.py:28
  28.4 0.9 %collective-permute-done.12.theirs_ref = bf16[80,1024]{1,0:T(8,128)(2,1)S(1)} collective-permute-done((bf16[80,1024]{1,0:T(8,128)(2,1)S(1)}, bf16[80,1024]{1,0:T(8,128)(2,1)S(1)}, u32[]{:S(2)}, u32[]{:S(2)}) %collective-permute-start.12) | collective-permute-done | bytes 163872 | tf_op jit(solution)/shard_map/ppermute | solution.py:28
  29.3 1.6 %collective-permute-start.13 = (bf16[80,1024]{1,0:T(8,128)(2,1)S(1)}, bf16[80,1024]{1,0:T(8,128)(2,1)S(1)}, u32[]{:S(2)}, u32[]{:S(2)}) collective-permute-start(bf16[80,1024]{1,0:T(8,128)(2,1)S(1)} %shard_map.60), channel_id=1, source_target_pairs={{0,16},{1,9},{2,18},{3,11},{4,20},{5,13},{6,22},{7,15},{8,24},{9,1... | collective-permute-start | bytes 491528 | tf_op jit(solution)/shard_map/ppermute | solution.py:28
  30.9 0.1 collective-permute-done.14.theirs_ref
  31.1 1.6 %collective-permute-start.15 = (bf16[80,1024]{1,0:T(8,128)(2,1)S(1)}, bf16[80,1024]{1,0:T(8,128)(2,1)S(1)}, u32[]{:S(2)}, u32[]{:S(2)}) collective-permute-start(bf16[80,1024]{1,0:T(8,128)(2,1)S(1)} %shard_map.61), channel_id=1, source_target_pairs={{0,16},{1,9},{2,18},{3,11},{4,20},{5,13},{6,22},{7,15},{8,24},{9,1... | collective-permute-start | bytes 491528 | tf_op jit(solution)/shard_map/ppermute | solution.py:28
  32.6 0.5 %shard_map.58.kept_ref = bf16[160,1024]{1,0:T(8,128)(2,1)S(1)} custom-call(bf16[160,1024]{1,0:T(8,128)(2,1)S(1)} %get-tuple-element.33.attn_ref, bf16[1024,4096]{1,0:T(8,128)(2,1)S(1)} %get-tuple-element.32.refs_5_.weight_ref), custom_call_target="tpu_custom_call" | custom-call | flops 335544320 | bytes 2097152 | tf_op jit(solution)/shard_map/pallas_call | solution.py:241
  33.2 2.2 %collective-permute-done.13.refs_0_ = bf16[80,1024]{1,0:T(8,128)(2,1)S(1)} collective-permute-done((bf16[80,1024]{1,0:T(8,128)(2,1)S(1)}, bf16[80,1024]{1,0:T(8,128)(2,1)S(1)}, u32[]{:S(2)}, u32[]{:S(2)}) %collective-permute-start.13) | collective-permute-done | bytes 163872 | tf_op jit(solution)/shard_map/ppermute | solution.py:28
  35.4 1.8 %collective-permute-done.15.refs_1_ = bf16[80,1024]{1,0:T(8,128)(2,1)S(1)} collective-permute-done((bf16[80,1024]{1,0:T(8,128)(2,1)S(1)}, bf16[80,1024]{1,0:T(8,128)(2,1)S(1)}, u32[]{:S(2)}, u32[]{:S(2)}) %collective-permute-start.15) | collective-permute-done | bytes 163872 | tf_op jit(solution)/shard_map/ppermute | solution.py:28
  37.1 0.7 %collective-permute-done.11.received_ref = bf16[160,1024]{1,0:T(8,128)(2,1)S(1)} collective-permute-done((bf16[160,1024]{1,0:T(8,128)(2,1)S(1)}, bf16[160,1024]{1,0:T(8,128)(2,1)S(1)}, u32[]{:S(2)}, u32[]{:S(2)}) %collective-permute-start.11) | collective-permute-done | bytes 327712 | tf_op jit(solution)/shard_map/ppermute | solution.py:28
  37.8 0.8 %shard_map.62 = bf16[160,1024]{1,0:T(8,128)(2,1)} custom-call(bf16[160,1024]{1,0:T(8,128)(2,1)S(1)} %shard_map.58.kept_ref, bf16[160,1024]{1,0:T(8,128)(2,1)S(1)} %collective-permute-done.11.received_ref, bf16[80,1024]{1,0:T(8,128)(2,1)S(1)} %collective-permute-done.13.refs_0_, bf16[80,1024]{1,0:T(8,128)(2,1)S(1)} %collective-permute-done.15.refs_1_), custom_call_target="tpu_custom_call" | custom-call | flops 655360 | bytes 1310720 | tf_op jit(solution)/shard_map/pallas_call | solution.py:272
  (17 shorter events, 0.1 us)
Async XLA Ops:
  0.8 9.1 %collective-permute-start.1 = (bf16[40,256]{1,0:T(8,128)(2,1)S(1)}, bf16[40,256]{1,0:T(8,128)(2,1)S(1)}, u32[]{:S(2)}, u32[]{:S(2)}) collective-permute-start(bf16[40,256]{1,0:T(8,128)(2,1)S(1)} %pad_maximum_fusion.3), channel_id=1, source_target_pairs={{0,16},{8,24},{16,0},{24,8},{1,17},{9,25},{17,1},{25,9},{2,18},{10... | collective-permute-start | bytes 61448 | tf_op jit(solution)/shard_map/ppermute | solution.py:21
  3.9 6.2 %collective-permute-start.2 = (bf16[40,256]{1,0:T(8,128)(2,1)S(1)}, bf16[40,256]{1,0:T(8,128)(2,1)S(1)}, u32[]{:S(2)}, u32[]{:S(2)}) collective-permute-start(bf16[40,256]{1,0:T(8,128)(2,1)S(1)} %pad_maximum_fusion.4), channel_id=1, source_target_pairs={{0,24},{8,16},{16,8},{24,0},{1,25},{9,17},{17,9},{25,1},{2,26},{10... | collective-permute-start | bytes 61448 | tf_op jit(solution)/shard_map/ppermute | solution.py:21
  5.3 4.7 %collective-permute-start = (bf16[40,256]{1,0:T(8,128)(2,1)S(1)}, bf16[40,256]{1,0:T(8,128)(2,1)S(1)}, u32[]{:S(2)}, u32[]{:S(2)}) collective-permute-start(bf16[40,256]{1,0:T(8,128)(2,1)S(1)} %pad_maximum_fusion.2), channel_id=1, source_target_pairs={{0,8},{8,0},{16,24},{24,16},{1,9},{9,1},{17,25},{25,17},{2,10},{10... | collective-permute-start | bytes 61448 | tf_op jit(solution)/shard_map/ppermute | solution.py:21
  6.5 7.7 %collective-permute-start.8 = (bf16[40,1024]{1,0:T(8,128)(2,1)S(1)}, bf16[40,1024]{1,0:T(8,128)(2,1)S(1)}, u32[]{:S(2)}, u32[]{:S(2)}) collective-permute-start(bf16[40,1024]{1,0:T(8,128)(2,1)S(1)} %get-tuple-element.39), channel_id=1, source_target_pairs={{0,24},{8,16},{16,8},{24,0},{1,25},{9,17},{17,9},{25,1},{2,26},{10... | collective-permute-start | bytes 245768 | tf_op jit(solution)/shard_map/ppermute | solution.py:21
  9.4 5.4 %collective-permute-start.6 = (bf16[40,1024]{1,0:T(8,128)(2,1)S(1)}, bf16[40,1024]{1,0:T(8,128)(2,1)S(1)}, u32[]{:S(2)}, u32[]{:S(2)}) collective-permute-start(bf16[40,1024]{1,0:T(8,128)(2,1)S(1)} %get-tuple-element.40), channel_id=1, source_target_pairs={{0,8},{8,0},{16,24},{24,16},{1,9},{9,1},{17,25},{25,17},{2,10},{10... | collective-permute-start | bytes 245768 | tf_op jit(solution)/shard_map/ppermute | solution.py:21
  9.9 4.8 %collective-permute-start.7 = (bf16[40,1024]{1,0:T(8,128)(2,1)S(1)}, bf16[40,1024]{1,0:T(8,128)(2,1)S(1)}, u32[]{:S(2)}, u32[]{:S(2)}) collective-permute-start(bf16[40,1024]{1,0:T(8,128)(2,1)S(1)} %get-tuple-element.42), channel_id=1, source_target_pairs={{0,16},{8,24},{16,0},{24,8},{1,17},{9,25},{17,1},{25,9},{2,18},{10... | collective-permute-start | bytes 245768 | tf_op jit(solution)/shard_map/ppermute | solution.py:21
  10.1 9.5 %collective-permute-start.5 = (bf16[160,256]{1,0:T(8,128)(2,1)S(1)}, bf16[160,256]{1,0:T(8,128)(2,1)S(1)}, u32[]{:S(2)}, u32[]{:S(2)}) collective-permute-start(bf16[160,256]{1,0:T(8,128)(2,1)S(1)} %pad_maximum_fusion.1.after_ref.refs_0_), channel_id=1, source_target_pairs={{0,6},{1,7},{2,4},{3,5},{4,2},{5,3},{6,0},{7,1},{8,14},{9,15},{10,... | collective-permute-start | bytes 245768 | tf_op jit(solution)/shard_map/ppermute | solution.py:21
  14.1 5.6 %collective-permute-start.4 = (bf16[160,256]{1,0:T(8,128)(2,1)S(1)}, bf16[160,256]{1,0:T(8,128)(2,1)S(1)}, u32[]{:S(2)}, u32[]{:S(2)}) collective-permute-start(bf16[160,256]{1,0:T(8,128)(2,1)S(1)} %pad_maximum_fusion.1.after_ref.refs_0_), channel_id=1, source_target_pairs={{0,4},{1,5},{2,6},{3,7},{4,0},{5,1},{6,2},{7,3},{8,12},{9,13},{10,... | collective-permute-start | bytes 245768 | tf_op jit(solution)/shard_map/ppermute | solution.py:21
  14.1 5.6 %collective-permute-start.3 = (bf16[160,256]{1,0:T(8,128)(2,1)S(1)}, bf16[160,256]{1,0:T(8,128)(2,1)S(1)}, u32[]{:S(2)}, u32[]{:S(2)}) collective-permute-start(bf16[160,256]{1,0:T(8,128)(2,1)S(1)} %pad_maximum_fusion.1.after_ref.refs_0_), channel_id=1, source_target_pairs={{0,2},{1,3},{2,0},{3,1},{4,6},{5,7},{6,4},{7,5},{8,10},{9,11},{10,... | collective-permute-start | bytes 245768 | tf_op jit(solution)/shard_map/ppermute | solution.py:21
  14.8 0.7 %copy-start = (s32[32]{0:T(128)S(1)}, s32[32]{0:T(128)}, u32[]{:S(2)}) copy-start(s32[32]{0:T(128)} %order_ref.1) | copy-start | bytes 388
  19.8 2.1 %collective-permute-start.10 = (bf16[480,256]{1,0:T(8,128)(2,1)S(1)}, bf16[480,256]{1,0:T(8,128)(2,1)S(1)}, u32[]{:S(2)}, u32[]{:S(2)}) collective-permute-start(bf16[480,256]{1,0:T(8,128)(2,1)S(1)} %pad_maximum_fusion), channel_id=1, source_target_pairs={{0,1},{1,0},{2,3},{3,2},{4,5},{5,4},{6,7},{7,6},{8,9},{9,8},{10,11... | collective-permute-start | bytes 737288 | tf_op jit(solution)/shard_map/ppermute | solution.py:21
  19.9 2.0 %collective-permute-start.9 = (bf16[160,256]{1,0:T(8,128)(2,1)S(1)}, bf16[160,256]{1,0:T(8,128)(2,1)S(1)}, u32[]{:S(2)}, u32[]{:S(2)}) collective-permute-start(bf16[160,256]{1,0:T(8,128)(2,1)S(1)} %pad_maximum_fusion.1.after_ref.refs_0_), channel_id=1, source_target_pairs={{0,1},{1,0},{2,3},{3,2},{4,5},{5,4},{6,7},{7,6},{8,9},{9,8},{10,11... | collective-permute-start | bytes 245768 | tf_op jit(solution)/shard_map/ppermute | solution.py:21
  23.9 5.4 %collective-permute-start.12 = (bf16[80,1024]{1,0:T(8,128)(2,1)S(1)}, bf16[80,1024]{1,0:T(8,128)(2,1)S(1)}, u32[]{:S(2)}, u32[]{:S(2)}) collective-permute-start(bf16[80,1024]{1,0:T(8,128)(2,1)S(1)} %get-tuple-element.36), channel_id=1, source_target_pairs={{0,8},{1,17},{2,10},{3,19},{4,12},{5,21},{6,14},{7,23},{8,0},{9,25... | collective-permute-start | bytes 491528 | tf_op jit(solution)/shard_map/ppermute | solution.py:28
  25.4 5.6 %collective-permute-start.14 = (bf16[80,1024]{1,0:T(8,128)(2,1)S(1)}, bf16[80,1024]{1,0:T(8,128)(2,1)S(1)}, u32[]{:S(2)}, u32[]{:S(2)}) collective-permute-start(bf16[80,1024]{1,0:T(8,128)(2,1)S(1)} %get-tuple-element.38), channel_id=1, source_target_pairs={{0,8},{1,17},{2,10},{3,19},{4,12},{5,21},{6,14},{7,23},{8,0},{9,25... | collective-permute-start | bytes 491528 | tf_op jit(solution)/shard_map/ppermute | solution.py:28
  26.9 11.0 %collective-permute-start.11 = (bf16[160,1024]{1,0:T(8,128)(2,1)S(1)}, bf16[160,1024]{1,0:T(8,128)(2,1)S(1)}, u32[]{:S(2)}, u32[]{:S(2)}) collective-permute-start(bf16[160,1024]{1,0:T(8,128)(2,1)S(1)} %get-tuple-element.34), channel_id=1, source_target_pairs={{0,8},{1,17},{2,10},{3,19},{4,12},{5,21},{6,14},{7,23},{8,0},{9,25... | collective-permute-start | bytes 983048 | tf_op jit(solution)/shard_map/ppermute | solution.py:28
  29.3 6.1 %collective-permute-start.13 = (bf16[80,1024]{1,0:T(8,128)(2,1)S(1)}, bf16[80,1024]{1,0:T(8,128)(2,1)S(1)}, u32[]{:S(2)}, u32[]{:S(2)}) collective-permute-start(bf16[80,1024]{1,0:T(8,128)(2,1)S(1)} %shard_map.60), channel_id=1, source_target_pairs={{0,16},{1,9},{2,18},{3,11},{4,20},{5,13},{6,22},{7,15},{8,24},{9,1... | collective-permute-start | bytes 491528 | tf_op jit(solution)/shard_map/ppermute | solution.py:28
  31.1 6.1 %collective-permute-start.15 = (bf16[80,1024]{1,0:T(8,128)(2,1)S(1)}, bf16[80,1024]{1,0:T(8,128)(2,1)S(1)}, u32[]{:S(2)}, u32[]{:S(2)}) collective-permute-start(bf16[80,1024]{1,0:T(8,128)(2,1)S(1)} %shard_map.61), channel_id=1, source_target_pairs={{0,16},{1,9},{2,18},{3,11},{4,20},{5,13},{6,22},{7,15},{8,24},{9,1... | collective-permute-start | bytes 491528 | tf_op jit(solution)/shard_map/ppermute | solution.py:28

commit v6 on v5

--- a/solution.py
+++ b/solution.py
@@ -38,8 +38,10 @@
     return jnp.sum(jnp.where(hits, order[None, :], 0), axis=1) * span + flat_rows % span
 
 
-def prepare_kernel(span, n_head, chunk_flips, order_ref, weight_ref, after_ref, *refs):
-    q_refs, (weight_out, qpos_ref, kpos_ref, q_out, q_s, sems) = refs[:n_head], refs[n_head:]
+def prepare_kernel(span, n_head, chunk_flips, order_hbm, weight_ref, after_ref, *refs):
+    weight_out, qpos_ref, kpos_ref, sems, order_ref, order_sem = refs[-6:]
+    order_copy = pltpu.make_async_copy(order_hbm, order_ref, order_sem)
+    order_copy.start()
     me, ctx = lax.axis_index("head"), lax.axis_index("ctx")
     step = weight_ref.shape[0] // FETCHES
     fetches = [
@@ -54,32 +56,29 @@
         for fetch in fetches:
             fetch.start()
 
+    order_copy.wait()
     row = lax.broadcasted_iota(jnp.int32, (span, D_HEAD), 0)
     for i, flip in enumerate(chunk_flips):
         for k in range(n_head):
             first = (i * n_head + k) * span
             block = order_ref[(ctx ^ flip) * n_head + (me ^ k)]
             kpos_ref[first : first + span, :] = row + block * span
-    heads = q_refs[0].shape[1] // D_HEAD
+    heads = qpos_ref.shape[1] // (span * n_head)
     lane = lax.broadcasted_iota(jnp.int32, qpos_ref.shape, 1)
     qpos = lane
     for i in range(heads * n_head):
         block = order_ref[ctx * n_head + i % n_head]
         qpos = jnp.where(lane >= i * span, lane + (block - i) * span, qpos)
     qpos_ref[...] = qpos
-    for k in range(n_head):
-        at = pl.multiple_of((me ^ k) * span, span)
-        q_s[pl.ds(at, span), :] = q_refs[k][...].astype(jnp.float32)
-    stacked = jnp.concatenate([q_s[:, h * D_HEAD : (h + 1) * D_HEAD] for h in range(heads)], axis=0)
-    q_out[...] = stacked.T.astype(jnp.bfloat16)
     for fetch in fetches:
         fetch.wait()
 
 
-def prepare(order, weight, after, q_pieces, chunk_flips, n_keys):
+def prepare(order, weight, after, q_pieces, others, chunk_flips, n_keys):
     n_head = len(q_pieces)
     span, width = q_pieces[0].shape
     columns = span * n_head * width // D_HEAD
+    n_order = order.shape[0]
     vmem = pl.BlockSpec(memory_space=pltpu.VMEM)
     return pl.pallas_call(
         functools.partial(prepare_kernel, span, n_head, chunk_flips),
@@ -87,22 +86,50 @@
             jax.ShapeDtypeStruct(weight.shape, weight.dtype),
             jax.ShapeDtypeStruct((1, columns), jnp.int32),
             jax.ShapeDtypeStruct((n_keys, D_HEAD), jnp.int32),
-            jax.ShapeDtypeStruct((D_HEAD, columns), jnp.bfloat16),
         ),
         in_specs=[
-            pl.BlockSpec(memory_space=pltpu.SMEM),
+            pl.BlockSpec(memory_space=pltpu.HBM),
             pl.BlockSpec(memory_space=pltpu.HBM),
             pl.BlockSpec(memory_space=pl.ANY),
         ]
-        + [vmem] * n_head,
-        out_specs=(vmem,) * 4,
+        + [pl.BlockSpec(memory_space=pl.ANY)] * len(others),
+        out_specs=(vmem,) * 3,
         scratch_shapes=[
-            pltpu.VMEM((span * n_head, width), jnp.float32),
             pltpu.SemaphoreType.DMA((FETCHES,)),
+            pltpu.SMEM((n_order,), jnp.int32),
+            pltpu.SemaphoreType.DMA(()),
         ],
         compiler_params=pltpu.CompilerParams(vmem_limit_bytes=ROOMY * 1024 * 1024),
         cost_estimate=pl.CostEstimate(flops=0, bytes_accessed=4 * 1024 * 1024, transcendentals=0),
-    )(order, weight, after, *q_pieces)
+    )(order, weight, after, *others)
+
+
+def assemble_kernel(*refs):
+    q_refs, (q_out, q_s) = refs[:-2], refs[-2:]
+    me = lax.axis_index("head")
+    span, width = q_refs[0].shape
+    for k, q_ref in enumerate(q_refs):
+        at = pl.multiple_of((me ^ k) * span, span)
+        q_s[pl.ds(at, span), :] = q_ref[...].astype(jnp.float32)
+    heads = range(width // D_HEAD)
+    stacked = jnp.concatenate([q_s[:, h * D_HEAD : (h + 1) * D_HEAD] for h in heads], axis=0)
+    q_out[...] = stacked.T.astype(jnp.bfloat16)
+
+
+def assemble(q_pieces):
+    n_head = len(q_pieces)
+    span, width = q_pieces[0].shape
+    seg = span * n_head
+    vmem = pl.BlockSpec(memory_space=pltpu.VMEM)
+    return pl.pallas_call(
+        assemble_kernel,
+        out_shape=jax.ShapeDtypeStruct((D_HEAD, seg * width // D_HEAD), jnp.bfloat16),
+        in_specs=[vmem] * n_head,
+        out_specs=vmem,
+        scratch_shapes=[pltpu.VMEM((seg, width), jnp.float32)],
+        compiler_params=pltpu.CompilerParams(vmem_limit_bytes=8 * 1024 * 1024),
+        cost_estimate=pl.CostEstimate(flops=0, bytes_accessed=1024 * 1024, transcendentals=0),
+    )(*q_pieces)
 
 
 def project(attn, weight_ref, flip, cols):
@@ -296,13 +323,14 @@
     flips = [2 * dz for dz in range(n_ctx // 2)]
     seg = own.shape[0]
     chunk_flips = tuple(flips + [f ^ 1 for f in flips])
-    weight, qpos, kpos, q_all = prepare(
-        stretch_order, out_weight, own, q_in, chunk_flips, own.shape[0] * n_ctx
+    q_all = assemble(q_in)
+    weight, qpos, kpos = prepare(
+        stretch_order, out_weight, own, q_in, [q_in[k] for k in (2, 3)], chunk_flips, own.shape[0] * n_ctx
     )
     far_keys = [swap(own, "ctx", f, n_ctx) for f in flips[1:]]
     far_keys, kpos = lax.optimization_barrier((far_keys, kpos))
     same_core = [own] + far_keys
-    other_core = [swap(own, "ctx", 1, n_ctx), swap(jnp.concatenate(far_keys, axis=0), "ctx", 1, n_ctx)]
+    other_core = [swap(x, "ctx", 1, n_ctx) for x in (own, *far_keys)]
     state = early_attend(kpos, qpos, q_all, same_core)
     attn, *far = attend(kpos, qpos, q_all, other_core, state, weight, n_head)
     passed = [swap_by_core(x, (1, 2), n_head, n_ctx) for x in far]

time: 38.9 us -> 38.6 us (level)
  starting transfers between devices: 20.2 us -> 20.6 us
  Pallas kernels: 9.93 us -> 9.53 us
    ppermute x5, waiting for transfers between devices: 5.62 us -> 4.91 us  [swap_by_core(): return lax.ppermute(x, ('head', 'ctx'), pairs)]
    pallas_call x1, Pallas kernels: 4.11 us -> 3.48 us  [prepare(): pl.pallas_call(functools.partial(prepare_kernel, span, n_head, chunk_flip...]
    ppermute x5, starting transfers between devices: 6.79 us -> 7.24 us  [swap_by_core(): return lax.ppermute(x, ('head', 'ctx'), pairs)]
    ppermute x11 -> x13, starting transfers between devices: 13.4 us -> 13.4 us  [swap(): return lax.ppermute(x, axis, [(i, i ^ flip) for i in range(size)])]
  transfers between devices with their start and end apart: 16 -> 18, of which waited for: 6 -> 4; matrix products, arithmetic and copies ran while one was open for 3% -> 3% of each run, Pallas kernels for 18% -> 17%
where the time goes in v6:
time: 38.6 us; the launch traced here: 38.3 us
  starting transfers between devices  20.6 us (53%)
  Pallas kernels  9.53 us (25%)
  waiting for transfers between devices  5.5 us (14%)
  local copies, waits for them, and re-layouts  2.51 us (7%)
    ppermute x13, starting transfers between devices, swap(): return lax.ppermute(x, axis, [(i, i ^ flip) for i in range(size)])  13.4 us
    ppermute x5, starting transfers between devices, swap_by_core(): return lax.ppermute(x, ('head', 'ctx'), pairs)  7.24 us
    ppermute x5, waiting for transfers between devices, swap_by_core(): return lax.ppermute(x, ('head', 'ctx'), pairs)  4.91 us
    pallas_call x1, Pallas kernels, prepare(): pl.pallas_call(functools.partial(prepare_kernel, span, n_head, chunk_flip...  3.48 us
    pallas_call x1, Pallas kernels, attend(): pl.pallas_call(functools.partial(attend_kernel, n_chunk), out_shape=(jax....  1.99 us
    dynamic_slice x2, local copies, waits for them, and re-layouts, cut(): return lax.dynamic_slice_in_dim(x[0], (me ^ k) * width, width, 1)  1.86 us
    pallas_call x1, Pallas kernels, early_attend(): pl.pallas_call(functools.partial(early_kernel, n_chunk), out_shape=(line,...  1.5 us
    pallas_call x2, Pallas kernels, project_rest(): pl.pallas_call(kernel, out_shape=tuple((jax.ShapeDtypeStruct((rows, cols)...  1.41 us
  transfers between devices with their start and end apart: 18, of which 4 were waited for; matrix products, arithmetic and copies ran while one was open for 3% of the time, Pallas kernels for 17%

profile of v6, /device:TPU:0, one launch (start us, length us, event | category | flops | bytes accessed | tf_op | source)
XLA Modules:
  0.0 38.3 jit_solution(5912880795333662131)
XLA Ops:
  0.0 0.8 %dynamic-slice_bitcast_fusion.10 = (bf16[40,128]{1,0:T(8,128)(2,1)S(1)}, bf16[40,128]{1,0:T(8,128)(2,1)S(1)}, bf16[40,128]{1,0:T(8,128)(2,1)S(1)}, bf16[40,128]{...) fusion(bf16[1,40,512]{2,1,0:T(8,128)(2,1)} %param.7, ...), kind=kLoop, calls=%fused_computation.14 | loop fusion | bytes 163856 | tf_op jit(solution)/shard_map/dynamic_slice | solution.py:314
  0.8 3.0 %collective-permute-start.1 = (bf16[40,256]{1,0:T(8,128)(2,1)S(1)}, bf16[40,256]{1,0:T(8,128)(2,1)S(1)}, u32[]{:S(2)}, u32[]{:S(2)}) collective-permute-start(bf16[40,256]{1,0:T(8,128)(2,1)S(1)} %pad_maximum_fusion.2), channel_id=1, source_target_pairs={{0,16},{8,24},{16,0},{24,8},{1,17},{9,25},{17,1},{25,9},{2,18},{10... | collective-permute-start | bytes 61448 | tf_op jit(solution)/shard_map/ppermute | solution.py:21
  3.9 1.4 %collective-permute-start.2 = (bf16[40,256]{1,0:T(8,128)(2,1)S(1)}, bf16[40,256]{1,0:T(8,128)(2,1)S(1)}, u32[]{:S(2)}, u32[]{:S(2)}) collective-permute-start(bf16[40,256]{1,0:T(8,128)(2,1)S(1)} %pad_maximum_fusion.3), channel_id=1, source_target_pairs={{0,24},{8,16},{16,8},{24,0},{1,25},{9,17},{17,9},{25,1},{2,26},{10... | collective-permute-start | bytes 61448 | tf_op jit(solution)/shard_map/ppermute | solution.py:21
  5.3 0.1 collective-permute-start
  5.5 1.0 %dynamic-slice_bitcast_fusion = (bf16[40,1024]{1,0:T(8,128)(2,1)S(1)}, bf16[40,1024]{1,0:T(8,128)(2,1)S(1)}, bf16[40,1024]{1,0:T(8,128)(2,1)S(1)}, bf16[40,1024]{1,0:T(8,128)(2,1)S(1)}) fusion(bf16[1,40,4096]{2,1,0:T(8,128)(2,1)} %param.5, s32[]{:T(128)S(6)} %select_n.35, s32[]{:T(128)S(6)} %select_n.33, s32[]{:T(128)S(6)} %select_n.32, s32[]{:T(128)S(6)} %select_n.34), kind=kLoop, calls=%fused_computation.1 | loop fusion | bytes 655376 | tf_op jit(solution)/shard_map/dynamic_slice | solution.py:314
  6.5 2.9 %collective-permute-start.7 = (bf16[40,1024]{1,0:T(8,128)(2,1)S(1)}, bf16[40,1024]{1,0:T(8,128)(2,1)S(1)}, u32[]{:S(2)}, u32[]{:S(2)}) collective-permute-start(bf16[40,1024]{1,0:T(8,128)(2,1)S(1)} %get-tuple-element.38), channel_id=1, source_target_pairs={{0,24},{8,16},{16,8},{24,0},{1,25},{9,17},{17,9},{25,1},{2,26},{10... | collective-permute-start | bytes 245768 | tf_op jit(solution)/shard_map/ppermute | solution.py:21
  9.4 0.5 %collective-permute-start.6 = (bf16[40,1024]{1,0:T(8,128)(2,1)S(1)}, bf16[40,1024]{1,0:T(8,128)(2,1)S(1)}, u32[]{:S(2)}, u32[]{:S(2)}) collective-permute-start(bf16[40,1024]{1,0:T(8,128)(2,1)S(1)} %get-tuple-element.39), channel_id=1, source_target_pairs={{0,16},{8,24},{16,0},{24,8},{1,17},{9,25},{17,1},{25,9},{2,18},{10... | collective-permute-start | bytes 245768 | tf_op jit(solution)/shard_map/ppermute | solution.py:21
  9.9 0.0 collective-permute-done.1
  9.9 0.0 collective-permute-done.2
  9.9 3.7 %collective-permute-start.5 = (bf16[160,256]{1,0:T(8,128)(2,1)S(1)}, bf16[160,256]{1,0:T(8,128)(2,1)S(1)}, u32[]{:S(2)}, u32[]{:S(2)}) collective-permute-start(bf16[160,256]{1,0:T(8,128)(2,1)S(1)} %pad_maximum_fusion.after_ref.refs_0_), channel_id=1, source_target_pairs={{0,6},{1,7},{2,4},{3,5},{4,2},{5,3},{6,0},{7,1},{8,14},{9,15},{10,... | collective-permute-start | bytes 245768 | tf_op jit(solution)/shard_map/ppermute | solution.py:21
  13.6 0.8 %collective-permute-start.3 = (bf16[160,256]{1,0:T(8,128)(2,1)S(1)}, bf16[160,256]{1,0:T(8,128)(2,1)S(1)}, u32[]{:S(2)}, u32[]{:S(2)}) collective-permute-start(bf16[160,256]{1,0:T(8,128)(2,1)S(1)} %pad_maximum_fusion.after_ref.refs_0_), channel_id=1, source_target_pairs={{0,2},{1,3},{2,0},{3,1},{4,6},{5,7},{6,4},{7,5},{8,10},{9,11},{10,... | collective-permute-start | bytes 245768 | tf_op jit(solution)/shard_map/ppermute | solution.py:21
  14.4 0.4 %collective-permute-start.8 = (bf16[40,1024]{1,0:T(8,128)(2,1)S(1)}, bf16[40,1024]{1,0:T(8,128)(2,1)S(1)}, u32[]{:S(2)}, u32[]{:S(2)}) collective-permute-start(bf16[40,1024]{1,0:T(8,128)(2,1)S(1)} %get-tuple-element.37), channel_id=1, source_target_pairs={{0,8},{8,0},{16,24},{24,16},{1,9},{9,1},{17,25},{25,17},{2,10},{10... | collective-permute-start | bytes 245768 | tf_op jit(solution)/shard_map/ppermute | solution.py:21
  14.8 0.7 %copy-done = s32[32]{0:T(128)S(1)} copy-done((s32[32]{0:T(128)S(1)}, s32[32]{0:T(128)}, u32[]{:S(2)}) %copy-start) | copy-done | bytes 152
  15.5 3.5 %shard_map.55 = (bf16[1024,4096]{1,0:T(8,128)(2,1)S(1)}, s32[1,1280]{1,0:T(1,128)S(1)}, s32[1280,128]{1,0:T(8,128)S(1)}) custom-call(s32[32]{0:T(128)S(1)} %copy-done, bf16[1024,4096]{1,0:T(8,128)(2,1)} %weight_ref.1, bf16[160,256]{1,0:T(8,128)(2,1)S(1)} %pad_maximum_fusion.after_ref.refs_0_, bf16[40,1024]{1,0:T(8,128)(2,1)S(1)} %collective-permute-done.6.refs_0_.refs_2_, ...), custom_call_target="tpu_custom_call" | custom-call | bytes 4194304 | tf_op jit(solution)/shard_map/pallas_call | solution.py:83
  19.0 0.6 %collective-permute-done.4.refs_2_ = bf16[160,256]{1,0:T(8,128)(2,1)S(1)} collective-permute-done((bf16[160,256]{1,0:T(8,128)(2,1)S(1)}, bf16[160,256]{1,0:T(8,128)(2,1)S(1)}, u32[]{:S(2)}, u32[]{:S(2)}) %collective-permute-start.4) | collective-permute-done | bytes 81952 | tf_op jit(solution)/shard_map/ppermute | solution.py:21
  19.5 0.0 collective-permute-start.10
  19.5 0.5 %collective-permute-start.11 = (bf16[160,256]{1,0:T(8,128)(2,1)S(1)}, bf16[160,256]{1,0:T(8,128)(2,1)S(1)}, u32[]{:S(2)}, u32[]{:S(2)}) collective-permute-start(bf16[160,256]{1,0:T(8,128)(2,1)S(1)} %collective-permute-done.4.refs_2_), channel_id=1, source_target_pairs={{0,1},{1,0},{2,3},{3,2},{4,5},{5,4},{6,7},{7,6},{8,9},{9,8},{10,11... | collective-permute-start | bytes 245768 | tf_op jit(solution)/shard_map/ppermute | solution.py:21
  20.0 0.0 collective-permute-start.12
  20.1 0.2 shard_map.56.q_ref
  20.3 1.5 %shard_map.57 = (f32[1,1280]{1,0:T(1,128)S(1)}, f32[1,1280]{1,0:T(1,128)S(1)}, f32[128,1280]{1,0:T(8,128)S(1)}) custom-call(s32[1280,128]{1,0:T(8,128)S(1)} %get-tuple-element.22.kpos_ref, s32[1,1280]{1,0:T(1,128)S(1)} %get-tuple-element.23.qpos_ref, bf16[128,1280]{1,0:T(8,128)(2,1)S(1)} %shard_map.56.q_ref, ...), custom_call_target="tpu_custom_call" | custom-call | flops 419430400 | bytes 4194304 | tf_op jit(solution)/shard_map/pallas_call | solution.py:192
  21.8 2.0 %shard_map.58 = (bf16[160,1024]{1,0:T(8,128)(2,1)S(1)}, bf16[80,1024]{1,0:T(8,128)(2,1)S(1)}, bf16[80,1024]{1,0:T(8,128)(2,1)S(1)}) custom-call(s32[1280,128]{1,0:T(8,128)S(1)} %get-tuple-element.22.kpos_ref, s32[1,1280]{1,0:T(1,128)S(1)} %get-tuple-element.23.qpos_ref, bf16[128,1280]{1,0:T(8,128)(2,1)S(1)} %shard_map.56.q_ref, ...), custom_call_target="tpu_custom_call" | custom-call | flops 754974720 | bytes 4194304 | tf_op jit(solution)/shard_map/pallas_call | solution.py:231
  23.8 1.7 %collective-permute-start.14 = (bf16[80,1024]{1,0:T(8,128)(2,1)S(1)}, bf16[80,1024]{1,0:T(8,128)(2,1)S(1)}, u32[]{:S(2)}, u32[]{:S(2)}) collective-permute-start(bf16[80,1024]{1,0:T(8,128)(2,1)S(1)} %get-tuple-element.34), channel_id=1, source_target_pairs={{0,8},{1,17},{2,10},{3,19},{4,12},{5,21},{6,14},{7,23},{8,0},{9,25... | collective-permute-start | bytes 491528 | tf_op jit(solution)/shard_map/ppermute | solution.py:28
  25.5 0.4 %collective-permute-start.16 = (bf16[80,1024]{1,0:T(8,128)(2,1)S(1)}, bf16[80,1024]{1,0:T(8,128)(2,1)S(1)}, u32[]{:S(2)}, u32[]{:S(2)}) collective-permute-start(bf16[80,1024]{1,0:T(8,128)(2,1)S(1)} %get-tuple-element.36), channel_id=1, source_target_pairs={{0,8},{1,17},{2,10},{3,19},{4,12},{5,21},{6,14},{7,23},{8,0},{9,25... | collective-permute-start | bytes 491528 | tf_op jit(solution)/shard_map/ppermute | solution.py:28
  25.9 0.9 %shard_map.60 = (bf16[160,1024]{1,0:T(8,128)(2,1)S(1)}, bf16[80,1024]{1,0:T(8,128)(2,1)S(1)}, bf16[80,1024]{1,0:T(8,128)(2,1)S(1)}) custom-call(bf16[160,1024]{1,0:T(8,128)(2,1)S(1)} %get-tuple-element.31.attn_ref, bf16[1024,4096]{1,0:T(8,128)(2,1)S(1)} %get-tuple-element.30.refs_7_.weight_ref), custom_call_target="tpu_custom_call" | custom-call | flops 671088640 | bytes 2097152 | tf_op jit(solution)/shard_map/pallas_call | solution.py:268
  26.8 1.7 %collective-permute-start.13 = (bf16[160,1024]{1,0:T(8,128)(2,1)S(1)}, bf16[160,1024]{1,0:T(8,128)(2,1)S(1)}, u32[]{:S(2)}, u32[]{:S(2)}) collective-permute-start(bf16[160,1024]{1,0:T(8,128)(2,1)S(1)} %get-tuple-element.32), channel_id=1, source_target_pairs={{0,8},{1,17},{2,10},{3,19},{4,12},{5,21},{6,14},{7,23},{8,0},{9,25... | collective-permute-start | bytes 983048 | tf_op jit(solution)/shard_map/ppermute | solution.py:28
  28.5 0.7 %collective-permute-done.14.theirs_ref = bf16[80,1024]{1,0:T(8,128)(2,1)S(1)} collective-permute-done((bf16[80,1024]{1,0:T(8,128)(2,1)S(1)}, bf16[80,1024]{1,0:T(8,128)(2,1)S(1)}, u32[]{:S(2)}, u32[]{:S(2)}) %collective-permute-start.14) | collective-permute-done | bytes 163872 | tf_op jit(solution)/shard_map/ppermute | solution.py:28
  29.3 1.7 %collective-permute-start.15 = (bf16[80,1024]{1,0:T(8,128)(2,1)S(1)}, bf16[80,1024]{1,0:T(8,128)(2,1)S(1)}, u32[]{:S(2)}, u32[]{:S(2)}) collective-permute-start(bf16[80,1024]{1,0:T(8,128)(2,1)S(1)} %shard_map.61), channel_id=1, source_target_pairs={{0,16},{1,9},{2,18},{3,11},{4,20},{5,13},{6,22},{7,15},{8,24},{9,1... | collective-permute-start | bytes 491528 | tf_op jit(solution)/shard_map/ppermute | solution.py:28
  31.0 1.7 %collective-permute-start.17 = (bf16[80,1024]{1,0:T(8,128)(2,1)S(1)}, bf16[80,1024]{1,0:T(8,128)(2,1)S(1)}, u32[]{:S(2)}, u32[]{:S(2)}) collective-permute-start(bf16[80,1024]{1,0:T(8,128)(2,1)S(1)} %shard_map.62), channel_id=1, source_target_pairs={{0,16},{1,9},{2,18},{3,11},{4,20},{5,13},{6,22},{7,15},{8,24},{9,1... | collective-permute-start | bytes 491528 | tf_op jit(solution)/shard_map/ppermute | solution.py:28
  32.7 0.5 %shard_map.59.kept_ref = bf16[160,1024]{1,0:T(8,128)(2,1)S(1)} custom-call(bf16[160,1024]{1,0:T(8,128)(2,1)S(1)} %get-tuple-element.31.attn_ref, bf16[1024,4096]{1,0:T(8,128)(2,1)S(1)} %get-tuple-element.30.refs_7_.weight_ref), custom_call_target="tpu_custom_call" | custom-call | flops 335544320 | bytes 2097152 | tf_op jit(solution)/shard_map/pallas_call | solution.py:268
  33.3 2.5 %collective-permute-done.15.refs_0_ = bf16[80,1024]{1,0:T(8,128)(2,1)S(1)} collective-permute-done((bf16[80,1024]{1,0:T(8,128)(2,1)S(1)}, bf16[80,1024]{1,0:T(8,128)(2,1)S(1)}, u32[]{:S(2)}, u32[]{:S(2)}) %collective-permute-start.15) | collective-permute-done | bytes 163872 | tf_op jit(solution)/shard_map/ppermute | solution.py:28
  35.7 1.8 %collective-permute-done.17.refs_1_ = bf16[80,1024]{1,0:T(8,128)(2,1)S(1)} collective-permute-done((bf16[80,1024]{1,0:T(8,128)(2,1)S(1)}, bf16[80,1024]{1,0:T(8,128)(2,1)S(1)}, u32[]{:S(2)}, u32[]{:S(2)}) %collective-permute-start.17) | collective-permute-done | bytes 163872 | tf_op jit(solution)/shard_map/ppermute | solution.py:28
  37.5 0.8 %shard_map.63 = bf16[160,1024]{1,0:T(8,128)(2,1)} custom-call(bf16[160,1024]{1,0:T(8,128)(2,1)S(1)} %shard_map.59.kept_ref, bf16[160,1024]{1,0:T(8,128)(2,1)S(1)} %collective-permute-done.13.received_ref, bf16[80,1024]{1,0:T(8,128)(2,1)S(1)} %collective-permute-done.15.refs_0_, bf16[80,1024]{1,0:T(8,128)(2,1)S(1)} %collective-permute-done.17.refs_1_), custom_call_target="tpu_custom_call" | custom-call | flops 655360 | bytes 1310720 | tf_op jit(solution)/shard_map/pallas_call | solution.py:299
  (21 shorter events, 0.1 us)
Async XLA Ops:
  0.8 9.1 %collective-permute-start.1 = (bf16[40,256]{1,0:T(8,128)(2,1)S(1)}, bf16[40,256]{1,0:T(8,128)(2,1)S(1)}, u32[]{:S(2)}, u32[]{:S(2)}) collective-permute-start(bf16[40,256]{1,0:T(8,128)(2,1)S(1)} %pad_maximum_fusion.2), channel_id=1, source_target_pairs={{0,16},{8,24},{16,0},{24,8},{1,17},{9,25},{17,1},{25,9},{2,18},{10... | collective-permute-start | bytes 61448 | tf_op jit(solution)/shard_map/ppermute | solution.py:21
  3.9 6.0 %collective-permute-start.2 = (bf16[40,256]{1,0:T(8,128)(2,1)S(1)}, bf16[40,256]{1,0:T(8,128)(2,1)S(1)}, u32[]{:S(2)}, u32[]{:S(2)}) collective-permute-start(bf16[40,256]{1,0:T(8,128)(2,1)S(1)} %pad_maximum_fusion.3), channel_id=1, source_target_pairs={{0,24},{8,16},{16,8},{24,0},{1,25},{9,17},{17,9},{25,1},{2,26},{10... | collective-permute-start | bytes 61448 | tf_op jit(solution)/shard_map/ppermute | solution.py:21
  5.3 4.6 %collective-permute-start = (bf16[40,256]{1,0:T(8,128)(2,1)S(1)}, bf16[40,256]{1,0:T(8,128)(2,1)S(1)}, u32[]{:S(2)}, u32[]{:S(2)}) collective-permute-start(bf16[40,256]{1,0:T(8,128)(2,1)S(1)} %pad_maximum_fusion.1), channel_id=1, source_target_pairs={{0,8},{8,0},{16,24},{24,16},{1,9},{9,1},{17,25},{25,17},{2,10},{10... | collective-permute-start | bytes 61448 | tf_op jit(solution)/shard_map/ppermute | solution.py:21
  6.5 7.9 %collective-permute-start.7 = (bf16[40,1024]{1,0:T(8,128)(2,1)S(1)}, bf16[40,1024]{1,0:T(8,128)(2,1)S(1)}, u32[]{:S(2)}, u32[]{:S(2)}) collective-permute-start(bf16[40,1024]{1,0:T(8,128)(2,1)S(1)} %get-tuple-element.38), channel_id=1, source_target_pairs={{0,24},{8,16},{16,8},{24,0},{1,25},{9,17},{17,9},{25,1},{2,26},{10... | collective-permute-start | bytes 245768 | tf_op jit(solution)/shard_map/ppermute | solution.py:21
  9.4 5.4 %collective-permute-start.6 = (bf16[40,1024]{1,0:T(8,128)(2,1)S(1)}, bf16[40,1024]{1,0:T(8,128)(2,1)S(1)}, u32[]{:S(2)}, u32[]{:S(2)}) collective-permute-start(bf16[40,1024]{1,0:T(8,128)(2,1)S(1)} %get-tuple-element.39), channel_id=1, source_target_pairs={{0,16},{8,24},{16,0},{24,8},{1,17},{9,25},{17,1},{25,9},{2,18},{10... | collective-permute-start | bytes 245768 | tf_op jit(solution)/shard_map/ppermute | solution.py:21
  9.9 9.0 %collective-permute-start.5 = (bf16[160,256]{1,0:T(8,128)(2,1)S(1)}, bf16[160,256]{1,0:T(8,128)(2,1)S(1)}, u32[]{:S(2)}, u32[]{:S(2)}) collective-permute-start(bf16[160,256]{1,0:T(8,128)(2,1)S(1)} %pad_maximum_fusion.after_ref.refs_0_), channel_id=1, source_target_pairs={{0,6},{1,7},{2,4},{3,5},{4,2},{5,3},{6,0},{7,1},{8,14},{9,15},{10,... | collective-permute-start | bytes 245768 | tf_op jit(solution)/shard_map/ppermute | solution.py:21
  13.6 5.9 %collective-permute-start.4 = (bf16[160,256]{1,0:T(8,128)(2,1)S(1)}, bf16[160,256]{1,0:T(8,128)(2,1)S(1)}, u32[]{:S(2)}, u32[]{:S(2)}) collective-permute-start(bf16[160,256]{1,0:T(8,128)(2,1)S(1)} %pad_maximum_fusion.after_ref.refs_0_), channel_id=1, source_target_pairs={{0,4},{1,5},{2,6},{3,7},{4,0},{5,1},{6,2},{7,3},{8,12},{9,13},{10,... | collective-permute-start | bytes 245768 | tf_op jit(solution)/shard_map/ppermute | solution.py:21
  13.6 5.9 %collective-permute-start.3 = (bf16[160,256]{1,0:T(8,128)(2,1)S(1)}, bf16[160,256]{1,0:T(8,128)(2,1)S(1)}, u32[]{:S(2)}, u32[]{:S(2)}) collective-permute-start(bf16[160,256]{1,0:T(8,128)(2,1)S(1)} %pad_maximum_fusion.after_ref.refs_0_), channel_id=1, source_target_pairs={{0,2},{1,3},{2,0},{3,1},{4,6},{5,7},{6,4},{7,5},{8,10},{9,11},{10,... | collective-permute-start | bytes 245768 | tf_op jit(solution)/shard_map/ppermute | solution.py:21
  14.4 5.7 %collective-permute-start.8 = (bf16[40,1024]{1,0:T(8,128)(2,1)S(1)}, bf16[40,1024]{1,0:T(8,128)(2,1)S(1)}, u32[]{:S(2)}, u32[]{:S(2)}) collective-permute-start(bf16[40,1024]{1,0:T(8,128)(2,1)S(1)} %get-tuple-element.37), channel_id=1, source_target_pairs={{0,8},{8,0},{16,24},{24,16},{1,9},{9,1},{17,25},{25,17},{2,10},{10... | collective-permute-start | bytes 245768 | tf_op jit(solution)/shard_map/ppermute | solution.py:21
  14.8 7.0 %collective-permute-start.9 = (bf16[160,256]{1,0:T(8,128)(2,1)S(1)}, bf16[160,256]{1,0:T(8,128)(2,1)S(1)}, u32[]{:S(2)}, u32[]{:S(2)}) collective-permute-start(bf16[160,256]{1,0:T(8,128)(2,1)S(1)} %pad_maximum_fusion.after_ref.refs_0_), channel_id=1, source_target_pairs={{0,1},{1,0},{2,3},{3,2},{4,5},{5,4},{6,7},{7,6},{8,9},{9,8},{10,11... | collective-permute-start | bytes 245768 | tf_op jit(solution)/shard_map/ppermute | solution.py:21
  14.8 0.7 %copy-start = (s32[32]{0:T(128)S(1)}, s32[32]{0:T(128)}, u32[]{:S(2)}) copy-start(s32[32]{0:T(128)} %order_hbm.1) | copy-start | bytes 388
  19.5 2.3 %collective-permute-start.10 = (bf16[160,256]{1,0:T(8,128)(2,1)S(1)}, bf16[160,256]{1,0:T(8,128)(2,1)S(1)}, u32[]{:S(2)}, u32[]{:S(2)}) collective-permute-start(bf16[160,256]{1,0:T(8,128)(2,1)S(1)} %collective-permute-done.3.refs_1_), channel_id=1, source_target_pairs={{0,1},{1,0},{2,3},{3,2},{4,5},{5,4},{6,7},{7,6},{8,9},{9,8},{10,11... | collective-permute-start | bytes 245768 | tf_op jit(solution)/shard_map/ppermute | solution.py:21
  19.5 2.3 %collective-permute-start.11 = (bf16[160,256]{1,0:T(8,128)(2,1)S(1)}, bf16[160,256]{1,0:T(8,128)(2,1)S(1)}, u32[]{:S(2)}, u32[]{:S(2)}) collective-permute-start(bf16[160,256]{1,0:T(8,128)(2,1)S(1)} %collective-permute-done.4.refs_2_), channel_id=1, source_target_pairs={{0,1},{1,0},{2,3},{3,2},{4,5},{5,4},{6,7},{7,6},{8,9},{9,8},{10,11... | collective-permute-start | bytes 245768 | tf_op jit(solution)/shard_map/ppermute | solution.py:21
  20.0 1.8 %collective-permute-start.12 = (bf16[160,256]{1,0:T(8,128)(2,1)S(1)}, bf16[160,256]{1,0:T(8,128)(2,1)S(1)}, u32[]{:S(2)}, u32[]{:S(2)}) collective-permute-start(bf16[160,256]{1,0:T(8,128)(2,1)S(1)} %collective-permute-done.5.refs_3_), channel_id=1, source_target_pairs={{0,1},{1,0},{2,3},{3,2},{4,5},{5,4},{6,7},{7,6},{8,9},{9,8},{10,11... | collective-permute-start | bytes 245768 | tf_op jit(solution)/shard_map/ppermute | solution.py:21
  23.8 5.4 %collective-permute-start.14 = (bf16[80,1024]{1,0:T(8,128)(2,1)S(1)}, bf16[80,1024]{1,0:T(8,128)(2,1)S(1)}, u32[]{:S(2)}, u32[]{:S(2)}) collective-permute-start(bf16[80,1024]{1,0:T(8,128)(2,1)S(1)} %get-tuple-element.34), channel_id=1, source_target_pairs={{0,8},{1,17},{2,10},{3,19},{4,12},{5,21},{6,14},{7,23},{8,0},{9,25... | collective-permute-start | bytes 491528 | tf_op jit(solution)/shard_map/ppermute | solution.py:28
  25.5 5.5 %collective-permute-start.16 = (bf16[80,1024]{1,0:T(8,128)(2,1)S(1)}, bf16[80,1024]{1,0:T(8,128)(2,1)S(1)}, u32[]{:S(2)}, u32[]{:S(2)}) collective-permute-start(bf16[80,1024]{1,0:T(8,128)(2,1)S(1)} %get-tuple-element.36), channel_id=1, source_target_pairs={{0,8},{1,17},{2,10},{3,19},{4,12},{5,21},{6,14},{7,23},{8,0},{9,25... | collective-permute-start | bytes 491528 | tf_op jit(solution)/shard_map/ppermute | solution.py:28
  26.8 10.7 %collective-permute-start.13 = (bf16[160,1024]{1,0:T(8,128)(2,1)S(1)}, bf16[160,1024]{1,0:T(8,128)(2,1)S(1)}, u32[]{:S(2)}, u32[]{:S(2)}) collective-permute-start(bf16[160,1024]{1,0:T(8,128)(2,1)S(1)} %get-tuple-element.32), channel_id=1, source_target_pairs={{0,8},{1,17},{2,10},{3,19},{4,12},{5,21},{6,14},{7,23},{8,0},{9,25... | collective-permute-start | bytes 983048 | tf_op jit(solution)/shard_map/ppermute | solution.py:28
  29.3 6.5 %collective-permute-start.15 = (bf16[80,1024]{1,0:T(8,128)(2,1)S(1)}, bf16[80,1024]{1,0:T(8,128)(2,1)S(1)}, u32[]{:S(2)}, u32[]{:S(2)}) collective-permute-start(bf16[80,1024]{1,0:T(8,128)(2,1)S(1)} %shard_map.61), channel_id=1, source_target_pairs={{0,16},{1,9},{2,18},{3,11},{4,20},{5,13},{6,22},{7,15},{8,24},{9,1... | collective-permute-start | bytes 491528 | tf_op jit(solution)/shard_map/ppermute | solution.py:28
  31.0 6.5 %collective-permute-start.17 = (bf16[80,1024]{1,0:T(8,128)(2,1)S(1)}, bf16[80,1024]{1,0:T(8,128)(2,1)S(1)}, u32[]{:S(2)}, u32[]{:S(2)}) collective-permute-start(bf16[80,1024]{1,0:T(8,128)(2,1)S(1)} %shard_map.62), channel_id=1, source_target_pairs={{0,16},{1,9},{2,18},{3,11},{4,20},{5,13},{6,22},{7,15},{8,24},{9,1... | collective-permute-start | bytes 491528 | tf_op jit(solution)/shard_map/ppermute | solution.py:28

commit v7 on v6

--- a/solution.py
+++ b/solution.py
@@ -12,6 +12,7 @@
 NEG_FILL = -1e30
 ROOMY = 42
 STRIPE = 256
+SUM_ROWS = 16
 FETCHES = 8
 PARTS = 2
 EXP2_SCALE = D_HEAD ** (-0.5) * math.log2(math.e)
@@ -141,6 +142,8 @@
 def fold_keys(kv_refs, kpos, qpos_ref, q_ref, state, emit):
     keys = jnp.concatenate([ref[:, :D_HEAD] for ref in kv_refs], axis=0)
     values = jnp.concatenate([ref[:, D_HEAD:] for ref in kv_refs], axis=0).T
+    ones = jnp.ones((SUM_ROWS, values.shape[1]), values.dtype)
+    values = jnp.concatenate([values, ones], axis=0)
     kpos = jnp.concatenate([kpos] * (STRIPE // D_HEAD), axis=1)
 
     def score(at):
@@ -152,10 +155,11 @@
         if state is not None:
             peak = jnp.maximum(state[0][:, at], peak)
         weights = jnp.exp2((scores - peak) * EXP2_SCALE)
-        return peak, jnp.sum(weights, axis=0, keepdims=True), weights.astype(jnp.bfloat16)
-
-    def finish(at, peak, denom, weights):
-        mixed = jnp.dot(values, weights, preferred_element_type=jnp.float32)
+        return peak, weights.astype(jnp.bfloat16)
+
+    def finish(at, peak, weights):
+        product = jnp.dot(values, weights, preferred_element_type=jnp.float32)
+        mixed, denom = product[:D_HEAD], product[D_HEAD : D_HEAD + 1]
         if state is not None:
             factor = jnp.exp2((state[0][:, at] - peak) * EXP2_SCALE)
             denom = factor * state[1][:, at] + denom

time: 38.6 us -> 38.5 us (level)
  no operation moved by 1% of the time
where the time goes in v7:
time: 38.5 us; the launch traced here: 38.3 us
  starting transfers between devices  20.7 us (54%)
  Pallas kernels  9.46 us (25%)
  waiting for transfers between devices  5.5 us (14%)
  local copies, waits for them, and re-layouts  2.51 us (7%)
    ppermute x13, starting transfers between devices, swap(): return lax.ppermute(x, axis, [(i, i ^ flip) for i in range(size)])  13.4 us
    ppermute x5, starting transfers between devices, swap_by_core(): return lax.ppermute(x, ('head', 'ctx'), pairs)  7.25 us
    ppermute x5, waiting for transfers between devices, swap_by_core(): return lax.ppermute(x, ('head', 'ctx'), pairs)  4.91 us
    pallas_call x1, Pallas kernels, prepare(): pl.pallas_call(functools.partial(prepare_kernel, span, n_head, chunk_flip...  3.48 us
    pallas_call x1, Pallas kernels, attend(): pl.pallas_call(functools.partial(attend_kernel, n_chunk), out_shape=(jax....  1.97 us
    dynamic_slice x2, local copies, waits for them, and re-layouts, cut(): return lax.dynamic_slice_in_dim(x[0], (me ^ k) * width, width, 1)  1.86 us
    pallas_call x1, Pallas kernels, early_attend(): pl.pallas_call(functools.partial(early_kernel, n_chunk), out_shape=(line,...  1.44 us
    pallas_call x2, Pallas kernels, project_rest(): pl.pallas_call(kernel, out_shape=tuple((jax.ShapeDtypeStruct((rows, cols)...  1.42 us
  transfers between devices with their start and end apart: 18, of which 4 were waited for; matrix products, arithmetic and copies ran while one was open for 3% of the time, Pallas kernels for 17%

profile of v7, /device:TPU:0, one launch (start us, length us, event | category | flops | bytes accessed | tf_op | source)
XLA Modules:
  0.0 38.3 jit_solution(5115304250390604231)
XLA Ops:
  0.0 0.8 %dynamic-slice_bitcast_fusion.10 = (bf16[40,128]{1,0:T(8,128)(2,1)S(1)}, bf16[40,128]{1,0:T(8,128)(2,1)S(1)}, bf16[40,128]{1,0:T(8,128)(2,1)S(1)}, bf16[40,128]{...) fusion(bf16[1,40,512]{2,1,0:T(8,128)(2,1)} %param.7, ...), kind=kLoop, calls=%fused_computation.14 | loop fusion | bytes 163856 | tf_op jit(solution)/shard_map/dynamic_slice | solution.py:318
  0.8 3.0 %collective-permute-start.1 = (bf16[40,256]{1,0:T(8,128)(2,1)S(1)}, bf16[40,256]{1,0:T(8,128)(2,1)S(1)}, u32[]{:S(2)}, u32[]{:S(2)}) collective-permute-start(bf16[40,256]{1,0:T(8,128)(2,1)S(1)} %pad_maximum_fusion.2), channel_id=1, source_target_pairs={{0,16},{8,24},{16,0},{24,8},{1,17},{9,25},{17,1},{25,9},{2,18},{10... | collective-permute-start | bytes 61448 | tf_op jit(solution)/shard_map/ppermute | solution.py:22
  3.9 1.4 %collective-permute-start.2 = (bf16[40,256]{1,0:T(8,128)(2,1)S(1)}, bf16[40,256]{1,0:T(8,128)(2,1)S(1)}, u32[]{:S(2)}, u32[]{:S(2)}) collective-permute-start(bf16[40,256]{1,0:T(8,128)(2,1)S(1)} %pad_maximum_fusion.3), channel_id=1, source_target_pairs={{0,24},{8,16},{16,8},{24,0},{1,25},{9,17},{17,9},{25,1},{2,26},{10... | collective-permute-start | bytes 61448 | tf_op jit(solution)/shard_map/ppermute | solution.py:22
  5.3 0.1 collective-permute-start
  5.5 1.0 %dynamic-slice_bitcast_fusion = (bf16[40,1024]{1,0:T(8,128)(2,1)S(1)}, bf16[40,1024]{1,0:T(8,128)(2,1)S(1)}, bf16[40,1024]{1,0:T(8,128)(2,1)S(1)}, bf16[40,1024]{1,0:T(8,128)(2,1)S(1)}) fusion(bf16[1,40,4096]{2,1,0:T(8,128)(2,1)} %param.5, s32[]{:T(128)S(6)} %select_n.35, s32[]{:T(128)S(6)} %select_n.33, s32[]{:T(128)S(6)} %select_n.32, s32[]{:T(128)S(6)} %select_n.34), kind=kLoop, calls=%fused_computation.1 | loop fusion | bytes 655376 | tf_op jit(solution)/shard_map/dynamic_slice | solution.py:318
  6.5 2.9 %collective-permute-start.7 = (bf16[40,1024]{1,0:T(8,128)(2,1)S(1)}, bf16[40,1024]{1,0:T(8,128)(2,1)S(1)}, u32[]{:S(2)}, u32[]{:S(2)}) collective-permute-start(bf16[40,1024]{1,0:T(8,128)(2,1)S(1)} %get-tuple-element.38), channel_id=1, source_target_pairs={{0,24},{8,16},{16,8},{24,0},{1,25},{9,17},{17,9},{25,1},{2,26},{10... | collective-permute-start | bytes 245768 | tf_op jit(solution)/shard_map/ppermute | solution.py:22
  9.4 0.5 %collective-permute-start.6 = (bf16[40,1024]{1,0:T(8,128)(2,1)S(1)}, bf16[40,1024]{1,0:T(8,128)(2,1)S(1)}, u32[]{:S(2)}, u32[]{:S(2)}) collective-permute-start(bf16[40,1024]{1,0:T(8,128)(2,1)S(1)} %get-tuple-element.39), channel_id=1, source_target_pairs={{0,16},{8,24},{16,0},{24,8},{1,17},{9,25},{17,1},{25,9},{2,18},{10... | collective-permute-start | bytes 245768 | tf_op jit(solution)/shard_map/ppermute | solution.py:22
  9.9 0.0 collective-permute-done.1
  9.9 3.7 %collective-permute-start.5 = (bf16[160,256]{1,0:T(8,128)(2,1)S(1)}, bf16[160,256]{1,0:T(8,128)(2,1)S(1)}, u32[]{:S(2)}, u32[]{:S(2)}) collective-permute-start(bf16[160,256]{1,0:T(8,128)(2,1)S(1)} %pad_maximum_fusion.after_ref.refs_0_), channel_id=1, source_target_pairs={{0,6},{1,7},{2,4},{3,5},{4,2},{5,3},{6,0},{7,1},{8,14},{9,15},{10,... | collective-permute-start | bytes 245768 | tf_op jit(solution)/shard_map/ppermute | solution.py:22
  13.6 0.0 collective-permute-start.4
  13.6 0.8 %collective-permute-start.3 = (bf16[160,256]{1,0:T(8,128)(2,1)S(1)}, bf16[160,256]{1,0:T(8,128)(2,1)S(1)}, u32[]{:S(2)}, u32[]{:S(2)}) collective-permute-start(bf16[160,256]{1,0:T(8,128)(2,1)S(1)} %pad_maximum_fusion.after_ref.refs_0_), channel_id=1, source_target_pairs={{0,2},{1,3},{2,0},{3,1},{4,6},{5,7},{6,4},{7,5},{8,10},{9,11},{10,... | collective-permute-start | bytes 245768 | tf_op jit(solution)/shard_map/ppermute | solution.py:22
  14.4 0.4 %collective-permute-start.8 = (bf16[40,1024]{1,0:T(8,128)(2,1)S(1)}, bf16[40,1024]{1,0:T(8,128)(2,1)S(1)}, u32[]{:S(2)}, u32[]{:S(2)}) collective-permute-start(bf16[40,1024]{1,0:T(8,128)(2,1)S(1)} %get-tuple-element.37), channel_id=1, source_target_pairs={{0,8},{8,0},{16,24},{24,16},{1,9},{9,1},{17,25},{25,17},{2,10},{10... | collective-permute-start | bytes 245768 | tf_op jit(solution)/shard_map/ppermute | solution.py:22
  14.8 0.7 %copy-done = s32[32]{0:T(128)S(1)} copy-done((s32[32]{0:T(128)S(1)}, s32[32]{0:T(128)}, u32[]{:S(2)}) %copy-start) | copy-done | bytes 152
  15.5 3.5 %shard_map.55 = (bf16[1024,4096]{1,0:T(8,128)(2,1)S(1)}, s32[1,1280]{1,0:T(1,128)S(1)}, s32[1280,128]{1,0:T(8,128)S(1)}) custom-call(s32[32]{0:T(128)S(1)} %copy-done, bf16[1024,4096]{1,0:T(8,128)(2,1)} %weight_ref.1, bf16[160,256]{1,0:T(8,128)(2,1)S(1)} %pad_maximum_fusion.after_ref.refs_0_, bf16[40,1024]{1,0:T(8,128)(2,1)S(1)} %collective-permute-done.6.refs_0_.refs_2_, ...), custom_call_target="tpu_custom_call" | custom-call | bytes 4194304 | tf_op jit(solution)/shard_map/pallas_call | solution.py:84
  19.0 0.6 %collective-permute-done.4.refs_2_ = bf16[160,256]{1,0:T(8,128)(2,1)S(1)} collective-permute-done((bf16[160,256]{1,0:T(8,128)(2,1)S(1)}, bf16[160,256]{1,0:T(8,128)(2,1)S(1)}, u32[]{:S(2)}, u32[]{:S(2)}) %collective-permute-start.4) | collective-permute-done | bytes 81952 | tf_op jit(solution)/shard_map/ppermute | solution.py:22
  19.5 0.0 collective-permute-start.10
  19.5 0.5 %collective-permute-start.11 = (bf16[160,256]{1,0:T(8,128)(2,1)S(1)}, bf16[160,256]{1,0:T(8,128)(2,1)S(1)}, u32[]{:S(2)}, u32[]{:S(2)}) collective-permute-start(bf16[160,256]{1,0:T(8,128)(2,1)S(1)} %collective-permute-done.4.refs_2_), channel_id=1, source_target_pairs={{0,1},{1,0},{2,3},{3,2},{4,5},{5,4},{6,7},{7,6},{8,9},{9,8},{10,11... | collective-permute-start | bytes 245768 | tf_op jit(solution)/shard_map/ppermute | solution.py:22
  20.0 0.0 collective-permute-start.12
  20.1 0.2 shard_map.56.q_ref
  20.3 1.4 %shard_map.57 = (f32[1,1280]{1,0:T(1,128)S(1)}, f32[1,1280]{1,0:T(1,128)S(1)}, f32[128,1280]{1,0:T(8,128)S(1)}) custom-call(s32[1280,128]{1,0:T(8,128)S(1)} %get-tuple-element.22.kpos_ref, s32[1,1280]{1,0:T(1,128)S(1)} %get-tuple-element.23.qpos_ref, bf16[128,1280]{1,0:T(8,128)(2,1)S(1)} %shard_map.56.q_ref, ...), custom_call_target="tpu_custom_call" | custom-call | flops 419430400 | bytes 4194304 | tf_op jit(solution)/shard_map/pallas_call | solution.py:196
  21.8 2.0 %shard_map.58 = (bf16[160,1024]{1,0:T(8,128)(2,1)S(1)}, bf16[80,1024]{1,0:T(8,128)(2,1)S(1)}, bf16[80,1024]{1,0:T(8,128)(2,1)S(1)}) custom-call(s32[1280,128]{1,0:T(8,128)S(1)} %get-tuple-element.22.kpos_ref, s32[1,1280]{1,0:T(1,128)S(1)} %get-tuple-element.23.qpos_ref, bf16[128,1280]{1,0:T(8,128)(2,1)S(1)} %shard_map.56.q_ref, ...), custom_call_target="tpu_custom_call" | custom-call | flops 754974720 | bytes 4194304 | tf_op jit(solution)/shard_map/pallas_call | solution.py:235
  23.8 1.7 %collective-permute-start.14 = (bf16[80,1024]{1,0:T(8,128)(2,1)S(1)}, bf16[80,1024]{1,0:T(8,128)(2,1)S(1)}, u32[]{:S(2)}, u32[]{:S(2)}) collective-permute-start(bf16[80,1024]{1,0:T(8,128)(2,1)S(1)} %get-tuple-element.34), channel_id=1, source_target_pairs={{0,8},{1,17},{2,10},{3,19},{4,12},{5,21},{6,14},{7,23},{8,0},{9,25... | collective-permute-start | bytes 491528 | tf_op jit(solution)/shard_map/ppermute | solution.py:29
  25.5 0.4 %collective-permute-start.16 = (bf16[80,1024]{1,0:T(8,128)(2,1)S(1)}, bf16[80,1024]{1,0:T(8,128)(2,1)S(1)}, u32[]{:S(2)}, u32[]{:S(2)}) collective-permute-start(bf16[80,1024]{1,0:T(8,128)(2,1)S(1)} %get-tuple-element.36), channel_id=1, source_target_pairs={{0,8},{1,17},{2,10},{3,19},{4,12},{5,21},{6,14},{7,23},{8,0},{9,25... | collective-permute-start | bytes 491528 | tf_op jit(solution)/shard_map/ppermute | solution.py:29
  25.8 0.9 %shard_map.60 = (bf16[160,1024]{1,0:T(8,128)(2,1)S(1)}, bf16[80,1024]{1,0:T(8,128)(2,1)S(1)}, bf16[80,1024]{1,0:T(8,128)(2,1)S(1)}) custom-call(bf16[160,1024]{1,0:T(8,128)(2,1)S(1)} %get-tuple-element.31.attn_ref, bf16[1024,4096]{1,0:T(8,128)(2,1)S(1)} %get-tuple-element.30.refs_7_.weight_ref), custom_call_target="tpu_custom_call" | custom-call | flops 671088640 | bytes 2097152 | tf_op jit(solution)/shard_map/pallas_call | solution.py:272
  26.7 1.7 %collective-permute-start.13 = (bf16[160,1024]{1,0:T(8,128)(2,1)S(1)}, bf16[160,1024]{1,0:T(8,128)(2,1)S(1)}, u32[]{:S(2)}, u32[]{:S(2)}) collective-permute-start(bf16[160,1024]{1,0:T(8,128)(2,1)S(1)} %get-tuple-element.32), channel_id=1, source_target_pairs={{0,8},{1,17},{2,10},{3,19},{4,12},{5,21},{6,14},{7,23},{8,0},{9,25... | collective-permute-start | bytes 983048 | tf_op jit(solution)/shard_map/ppermute | solution.py:29
  28.4 0.7 %collective-permute-done.14.theirs_ref = bf16[80,1024]{1,0:T(8,128)(2,1)S(1)} collective-permute-done((bf16[80,1024]{1,0:T(8,128)(2,1)S(1)}, bf16[80,1024]{1,0:T(8,128)(2,1)S(1)}, u32[]{:S(2)}, u32[]{:S(2)}) %collective-permute-start.14) | collective-permute-done | bytes 163872 | tf_op jit(solution)/shard_map/ppermute | solution.py:29
  29.2 1.7 %collective-permute-start.15 = (bf16[80,1024]{1,0:T(8,128)(2,1)S(1)}, bf16[80,1024]{1,0:T(8,128)(2,1)S(1)}, u32[]{:S(2)}, u32[]{:S(2)}) collective-permute-start(bf16[80,1024]{1,0:T(8,128)(2,1)S(1)} %shard_map.61), channel_id=1, source_target_pairs={{0,16},{1,9},{2,18},{3,11},{4,20},{5,13},{6,22},{7,15},{8,24},{9,1... | collective-permute-start | bytes 491528 | tf_op jit(solution)/shard_map/ppermute | solution.py:29
  31.0 1.7 %collective-permute-start.17 = (bf16[80,1024]{1,0:T(8,128)(2,1)S(1)}, bf16[80,1024]{1,0:T(8,128)(2,1)S(1)}, u32[]{:S(2)}, u32[]{:S(2)}) collective-permute-start(bf16[80,1024]{1,0:T(8,128)(2,1)S(1)} %shard_map.62), channel_id=1, source_target_pairs={{0,16},{1,9},{2,18},{3,11},{4,20},{5,13},{6,22},{7,15},{8,24},{9,1... | collective-permute-start | bytes 491528 | tf_op jit(solution)/shard_map/ppermute | solution.py:29
  32.7 0.5 %shard_map.59.kept_ref = bf16[160,1024]{1,0:T(8,128)(2,1)S(1)} custom-call(bf16[160,1024]{1,0:T(8,128)(2,1)S(1)} %get-tuple-element.31.attn_ref, bf16[1024,4096]{1,0:T(8,128)(2,1)S(1)} %get-tuple-element.30.refs_7_.weight_ref), custom_call_target="tpu_custom_call" | custom-call | flops 335544320 | bytes 2097152 | tf_op jit(solution)/shard_map/pallas_call | solution.py:272
  33.2 2.5 %collective-permute-done.15.refs_0_ = bf16[80,1024]{1,0:T(8,128)(2,1)S(1)} collective-permute-done((bf16[80,1024]{1,0:T(8,128)(2,1)S(1)}, bf16[80,1024]{1,0:T(8,128)(2,1)S(1)}, u32[]{:S(2)}, u32[]{:S(2)}) %collective-permute-start.15) | collective-permute-done | bytes 163872 | tf_op jit(solution)/shard_map/ppermute | solution.py:29
  35.7 1.8 %collective-permute-done.17.refs_1_ = bf16[80,1024]{1,0:T(8,128)(2,1)S(1)} collective-permute-done((bf16[80,1024]{1,0:T(8,128)(2,1)S(1)}, bf16[80,1024]{1,0:T(8,128)(2,1)S(1)}, u32[]{:S(2)}, u32[]{:S(2)}) %collective-permute-start.17) | collective-permute-done | bytes 163872 | tf_op jit(solution)/shard_map/ppermute | solution.py:29
  37.4 0.8 %shard_map.63 = bf16[160,1024]{1,0:T(8,128)(2,1)} custom-call(bf16[160,1024]{1,0:T(8,128)(2,1)S(1)} %shard_map.59.kept_ref, bf16[160,1024]{1,0:T(8,128)(2,1)S(1)} %collective-permute-done.13.received_ref, bf16[80,1024]{1,0:T(8,128)(2,1)S(1)} %collective-permute-done.15.refs_0_, bf16[80,1024]{1,0:T(8,128)(2,1)S(1)} %collective-permute-done.17.refs_1_), custom_call_target="tpu_custom_call" | custom-call | flops 655360 | bytes 1310720 | tf_op jit(solution)/shard_map/pallas_call | solution.py:303
  (21 shorter events, 0.1 us)
Async XLA Ops:
  0.8 9.1 %collective-permute-start.1 = (bf16[40,256]{1,0:T(8,128)(2,1)S(1)}, bf16[40,256]{1,0:T(8,128)(2,1)S(1)}, u32[]{:S(2)}, u32[]{:S(2)}) collective-permute-start(bf16[40,256]{1,0:T(8,128)(2,1)S(1)} %pad_maximum_fusion.2), channel_id=1, source_target_pairs={{0,16},{8,24},{16,0},{24,8},{1,17},{9,25},{17,1},{25,9},{2,18},{10... | collective-permute-start | bytes 61448 | tf_op jit(solution)/shard_map/ppermute | solution.py:22
  3.9 6.0 %collective-permute-start.2 = (bf16[40,256]{1,0:T(8,128)(2,1)S(1)}, bf16[40,256]{1,0:T(8,128)(2,1)S(1)}, u32[]{:S(2)}, u32[]{:S(2)}) collective-permute-start(bf16[40,256]{1,0:T(8,128)(2,1)S(1)} %pad_maximum_fusion.3), channel_id=1, source_target_pairs={{0,24},{8,16},{16,8},{24,0},{1,25},{9,17},{17,9},{25,1},{2,26},{10... | collective-permute-start | bytes 61448 | tf_op jit(solution)/shard_map/ppermute | solution.py:22
  5.3 4.6 %collective-permute-start = (bf16[40,256]{1,0:T(8,128)(2,1)S(1)}, bf16[40,256]{1,0:T(8,128)(2,1)S(1)}, u32[]{:S(2)}, u32[]{:S(2)}) collective-permute-start(bf16[40,256]{1,0:T(8,128)(2,1)S(1)} %pad_maximum_fusion.1), channel_id=1, source_target_pairs={{0,8},{8,0},{16,24},{24,16},{1,9},{9,1},{17,25},{25,17},{2,10},{10... | collective-permute-start | bytes 61448 | tf_op jit(solution)/shard_map/ppermute | solution.py:22
  6.5 7.9 %collective-permute-start.7 = (bf16[40,1024]{1,0:T(8,128)(2,1)S(1)}, bf16[40,1024]{1,0:T(8,128)(2,1)S(1)}, u32[]{:S(2)}, u32[]{:S(2)}) collective-permute-start(bf16[40,1024]{1,0:T(8,128)(2,1)S(1)} %get-tuple-element.38), channel_id=1, source_target_pairs={{0,24},{8,16},{16,8},{24,0},{1,25},{9,17},{17,9},{25,1},{2,26},{10... | collective-permute-start | bytes 245768 | tf_op jit(solution)/shard_map/ppermute | solution.py:22
  9.4 5.4 %collective-permute-start.6 = (bf16[40,1024]{1,0:T(8,128)(2,1)S(1)}, bf16[40,1024]{1,0:T(8,128)(2,1)S(1)}, u32[]{:S(2)}, u32[]{:S(2)}) collective-permute-start(bf16[40,1024]{1,0:T(8,128)(2,1)S(1)} %get-tuple-element.39), channel_id=1, source_target_pairs={{0,16},{8,24},{16,0},{24,8},{1,17},{9,25},{17,1},{25,9},{2,18},{10... | collective-permute-start | bytes 245768 | tf_op jit(solution)/shard_map/ppermute | solution.py:22
  9.9 9.0 %collective-permute-start.5 = (bf16[160,256]{1,0:T(8,128)(2,1)S(1)}, bf16[160,256]{1,0:T(8,128)(2,1)S(1)}, u32[]{:S(2)}, u32[]{:S(2)}) collective-permute-start(bf16[160,256]{1,0:T(8,128)(2,1)S(1)} %pad_maximum_fusion.after_ref.refs_0_), channel_id=1, source_target_pairs={{0,6},{1,7},{2,4},{3,5},{4,2},{5,3},{6,0},{7,1},{8,14},{9,15},{10,... | collective-permute-start | bytes 245768 | tf_op jit(solution)/shard_map/ppermute | solution.py:22
  13.6 5.9 %collective-permute-start.4 = (bf16[160,256]{1,0:T(8,128)(2,1)S(1)}, bf16[160,256]{1,0:T(8,128)(2,1)S(1)}, u32[]{:S(2)}, u32[]{:S(2)}) collective-permute-start(bf16[160,256]{1,0:T(8,128)(2,1)S(1)} %pad_maximum_fusion.after_ref.refs_0_), channel_id=1, source_target_pairs={{0,4},{1,5},{2,6},{3,7},{4,0},{5,1},{6,2},{7,3},{8,12},{9,13},{10,... | collective-permute-start | bytes 245768 | tf_op jit(solution)/shard_map/ppermute | solution.py:22
  13.6 5.9 %collective-permute-start.3 = (bf16[160,256]{1,0:T(8,128)(2,1)S(1)}, bf16[160,256]{1,0:T(8,128)(2,1)S(1)}, u32[]{:S(2)}, u32[]{:S(2)}) collective-permute-start(bf16[160,256]{1,0:T(8,128)(2,1)S(1)} %pad_maximum_fusion.after_ref.refs_0_), channel_id=1, source_target_pairs={{0,2},{1,3},{2,0},{3,1},{4,6},{5,7},{6,4},{7,5},{8,10},{9,11},{10,... | collective-permute-start | bytes 245768 | tf_op jit(solution)/shard_map/ppermute | solution.py:22
  14.4 5.7 %collective-permute-start.8 = (bf16[40,1024]{1,0:T(8,128)(2,1)S(1)}, bf16[40,1024]{1,0:T(8,128)(2,1)S(1)}, u32[]{:S(2)}, u32[]{:S(2)}) collective-permute-start(bf16[40,1024]{1,0:T(8,128)(2,1)S(1)} %get-tuple-element.37), channel_id=1, source_target_pairs={{0,8},{8,0},{16,24},{24,16},{1,9},{9,1},{17,25},{25,17},{2,10},{10... | collective-permute-start | bytes 245768 | tf_op jit(solution)/shard_map/ppermute | solution.py:22
  14.8 6.9 %collective-permute-start.9 = (bf16[160,256]{1,0:T(8,128)(2,1)S(1)}, bf16[160,256]{1,0:T(8,128)(2,1)S(1)}, u32[]{:S(2)}, u32[]{:S(2)}) collective-permute-start(bf16[160,256]{1,0:T(8,128)(2,1)S(1)} %pad_maximum_fusion.after_ref.refs_0_), channel_id=1, source_target_pairs={{0,1},{1,0},{2,3},{3,2},{4,5},{5,4},{6,7},{7,6},{8,9},{9,8},{10,11... | collective-permute-start | bytes 245768 | tf_op jit(solution)/shard_map/ppermute | solution.py:22
  14.8 0.7 %copy-start = (s32[32]{0:T(128)S(1)}, s32[32]{0:T(128)}, u32[]{:S(2)}) copy-start(s32[32]{0:T(128)} %order_hbm.1) | copy-start | bytes 388
  19.5 2.2 %collective-permute-start.10 = (bf16[160,256]{1,0:T(8,128)(2,1)S(1)}, bf16[160,256]{1,0:T(8,128)(2,1)S(1)}, u32[]{:S(2)}, u32[]{:S(2)}) collective-permute-start(bf16[160,256]{1,0:T(8,128)(2,1)S(1)} %collective-permute-done.3.refs_1_), channel_id=1, source_target_pairs={{0,1},{1,0},{2,3},{3,2},{4,5},{5,4},{6,7},{7,6},{8,9},{9,8},{10,11... | collective-permute-start | bytes 245768 | tf_op jit(solution)/shard_map/ppermute | solution.py:22
  19.5 2.2 %collective-permute-start.11 = (bf16[160,256]{1,0:T(8,128)(2,1)S(1)}, bf16[160,256]{1,0:T(8,128)(2,1)S(1)}, u32[]{:S(2)}, u32[]{:S(2)}) collective-permute-start(bf16[160,256]{1,0:T(8,128)(2,1)S(1)} %collective-permute-done.4.refs_2_), channel_id=1, source_target_pairs={{0,1},{1,0},{2,3},{3,2},{4,5},{5,4},{6,7},{7,6},{8,9},{9,8},{10,11... | collective-permute-start | bytes 245768 | tf_op jit(solution)/shard_map/ppermute | solution.py:22
  20.0 1.7 %collective-permute-start.12 = (bf16[160,256]{1,0:T(8,128)(2,1)S(1)}, bf16[160,256]{1,0:T(8,128)(2,1)S(1)}, u32[]{:S(2)}, u32[]{:S(2)}) collective-permute-start(bf16[160,256]{1,0:T(8,128)(2,1)S(1)} %collective-permute-done.5.refs_3_), channel_id=1, source_target_pairs={{0,1},{1,0},{2,3},{3,2},{4,5},{5,4},{6,7},{7,6},{8,9},{9,8},{10,11... | collective-permute-start | bytes 245768 | tf_op jit(solution)/shard_map/ppermute | solution.py:22
  23.8 5.4 %collective-permute-start.14 = (bf16[80,1024]{1,0:T(8,128)(2,1)S(1)}, bf16[80,1024]{1,0:T(8,128)(2,1)S(1)}, u32[]{:S(2)}, u32[]{:S(2)}) collective-permute-start(bf16[80,1024]{1,0:T(8,128)(2,1)S(1)} %get-tuple-element.34), channel_id=1, source_target_pairs={{0,8},{1,17},{2,10},{3,19},{4,12},{5,21},{6,14},{7,23},{8,0},{9,25... | collective-permute-start | bytes 491528 | tf_op jit(solution)/shard_map/ppermute | solution.py:29
  25.5 5.5 %collective-permute-start.16 = (bf16[80,1024]{1,0:T(8,128)(2,1)S(1)}, bf16[80,1024]{1,0:T(8,128)(2,1)S(1)}, u32[]{:S(2)}, u32[]{:S(2)}) collective-permute-start(bf16[80,1024]{1,0:T(8,128)(2,1)S(1)} %get-tuple-element.36), channel_id=1, source_target_pairs={{0,8},{1,17},{2,10},{3,19},{4,12},{5,21},{6,14},{7,23},{8,0},{9,25... | collective-permute-start | bytes 491528 | tf_op jit(solution)/shard_map/ppermute | solution.py:29
  26.7 10.7 %collective-permute-start.13 = (bf16[160,1024]{1,0:T(8,128)(2,1)S(1)}, bf16[160,1024]{1,0:T(8,128)(2,1)S(1)}, u32[]{:S(2)}, u32[]{:S(2)}) collective-permute-start(bf16[160,1024]{1,0:T(8,128)(2,1)S(1)} %get-tuple-element.32), channel_id=1, source_target_pairs={{0,8},{1,17},{2,10},{3,19},{4,12},{5,21},{6,14},{7,23},{8,0},{9,25... | collective-permute-start | bytes 983048 | tf_op jit(solution)/shard_map/ppermute | solution.py:29
  29.2 6.5 %collective-permute-start.15 = (bf16[80,1024]{1,0:T(8,128)(2,1)S(1)}, bf16[80,1024]{1,0:T(8,128)(2,1)S(1)}, u32[]{:S(2)}, u32[]{:S(2)}) collective-permute-start(bf16[80,1024]{1,0:T(8,128)(2,1)S(1)} %shard_map.61), channel_id=1, source_target_pairs={{0,16},{1,9},{2,18},{3,11},{4,20},{5,13},{6,22},{7,15},{8,24},{9,1... | collective-permute-start | bytes 491528 | tf_op jit(solution)/shard_map/ppermute | solution.py:29
  31.0 6.5 %collective-permute-start.17 = (bf16[80,1024]{1,0:T(8,128)(2,1)S(1)}, bf16[80,1024]{1,0:T(8,128)(2,1)S(1)}, u32[]{:S(2)}, u32[]{:S(2)}) collective-permute-start(bf16[80,1024]{1,0:T(8,128)(2,1)S(1)} %shard_map.62), channel_id=1, source_target_pairs={{0,16},{1,9},{2,18},{3,11},{4,20},{5,13},{6,22},{7,15},{8,24},{9,1... | collective-permute-start | bytes 491528 | tf_op jit(solution)/shard_map/ppermute | solution.py:29
